TPU v7x, 128 devices: a whole 4x4x4 slice. The times are simulated.
128 devices in a mesh: group: 8 (over y, core), tensor: 16 (over x, z).
Axes of the slice: x: 4, y: 4, z: 4, core: 2. Of those that a mesh axis runs over, the one named last changes fastest.
Arguments:
- hidden_states: bfloat16 [2048, 8192], P('group', 'tensor'), may hold values from -6 to 6
- norm_gain: bfloat16 [8192], replicated, may hold values from 0.25 to 1.75
- w_query: bfloat16 [8192, 8192], P(None, 'tensor'), may hold values from -0.0625 to 0.0625
- b_query: bfloat16 [8192], P('tensor'), may hold values from -4 to 4
- w_key: bfloat16 [8192, 1024], P(None, 'tensor'), may hold values from -0.0625 to 0.0625
- b_key: bfloat16 [1024], P('tensor'), may hold values from -4 to 4
- w_value: bfloat16 [8192, 1024], P(None, 'tensor'), may hold values from -0.0625 to 0.0625
- b_value: bfloat16 [1024], P('tensor'), may hold values from -4 to 4
- w_out: bfloat16 [8192, 8192], P('tensor'), may hold values from -0.0625 to 0.0625
- pool_keys: bfloat16 [2048, 8, 64, 128], P(('group', 'tensor')), may hold values from -80 to 80
- pool_values: bfloat16 [2048, 8, 64, 128], P(('group', 'tensor')), may hold values from -6 to 6
- conv_slots: int32 [32], replicated, may hold values from 0 to 31, as said below
- page_table: int32 [32, 64], replicated, may hold values from 0 to 2047, as said below
- prefix_len: int32 [32], replicated, may hold values from 1 to 4096, as said below
- suffix_len: int32 [32], replicated, may hold values from 1 to 64, as said below
- new_dest: int32 [32], replicated, may hold values from 0 to 127, as said below
Outputs:
- attn_out: bfloat16 [2048, 8192], P('group', 'tensor')
- new_keys: bfloat16 [128, 8, 64, 128], P(('group', 'tensor'))
- new_values: bfloat16 [128, 8, 64, 128], P(('group', 'tensor'))
Inputs may be any that keep to these rules, and one draw needn't show every extreme that they name: A permutation: slot s, of group s // 4, holds conversation conv_slots[s]. `page_table`: entry = device * 16 + local slot, with device = group index * 16 + tensor index; the pages of a conversation held by group g lie in local slots g * 2 to (g + 1) * 2 - 1; every pool slot holds exactly one page. `prefix_len`: some conversation has exactly 4096. `suffix_len`: some conversation has exactly 64. `new_dest`: all distinct.
All inputs are finite; a program needn't handle non-finite values.
Results may differ from a plain program's by a relative error of at most 0.02.
Values may be sent and summed in bfloat16 or wider, within the bound.
A program may use at most 128 MiB of HBM per device.

v0:
```python
import math

import jax
import jax.numpy as jnp
from jax import lax
from jax.sharding import PartitionSpec as P

HD = 128
SUF = 64


THETA = 1000000.0
EPSILON = 1e-06
NEGATIVE = -1e30


def from_partner(value, axis, stride):
    mask = 2**stride
    pairs = [(source, source ^ mask) for source in range(lax.axis_size(axis))]
    return lax.ppermute(value, axis, pairs)


def rotate(values, positions):
    width = values.shape[-1]
    half_width = width // 2
    freq = THETA ** (-(jnp.arange(half_width, dtype=jnp.float32) * 2.0 / width))
    angle = positions.astype(jnp.float32)[:, None] * freq[None, :]
    cosine = jnp.concatenate([jnp.cos(angle), jnp.cos(angle)], axis=1)[:, None, :]
    sine = jnp.concatenate([jnp.sin(angle), jnp.sin(angle)], axis=1)[:, None, :]
    turned = jnp.concatenate([-values[..., half_width:], values[..., :half_width]], axis=-1)
    return values * cosine + turned * sine


def attend(carry, query, keys, values, mask):
    peak, total, accum = carry
    scores = jnp.einsum("rhd,bd->hrb", query, keys, preferred_element_type=jnp.float32) * HD ** (
        -0.5
    )
    scores = jnp.where(mask[None], scores, NEGATIVE)
    fresh = jnp.maximum(peak, jnp.max(scores, axis=-1))
    shrink = jnp.exp(peak - fresh)
    weights = jnp.exp(scores - fresh[..., None])
    total = total * shrink + jnp.sum(weights, axis=-1)
    accum = accum * shrink[..., None] + jnp.einsum(
        "hrb,bd->hrd", weights.astype(jnp.bfloat16), values, preferred_element_type=jnp.float32
    )
    return (fresh, total, accum)


def shards(
    hidden_states,
    norm_gain,
    w_query,
    b_query,
    w_key,
    b_key,
    w_value,
    b_value,
    w_out,
    pool_keys,
    pool_values,
    conv_slots,
    page_table,
    prefix_len,
    suffix_len,
    new_dest,
):
    n_group = lax.axis_size("group")
    n_tensor = lax.axis_size("tensor")
    devices = n_group * n_tensor
    group_idx = lax.axis_index("group")
    tensor_idx = lax.axis_index("tensor")
    rows = hidden_states.shape[0]
    conv_grp = rows // SUF
    heads = w_query.shape[1] // HD
    half_width = HD // 2
    conv_count = conv_slots.shape[0]
    pages_max = page_table.shape[1]
    page_len = pool_keys.shape[2]
    features = lax.all_gather(hidden_states, "tensor", axis=1, tiled=True)
    wide = features.astype(jnp.float32)
    factor = lax.rsqrt(jnp.mean(wide * wide, axis=-1, keepdims=True) + EPSILON)
    normed = (wide * factor * norm_gain.astype(jnp.float32)).astype(jnp.bfloat16)
    conv_ids = jnp.arange(conv_count, dtype=jnp.int32)
    slot_conv = lax.dynamic_slice_in_dim(conv_slots, group_idx * conv_grp, conv_grp, 0)
    slot_match = slot_conv[:, None] == conv_ids[None, :]
    slot_prefix = jnp.sum(jnp.where(slot_match, prefix_len[None, :], 0), axis=1)
    slot_suffix = jnp.sum(jnp.where(slot_match, suffix_len[None, :], 0), axis=1)
    row_ids = jnp.arange(rows, dtype=jnp.int32)
    row_conv = row_ids // SUF
    row_pos = row_ids % SUF
    positions = jnp.repeat(slot_prefix, SUF) + row_pos
    live_row = row_pos < jnp.repeat(slot_suffix, SUF)
    query = jnp.dot(normed, w_query, preferred_element_type=jnp.float32) + b_query.astype(
        jnp.float32
    )
    query = rotate(query.reshape(rows, heads, HD), positions).astype(jnp.bfloat16)
    key_half = (
        jnp.dot(normed, w_key, preferred_element_type=jnp.float32) + b_key.astype(jnp.float32)
    ).astype(jnp.bfloat16)
    value_half = (
        jnp.dot(normed, w_value, preferred_element_type=jnp.float32) + b_value.astype(jnp.float32)
    ).astype(jnp.bfloat16)
    other_key, other_value = from_partner((key_half, value_half), "tensor", 0)
    parity = tensor_idx % 2
    key_raw = jnp.where(
        parity == 0,
        jnp.concatenate([key_half, other_key], axis=1),
        jnp.concatenate([other_key, key_half], axis=1),
    )
    value_new = jnp.where(
        parity == 0,
        jnp.concatenate([value_half, other_value], axis=1),
        jnp.concatenate([other_value, value_half], axis=1),
    )
    key_new = rotate(key_raw.astype(jnp.float32)[:, None, :], positions)[:, 0, :].astype(
        jnp.bfloat16
    )
    pool_dev = pool_keys.shape[0]
    slots_grp = pool_dev // n_group
    received = devices * slots_grp
    order = jnp.arange(received, dtype=jnp.int32)

    def arrange(pool):
        spread = jnp.repeat(
            pool.reshape(n_group, slots_grp, n_tensor // 2, page_len, HD), 2, axis=2
        )
        return jnp.transpose(spread, (0, 2, 1, 3, 4)).reshape(received, page_len, HD)

    got_keys, got_values = (
        lax.all_to_all(
            arrange(pool_keys), ("group", "tensor"), split_axis=0, concat_axis=0, tiled=True
        ),
        lax.all_to_all(
            arrange(pool_values), ("group", "tensor"), split_axis=0, concat_axis=0, tiled=True
        ),
    )
    source = order // slots_grp
    within = order % slots_grp
    slot_ids = source * pool_dev + group_idx * slots_grp + within
    needed = jnp.sum(jnp.where(slot_match[:, :, None], page_table[None, :, :], 0), axis=1).reshape(
        conv_grp * pages_max
    )
    match = slot_ids[:, None] == needed[None, :]
    flat_ids = jnp.arange(conv_grp * pages_max, dtype=jnp.int32)
    key_conv = jnp.sum(jnp.where(match, flat_ids[None, :] // pages_max, 0), axis=1)
    key_page = jnp.sum(jnp.where(match, flat_ids[None, :] % pages_max, 0), axis=1)
    page_prefix = jnp.sum(
        jnp.where(
            key_conv[:, None] == jnp.arange(conv_grp, dtype=jnp.int32)[None, :],
            slot_prefix[None, :],
            0,
        ),
        axis=1,
    )
    token_live = (
        key_page[:, None] * page_len + jnp.arange(page_len, dtype=jnp.int32)[None, :]
        < page_prefix[:, None]
    )
    init = (
        jnp.full((heads, rows), NEGATIVE, jnp.float32),
        jnp.zeros((heads, rows), jnp.float32),
        jnp.zeros((heads, rows, HD), jnp.float32),
    )
    own_mask = (row_conv[:, None] == row_conv[None, :]) & (row_pos[None, :] <= row_pos[:, None])
    carry = attend(init, query, key_new, value_new, own_mask)
    block_pages = math.gcd(received, max(1, 1024 // page_len))

    def make_step(keys_src, values_src, conv_src, live_src):

        def step_block(index, state):
            start = index * block_pages
            keys = lax.dynamic_slice_in_dim(keys_src, start, block_pages, 0).reshape(
                block_pages * page_len, HD
            )
            values = lax.dynamic_slice_in_dim(values_src, start, block_pages, 0).reshape(
                block_pages * page_len, HD
            )
            conv_tok = jnp.repeat(
                lax.dynamic_slice_in_dim(conv_src, start, block_pages, 0), page_len
            )
            live_tok = lax.dynamic_slice_in_dim(live_src, start, block_pages, 0).reshape(
                block_pages * page_len
            )
            mask = (row_conv[:, None] == conv_tok[None, :]) & live_tok[None, :]
            return attend(state, query, keys, values, mask)

        return step_block

    carry = lax.fori_loop(
        0, received // block_pages, make_step(got_keys, got_values, key_conv, token_live), carry
    )
    peak, total, accum = carry
    mixed = jnp.transpose(accum / total[..., None], (1, 0, 2))
    mixed = (
        jnp.where(live_row[:, None, None], mixed, jnp.zeros_like(mixed))
        .astype(jnp.bfloat16)
        .reshape(rows, heads * HD)
    )
    partial_value = jnp.dot(mixed, w_out, preferred_element_type=jnp.float32)
    attn_out = lax.psum_scatter(
        partial_value.astype(jnp.bfloat16), "tensor", scatter_dimension=1, tiled=True
    )
    my_keys = lax.dynamic_slice_in_dim(key_new, parity * half_width, half_width, 1)
    my_keys = jnp.where(live_row[:, None], my_keys, jnp.zeros_like(my_keys)).reshape(
        conv_grp, SUF, half_width
    )
    my_values = jnp.where(live_row[:, None], value_half, jnp.zeros_like(value_half)).reshape(
        conv_grp, SUF, half_width
    )
    dest_slot = jnp.sum(
        jnp.where(conv_slots[:, None] == conv_ids[None, :], new_dest[None, :], 0), axis=1
    )
    me_index = group_idx * n_tensor + tensor_idx
    all_keys, all_values = (
        lax.all_gather(my_keys, ("group", "tensor"), axis=0, tiled=True),
        lax.all_gather(my_values, ("group", "tensor"), axis=0, tiled=True),
    )
    select = (dest_slot == me_index).reshape(n_group, conv_grp).astype(jnp.bfloat16)
    page_keys = jnp.einsum(
        "gk,gtkph->tph",
        select,
        all_keys.reshape(n_group, n_tensor, conv_grp, SUF, half_width),
        preferred_element_type=jnp.float32,
    )
    page_values = jnp.einsum(
        "gk,gtkph->tph",
        select,
        all_values.reshape(n_group, n_tensor, conv_grp, SUF, half_width),
        preferred_element_type=jnp.float32,
    )

    def assemble(page):
        split = page.reshape(n_tensor // 2, 2, SUF, half_width)
        return (
            jnp.transpose(split, (0, 2, 1, 3))
            .reshape(1, n_tensor // 2, SUF, HD)
            .astype(jnp.bfloat16)
        )

    return (attn_out, assemble(page_keys), assemble(page_values))


def solution(mesh):
    in_specs = (
        P("group", "tensor"),
        P(),
        P(None, "tensor"),
        P("tensor"),
        P(None, "tensor"),
        P("tensor"),
        P(None, "tensor"),
        P("tensor"),
        P("tensor", None),
        P(("group", "tensor"), None, None, None),
        P(("group", "tensor"), None, None, None),
        P(),
        P(),
        P(),
        P(),
        P(),
    )
    out_specs = (
        P("group", "tensor"),
        P(("group", "tensor"), None, None, None),
        P(("group", "tensor"), None, None, None),
    )
    return jax.shard_map(shards, mesh=mesh, in_specs=in_specs, out_specs=out_specs, check_vma=False)
```

profile of v0, /device:TPU:0, one launch (start us, length us, event | category | flops | bytes accessed | tf_op | source)
XLA Modules:
  0.0 384.3 jit_solution(8674249002946436696)
XLA Ops:
  11.6 58.7 %all-gather.4.cloned.1.call-done = bf16[256,8192]{1,0:T(8,128)(2,1)} async-done(((bf16[256,512]{1,0:T(8,128)(2,1)}), bf16[256,8192]{1,0:T(8,128)(2,1)}) %all-gather.4.cloned.1.call-update) | async-done | bytes 4194320 | tf_op jit(solution)/shard_map/all_gather | solution.py:80
  70.3 3.3 fusion.13
  73.8 2.7 fusion.23
  78.2 2.3 collective-permute-done
  80.6 4.3 %broadcast_select_fusion = (bf16[256,64]{0,1:T(8,128)(2,1)S(1)}, bf16[256,64]{0,1:T(8,128)(2,1)}, bf16[256,64]{0,1:T(8,128)(2,1)S(1)}) fusion(pred[256]{0:T(512)(128)(4,1)S(1)} %fusion.54, bf16[256,128]{0,1:T(8,128)(2,1)S(1)} %get-tuple-element.227, s32[]{:T(128)S(6)} %select_n.191, f32[64]{0:T(128)} %convert_element_type.118, ...), kind=kOutput, calls=%fused_computation.84 | convolution fusion | flops 276889600 | bytes 5408260 | tf_op jit(solution)/shard_map/dot_general | solution.py:102
  84.9 1.5 copy.81
  86.6 3.0 broadcast_in_dim.233
  89.6 8.5 %all-to-all-start = ((bf16[256,64,128]{2,1,0:T(8,128)(2,1)}), bf16[256,64,128]{2,1,0:T(8,128)(2,1)}, u32[]{:S(2)}, u32[]{:S(2)}) async-start(bf16[256,64,128]{2,1,0:T(8,128)(2,1)} %bitcast.114), calls=%async_computation | async-start | bytes 8388608 | tf_op jit(solution)/shard_map/all_to_all | solution.py:131
  98.1 1.8 copy.66
  99.9 50.4 %all-to-all-done = bf16[256,64,128]{2,1,0:T(8,128)(2,1)} async-done(((bf16[256,64,128]{2,1,0:T(8,128)(2,1)}), bf16[256,64,128]{2,1,0:T(8,128)(2,1)}, u32[]{:S(2)}, u32[]{:S(2)}) %all-to-all-start) | async-done | bytes 4194336 | tf_op jit(solution)/shard_map/all_to_all | solution.py:131
  150.3 3.0 broadcast_in_dim.234
  153.3 6.0 %all-to-all-start.1 = ((bf16[256,64,128]{2,1,0:T(8,128)(2,1)}), bf16[256,64,128]{2,1,0:T(8,128)(2,1)}, u32[]{:S(2)}, u32[]{:S(2)}) async-start(bf16[256,64,128]{2,1,0:T(8,128)(2,1)} %bitcast.113), calls=%async_computation.1 | async-start | bytes 8388608 | tf_op jit(solution)/shard_map/all_to_all | solution.py:134
  160.2 7.0 %fusion.22 = f32[32,4,8,128]{3,2,1,0:T(8,128)S(1)} fusion(bf16[8192,512]{1,0:T(8,128)(2,1)} %param.20, f32[512]{0:T(512)S(1)} %convert_element_type.115, bf16[256,8192]{1,0:T(8,128)(2,1)} %all-gather.4.cloned.1.call-done, f32[8192]{0:T(1024)S(1)} %copy-done.5, f32[256]{0:T(256)S(1)} %add_rsqrt_fusion), kind=kOutput, calls=%fused_computation.35 | convolution fusion | flops 2156003328 | bytes 13143040 | tf_op jit(solution)/shard_map/dot_general | solution.py:94
  170.6 37.3 %collective-permute-done.1 = bf16[256,64]{0,1:T(8,128)(2,1)S(1)} collective-permute-done((bf16[256,64]{0,1:T(8,128)(2,1)S(1)}, bf16[256,64]{0,1:T(8,128)(2,1)S(1)}, u32[]{:S(2)}, u32[]{:S(2)}) %collective-permute-start.1) | collective-permute-done | bytes 32800 | tf_op jit(solution)/shard_map/ppermute | solution.py:20
  208.2 7.9 %all-to-all-done.1 = bf16[256,64,128]{2,1,0:T(8,128)(2,1)} async-done(((bf16[256,64,128]{2,1,0:T(8,128)(2,1)}), bf16[256,64,128]{2,1,0:T(8,128)(2,1)}, u32[]{:S(2)}, u32[]{:S(2)}) %all-to-all-start.1) | async-done | bytes 4194336 | tf_op jit(solution)/shard_map/all_to_all | solution.py:134
  216.2 78.0 %while.18 = (s32[]{:T(128)}, f32[4,256]{1,0:T(4,128)S(1)}, f32[4,256]{1,0:T(4,128)S(1)}, f32[4,256,128]{2,1,0:T(8,128)S(1)}, s32[256]{0:T(256)S(1)}, /*index=5*/...) while((s32[]{:T(128)}, f32[4,256]{1,0:T(4,128)S(1)}, ...), condition=%wide.region_12.13_spmd.clone, body=%wide.region_9.12_spmd.clone.sunk | while | flops 549195776 | bytes 16604535 | solution.py:190
  219.7 1.3 fusion.85
  224.6 1.3 fusion.85
  229.4 1.3 fusion.85
  234.3 1.3 fusion.85
  239.2 1.3 fusion.85
  244.1 1.3 fusion.85
  248.9 1.3 fusion.85
  258.7 1.3 fusion.85
  268.5 1.3 fusion.85
  278.2 1.3 fusion.85
  288.0 1.3 fusion.85
  292.9 1.3 fusion.85
  294.5 7.7 %convolution_convert_fusion = bf16[256,8192]{1,0:T(8,128)(2,1)} fusion(bf16[256,512]{0,1:T(8,128)(2,1)S(1)} %bitcast.121, bf16[512,8192]{1,0:T(8,128)(2,1)} %param.26), kind=kOutput, calls=%fused_computation.22 | convolution fusion | flops 2149580800 | bytes 12845056 | tf_op jit(solution)/shard_map/dot_general | solution.py:200
  303.3 8.4 %fusion.18 = bf16[1,8,2,64,64,1]{4,0,5,3,2,1:T(2,128)(2,1)S(1)} fusion(pred[8,4,1,1,1,1]{0,2,1,5,4,3:T(4,128)(4,1)S(1)} %copy.74, bf16[8,2,64,64,8,4]{3,2,5,1,0,4:T(8,128)(2,1)} %bitcast.126), kind=kOutput, calls=%fused_computation.28 | convolution fusion | flops 4194304 | bytes 4325408 | tf_op jit(solution)/shard_map/gk,gtkph->tph/dot_general | solution.py:220
  312.9 8.6 %fusion.16 = bf16[1,8,2,64,64,1]{4,0,5,3,2,1:T(2,128)(2,1)S(1)} fusion(pred[8,4,1,1,1,1]{0,2,1,5,4,3:T(4,128)(4,1)S(1)} %copy.74, bf16[8,2,64,64,8,4]{3,2,5,1,0,4:T(8,128)(2,1)} %bitcast.127), kind=kOutput, calls=%fused_computation.26 | convolution fusion | flops 4194304 | bytes 4325408 | tf_op jit(solution)/shard_map/gk,gtkph->tph/dot_general | solution.py:226
  322.6 55.1 %reduce-scatter.2.cloned.1.call-done = bf16[256,512]{1,0:T(8,128)(2,1)} async-done(((bf16[256,8192]{1,0:T(8,128)(2,1)}), bf16[256,512]{1,0:T(8,128)(2,1)}) %reduce-scatter.2.cloned.1.call-update) | async-done | bytes 262160 | tf_op jit(solution)/shard_map/reduce_scatter | solution.py:201
  (296 shorter events, 75.9 us)
Async XLA Ops:
  7.2 73.4 %copy-start = (bf16[8192,64]{0,1:T(8,128)(2,1)S(1)}, bf16[8192,64]{0,1:T(8,128)(2,1)}, u32[]{:S(2)}) copy-start(bf16[8192,64]{0,1:T(8,128)(2,1)} %param.24) | copy-start | bytes 3145732
  7.2 63.1 %all-gather.4.cloned.1.call-start = ((), (), s32[]{:S(2)}) async-start(), calls=%async_computation.3 | async-start | bytes 4456448 | tf_op jit(solution)/shard_map/all_gather | solution.py:80
  7.9 295.3 %all-gather.6.cloned.1.call-start = ((), (), s32[]{:S(2)}) async-start(), calls=%async_computation.5 | async-start | bytes 8454144 | tf_op jit(solution)/shard_map/all_gather | solution.py:216
  8.7 67.8 %copy-start.4 = (f32[8192]{0:T(1024)}, f32[8192]{0:T(1024)S(1)}, u32[]{:S(2)}) copy-start(f32[8192]{0:T(1024)S(1)} %convert_element_type.107) | copy-start | bytes 98308
  70.3 3.4 copy-start.2
  73.8 3.9 %copy-start.8 = (bf16[64]{0:T(256)(128)(2,1)S(1)}, bf16[64]{0:T(256)(128)(2,1)}, u32[]{:S(2)}) copy-start(bf16[64]{0:T(256)(128)(2,1)} %param.25) | copy-start | bytes 388
  76.5 4.0 %collective-permute-start = (bf16[256,64]{0,1:T(8,128)(2,1)S(1)}, bf16[256,64]{0,1:T(8,128)(2,1)S(1)}, u32[]{:S(2)}, u32[]{:S(2)}) collective-permute-start(bf16[256,64]{0,1:T(8,128)(2,1)S(1)} %fusion.23), channel_id=1, source_target_pairs={{0,1},{1,0},{2,3},{3,2},{4,5},{5,4},{6,7},{7,6},{8,9},{9,8},{10,11... | collective-permute-start | bytes 98312 | tf_op jit(solution)/shard_map/ppermute | solution.py:20
  80.6 5.8 %copy-start.3 = (bf16[16,8,64,128]{3,2,1,0:T(8,128)(2,1)S(1)}, bf16[16,8,64,128]{3,2,1,0:T(8,128)(2,1)}, u32[]{:S(2)}) copy-start(bf16[16,8,64,128]{3,2,1,0:T(8,128)(2,1)} %param.27) | copy-start | bytes 6291460
  89.6 60.7 %all-to-all-start = ((bf16[256,64,128]{2,1,0:T(8,128)(2,1)}), bf16[256,64,128]{2,1,0:T(8,128)(2,1)}, u32[]{:S(2)}, u32[]{:S(2)}) async-start(bf16[256,64,128]{2,1,0:T(8,128)(2,1)} %bitcast.114), calls=%async_computation | async-start | bytes 8388608 | tf_op jit(solution)/shard_map/all_to_all | solution.py:131
  153.3 6.0 %copy-start.7 = (bf16[512]{0:T(512)(128)(2,1)S(1)}, bf16[512]{0:T(512)(128)(2,1)}, u32[]{:S(2)}) copy-start(bf16[512]{0:T(512)(128)(2,1)} %param.21) | copy-start | bytes 3076
  153.3 6.1 %copy-start.6 = (s32[32,64]{1,0:T(8,128)S(1)}, s32[32,64]{1,0:T(8,128)}, u32[]{:S(2)}) copy-start(s32[32,64]{1,0:T(8,128)} %param.30) | copy-start | bytes 24580
  153.3 6.9 %copy-start.5 = (f32[8192]{0:T(1024)S(1)}, f32[8192]{0:T(1024)}, u32[]{:S(2)}) copy-start(f32[8192]{0:T(1024)} %copy-done.4) | copy-start | bytes 98308
  153.3 62.9 %all-to-all-start.1 = ((bf16[256,64,128]{2,1,0:T(8,128)(2,1)}), bf16[256,64,128]{2,1,0:T(8,128)(2,1)}, u32[]{:S(2)}, u32[]{:S(2)}) async-start(bf16[256,64,128]{2,1,0:T(8,128)(2,1)} %bitcast.113), calls=%async_computation.1 | async-start | bytes 8388608 | tf_op jit(solution)/shard_map/all_to_all | solution.py:134
  159.3 153.6 %all-gather.8.cloned.1.call-start = ((), (), s32[]{:S(2)}) async-start(), calls=%async_computation.6 | async-start | bytes 8454144 | tf_op jit(solution)/shard_map/all_gather | solution.py:217
  167.7 40.2 %collective-permute-start.1 = (bf16[256,64]{0,1:T(8,128)(2,1)S(1)}, bf16[256,64]{0,1:T(8,128)(2,1)S(1)}, u32[]{:S(2)}, u32[]{:S(2)}) collective-permute-start(bf16[256,64]{0,1:T(8,128)(2,1)S(1)} %get-tuple-element.238), channel_id=1, source_target_pairs={{0,1},{1,0},{2,3},{3,2},{4,5},{5,4},{6,7},{7,6},{8,9},{9,8},{10,11... | collective-permute-start | bytes 98312 | tf_op jit(solution)/shard_map/ppermute | solution.py:20
  170.3 207.4 %reduce-scatter.2.cloned.1.call-start = ((), (), s32[]{:S(2)}) async-start(), calls=%async_computation.4 | async-start | bytes 4456448 | tf_op jit(solution)/shard_map/reduce_scatter | solution.py:201
  302.2 0.7 copy-start.9
  302.2 0.7 copy-start.10
  312.9 64.9 %copy-start.1 = (bf16[8192,64]{0,1:T(8,128)(2,1)S(1)}, bf16[8192,64]{0,1:T(8,128)(2,1)}, u32[]{:S(2)}) copy-start(bf16[8192,64]{0,1:T(8,128)(2,1)} %param.24) | copy-start | bytes 3145732
Sparse Core Ops, SparseCore 0:
  10.1 60.1 all-gather.3
  86.5 136.7 all-gather.5
  226.4 67.8 all-gather.7
  302.3 75.3 reduce-scatter.1
where the time goes:
time: 385 us; the launch traced here: 384 us
  waiting for transfers between devices  212 us (55%)
  matrix products  73.6 us (19%)
  local copies, waits for them, and re-layouts  37.5 us (10%)
  other arithmetic  28.6 us (7%)
  starting transfers between devices  17.1 us (4%)
  between operations  14 us (4%)
    all_gather x1, waiting for transfers between devices, shards(): features = lax.all_gather(hidden_states, 'tensor', axis=1, tiled=True)  58.7 us
    reduce_scatter x1, waiting for transfers between devices, shards(): lax.psum_scatter(partial_value.astype(jnp.bfloat16), 'tensor', scatter_di...  55.1 us
    all_to_all x1, waiting for transfers between devices, shards(): lax.all_to_all(arrange(pool_keys), ('group', 'tensor'), split_axis=0, con...  50.4 us
    ppermute x2, waiting for transfers between devices, from_partner(): return lax.ppermute(value, axis, pairs)  39.6 us
    dot_general x17, matrix products, attend(): jnp.einsum('hrb,bd->hrd', weights.astype(jnp.bfloat16), values, preferred...  21.7 us
    dynamic_slice x16, local copies, waits for them, and re-layouts, step_block(): lax.dynamic_slice_in_dim(values_src, start, block_pages, 0)  17.2 us
    reduce_sum x17, other arithmetic, attend(): total = total * shrink + jnp.sum(weights, axis=-1)  14.9 us
    dot_general x17, matrix products, attend(): jnp.einsum('rhd,bd->hrb', query, keys, preferred_element_type=jnp.float32)  13.3 us
  transfers between devices with their start and end apart: 8, of which 6 were waited for; matrix products, arithmetic and copies ran while one was open for 33% of the time, Pallas kernels for 0%

commit v1 on v0

v1 whole, which is shorter than its diff:
```python
import jax
import jax.numpy as jnp
import numpy as np
from jax import lax
from jax.experimental import pallas as pl
from jax.experimental.pallas import tpu as pltpu
from jax.sharding import PartitionSpec as P

HD = 128
SUF = 64
CONVS = 4
ROWS = CONVS * SUF
GROUPS = 8
TENSOR = 16
WIDTH = 8192
PART = WIDTH // TENSOR
PAGES = 64
PAGE = 64
HEADS = 4
THETA = 1000000.0
EPSILON = 1e-06
NEGATIVE = -1e30
SCALE = HD**-0.5 * 1.4426950408889634
LN2 = 0.6931471805599453
MESH = pl.DeviceIdType.MESH
BF16 = jnp.bfloat16
F32 = jnp.float32
I32 = jnp.int32


def remote(src, dst, send_sem, recv_sem, group, tensor):
    return pltpu.make_async_remote_copy(
        src_ref=src,
        dst_ref=dst,
        send_sem=send_sem,
        recv_sem=recv_sem,
        device_id=(group, tensor),
        device_id_type=MESH,
    )


def place():
    group = lax.axis_index("group")
    tensor = lax.axis_index("tensor")
    return (
        group,
        tensor,
        lax.div(group, 2),
        lax.rem(group, 2),
        lax.div(tensor, 4),
        lax.rem(tensor, 4),
    )


def offset_device(off, y, core, x, z):
    flip = lax.rem(off, 2)
    other_x = lax.rem(x + lax.rem(lax.div(off, 2), 4), 4)
    other_core = lax.rem(core + lax.rem(lax.div(off, 8), 2), 2)
    other_y = lax.rem(y + lax.div(off, 16), 4)
    other_z = z + flip * (3 - 2 * z)
    return other_y * 2 + other_core, other_x, other_z


def lane_iota(shape):
    return lax.broadcasted_iota(I32, shape, len(shape) - 1)


def row_iota(shape):
    return lax.broadcasted_iota(I32, shape, len(shape) - 2)


def gather_kernel(
    conv_ref,
    prefix_ref,
    suffix_ref,
    dest_ref,
    table_ref,
    hidden,
    pool_k,
    pool_v,
    w_query,
    w_key,
    w_value,
    gain_ref,
    b_query,
    b_key,
    b_value,
    freq_ref,
    got_k,
    got_v,
    query_own,
    query_other,
    key_new,
    value_new,
    lists,
    new_pages,
    feat,
    wq,
    wk,
    wv,
    acc_q,
    acc_k,
    acc_v,
    kv_own,
    kv_other,
    new_all,
    new_send,
    local_sem,
    ring_send,
    ring_recv,
    pool_send,
    pool_recv,
    pair_send,
    pair_recv,
    group_send,
    group_recv,
    page_send,
    page_recv,
):
    group, tensor, y, core, x, z = place()
    pair_z = z + 1 - 2 * lax.rem(z, 2)
    parity = lax.rem(z, 2)
    own = pltpu.make_async_copy(hidden, feat.at[x, z], local_sem.at[0])
    own.start()
    loads = [
        pltpu.make_async_copy(w_query, wq, local_sem.at[1]),
        pltpu.make_async_copy(w_key, wk, local_sem.at[2]),
        pltpu.make_async_copy(w_value, wv, local_sem.at[3]),
    ]
    for load in loads:
        load.start()
    my_head = 2 * x + lax.div(z, 2)
    keep = [
        pltpu.make_async_copy(
            pool_k.at[pl.ds(2 * group, 2), my_head], got_k.at[0], local_sem.at[4]
        ),
        pltpu.make_async_copy(
            pool_v.at[pl.ds(2 * group, 2), my_head], got_v.at[0], local_sem.at[5]
        ),
    ]
    for copy in keep:
        copy.start()

    barrier = pltpu.get_barrier_semaphore()

    def greet(off, carry):
        to_group, to_x, to_z = offset_device(off, y, core, x, z)
        pl.semaphore_signal(
            barrier, inc=1, device_id=(to_group, to_x * 4 + to_z), device_id_type=MESH
        )
        return carry

    lax.fori_loop(1, 64, greet, 0)

    def greet_rest(off, carry):
        to_x = lax.div(off, 2)
        to_z = pair_z + lax.rem(off, 2) * (3 - 2 * pair_z)
        pl.semaphore_signal(
            barrier, inc=1, device_id=(group, to_x * 4 + to_z), device_id_type=MESH
        )
        return carry

    lax.fori_loop(0, 8, greet_rest, 0)
    pl.semaphore_wait(barrier, 71)

    own.wait()
    x_up, x_down = lax.rem(x + 1, 4), lax.rem(x + 3, 4)
    z_up, z_down = lax.rem(z + 1, 4), lax.rem(z + 3, 4)
    to_x_up, to_x_down = x_up * 4 + z, x_down * 4 + z
    to_z_up, to_z_down = x * 4 + z_up, x * 4 + z_down
    sent = []

    def ring(index, ref, to):
        copy = remote(ref, ref, ring_send.at[index], ring_recv.at[index], group, to)
        copy.start()
        sent.append(copy)
        return copy

    half_a, half_b = pl.ds(0, 128), pl.ds(128, 128)
    a0 = ring(0, feat.at[x, z, half_a], to_x_up)
    a1 = ring(1, feat.at[x, z, half_a], to_x_down)
    b0 = ring(2, feat.at[x, z, half_b], to_z_up)
    b1 = ring(3, feat.at[x, z, half_b], to_z_down)

    def pool_copies(off):
        to_group, to_x, to_z = offset_device(off, y, core, x, z)
        to = to_x * 4 + to_z
        head = 2 * to_x + lax.div(to_z, 2)
        slots = pl.ds(2 * to_group, 2)
        return (
            remote(
                pool_k.at[slots, head],
                got_k.at[off],
                pool_send.at[0, off],
                pool_recv.at[0, off],
                to_group,
                to,
            ),
            remote(
                pool_v.at[slots, head],
                got_v.at[off],
                pool_send.at[1, off],
                pool_recv.at[1, off],
                to_group,
                to,
            ),
        )

    def push(off, carry):
        first, second = pool_copies(off)
        first.start()
        second.start()
        return carry

    lax.fori_loop(1, 64, push, 0)

    a0.wait_recv()
    a2 = ring(4, feat.at[x_down, z, pl.ds(0, 64)], to_x_up)
    a1.wait_recv()
    a3 = ring(5, feat.at[x_up, z, pl.ds(64, 64)], to_x_down)
    b0.wait_recv()
    b2 = ring(6, feat.at[x, z_down, pl.ds(128, 64)], to_z_up)
    b1.wait_recv()
    b3 = ring(7, feat.at[x, z_up, pl.ds(192, 64)], to_z_down)
    a2.wait_recv()
    a3.wait_recv()
    a4 = ring(8, feat.at[:, z, half_a], to_z_up)
    a5 = ring(9, feat.at[:, z, half_a], to_z_down)
    b2.wait_recv()
    b3.wait_recv()
    b4 = ring(10, feat.at[x, :, half_b], to_x_up)
    b5 = ring(11, feat.at[x, :, half_b], to_x_down)

    prefix = [prefix_ref[conv_ref[group * CONVS + i]] for i in range(CONVS)]
    suffix = [suffix_ref[conv_ref[group * CONVS + i]] for i in range(CONVS)]

    offsets = row_iota((SUF, HD))
    positions = jnp.concatenate([offsets + prefix[i] for i in range(CONVS)], axis=0)
    angle = positions.astype(F32) * freq_ref[...]
    cosine = jnp.cos(angle)
    sine = jnp.sin(angle)
    sine = jnp.where(lane_iota((ROWS, HD)) < HD // 2, -sine, sine)

    page_ids = lane_iota((1, PAGES))
    below = (row_iota((PAGES, PAGES)) < lane_iota((PAGES, PAGES))).astype(F32)
    lane = lane_iota((PAGES, HD))
    table = jnp.zeros((PAGES, HD), F32)
    counts = jnp.zeros((8, HD), F32)
    for i in range(CONVS):
        entry = table_ref[pl.ds(conv_ref[group * CONVS + i], 1), :]
        source = entry >> 4
        source_y, source_core = source >> 5, (source >> 4) & 1
        source_x, source_z = (source >> 2) & 3, source & 3
        live = jnp.clip(prefix[i] - page_ids * PAGE, 0, PAGE)
        here = ((source_z == z) | (source_z == 3 - z)) & (live > 0)
        off = (((y - source_y) & 3) * 2 + ((core - source_core) & 1)) * 4
        off = (off + ((x - source_x) & 3)) * 2 + jnp.where(source_z == z, 0, 1)
        value = ((off * 2 + (entry & 1)) * 128 + live).astype(F32)
        here_f = here.astype(F32)
        order = jnp.dot(
            jnp.broadcast_to(here_f, (8, PAGES)), below, preferred_element_type=F32
        )[0:1, :]
        match = (order == row_iota((PAGES, PAGES)).astype(F32)) & (
            jnp.broadcast_to(here_f, (PAGES, PAGES)) > 0.5
        )
        column = jnp.sum(jnp.where(match, value, 0.0), axis=1, keepdims=True)
        table = jnp.where(lane == i, column, table)
        counts = jnp.where(
            lane_iota((8, HD)) == i, jnp.sum(here_f, axis=1, keepdims=True), counts
        )
    lists[pl.ds(0, PAGES), :] = table.astype(I32)
    lists[pl.ds(PAGES, 8), :] = counts.astype(I32)

    a4.wait_recv()
    a6 = ring(12, feat.at[:, z_down, pl.ds(0, 64)], to_z_up)
    a5.wait_recv()
    a7 = ring(13, feat.at[:, z_up, pl.ds(64, 64)], to_z_down)
    b4.wait_recv()
    b6 = ring(14, feat.at[x_down, :, pl.ds(128, 64)], to_x_up)
    b5.wait_recv()
    b7 = ring(15, feat.at[x_up, :, pl.ds(192, 64)], to_x_down)
    for load in loads:
        load.wait()
    for copy in (a6, a7, b6, b7):
        copy.wait_recv()

    def square(bx, total):
        for bz in range(4):
            wide = feat[bx, bz].astype(F32)
            wide = wide * wide
            for part in range(PART // HD):
                total = total + wide[:, part * HD : (part + 1) * HD]
        return total

    total = lax.fori_loop(0, 4, square, jnp.zeros((ROWS, HD), F32))
    factor = lax.rsqrt(jnp.sum(total, axis=1, keepdims=True) * (1.0 / WIDTH) + EPSILON)
    acc_q[...] = jnp.zeros_like(acc_q)
    acc_k[...] = jnp.zeros_like(acc_k)
    acc_v[...] = jnp.zeros_like(acc_v)

    def project(bx, carry):
        for bz in range(4):
            block = bx * 4 + bz
            rows = pl.ds(pl.multiple_of(block * PART, PART), PART)
            wide = feat[bx, bz].astype(F32)
            normed = (wide * factor * gain_ref[block]).astype(BF16)
            acc_q[...] += jnp.dot(normed, wq[rows, :], preferred_element_type=F32)
            acc_k[...] += jnp.dot(normed, wk[rows, :], preferred_element_type=F32)
            acc_v[...] += jnp.dot(normed, wv[rows, :], preferred_element_type=F32)
        return carry

    lax.fori_loop(0, 4, project, 0)

    kv_own[...] = jnp.concatenate(
        [
            acc_k[...] + b_key[...].astype(F32),
            acc_v[...] + b_value[...].astype(F32),
        ],
        axis=1,
    ).astype(BF16)
    pair = x * 4 + pair_z
    kv_copy = remote(kv_own, kv_other, pair_send.at[0], pair_recv.at[0], group, pair)
    kv_copy.start()

    def rotate(values):
        return values * cosine + pltpu.roll(values, HD // 2, 1) * sine

    for head in range(HEADS):
        columns = slice(head * HD, (head + 1) * HD)
        values = acc_q[:, columns] + b_query[:, columns].astype(F32)
        values = rotate(values).astype(BF16)
        for i in range(CONVS):
            query_own[i, head * SUF : (head + 1) * SUF, :] = values[i * SUF : (i + 1) * SUF, :]
    query_copy = remote(
        query_own, query_other, pair_send.at[1], pair_recv.at[1], group, pair
    )
    query_copy.start()

    kv_copy.wait_recv()
    mine = kv_own[...].astype(F32)
    theirs = kv_other[...].astype(F32)
    even = jnp.where(parity == 0, mine, theirs)
    odd = jnp.where(parity == 0, theirs, mine)
    low = lane_iota((ROWS, HD)) < HD // 2
    keys = jnp.where(low, even, pltpu.roll(odd, HD // 2, 1))
    keys = rotate(keys)
    values = jnp.where(low, pltpu.roll(even, HD // 2, 1), odd)
    key_new[...] = keys.astype(BF16)
    value_new[...] = values.astype(BF16)

    page = jnp.where(parity == 0, keys.astype(BF16).astype(F32), values)
    live_row = jnp.concatenate([offsets < suffix[i] for i in range(CONVS)], axis=0)
    page = jnp.where(live_row, page, 0.0).astype(BF16)
    new_all[pl.ds(group * CONVS, CONVS)] = page.reshape(CONVS, SUF, HD)

    def group_copy(off):
        to_y = lax.rem(y + lax.div(off, 2), 4)
        to_core = lax.rem(core + lax.rem(off, 2), 2)
        ref = new_all.at[pl.ds(group * CONVS, CONVS)]
        return remote(
            ref, ref, group_send.at[off], group_recv.at[off], to_y * 2 + to_core, tensor
        )

    def group_start(off, carry):
        group_copy(off).start()
        return carry

    lax.fori_loop(1, 8, group_start, 0)

    def group_wait(off, carry):
        group_copy(off).wait_recv()
        return carry

    lax.fori_loop(1, 8, group_wait, 0)

    def choose(to, carry):
        target = group * TENSOR + to
        index = jnp.int32(0)
        found = jnp.float32(0)
        for slot in range(GROUPS * CONVS):
            hit = dest_ref[conv_ref[slot]] == target
            index = jnp.where(hit, slot, index)
            found = jnp.where(hit, 1.0, found)
        new_send[to] = (new_all[index].astype(F32) * found).astype(BF16)
        return carry

    lax.fori_loop(0, TENSOR, choose, 0)
    mine_copy = pltpu.make_async_copy(
        new_send.at[tensor], new_pages.at[tensor], local_sem.at[6]
    )
    mine_copy.start()

    def page_copy(off):
        to = lax.rem(tensor + off, TENSOR)
        return remote(
            new_send.at[to],
            new_pages.at[tensor],
            page_send.at[off],
            page_recv.at[off],
            group,
            to,
        )

    def page_start(off, carry):
        page_copy(off).start()
        return carry

    lax.fori_loop(1, TENSOR, page_start, 0)

    mine_copy.wait()
    for copy in keep:
        copy.wait()
    for copy in sent:
        copy.wait_send()
    kv_copy.wait_send()
    query_copy.wait()

    def group_end(off, carry):
        group_copy(off).wait_send()
        return carry

    lax.fori_loop(1, 8, group_end, 0)

    def page_end(off, carry):
        page_copy(off).wait()
        return carry

    lax.fori_loop(1, TENSOR, page_end, 0)

    def pool_end(off, carry):
        first, second = pool_copies(off)
        first.wait()
        second.wait()
        return carry

    lax.fori_loop(1, 64, pool_end, 0)


def attend_kernel(
    lists,
    got_k,
    got_v,
    query_own,
    query_other,
    key_new,
    value_new,
    mixed_own,
    mixed_other,
    lse_own,
    lse_other,
):
    half = HEADS * SUF
    token = row_iota((SUF, 2 * half))
    causal = row_iota((SUF, half)) <= (lane_iota((SUF, half)) & (SUF - 1))
    step = 4

    def one(i, carry):
        first = query_own[i]
        both = jnp.concatenate([first, query_other[i]], axis=0)
        rows = pl.ds(pl.multiple_of(i * SUF, SUF), SUF)
        scores = lax.dot_general(
            key_new[rows, :], first, (((1,), (1,)), ((), ())), preferred_element_type=F32
        )
        scores = jnp.where(causal, scores * SCALE, NEGATIVE)
        peak = jnp.max(scores, axis=0, keepdims=True)
        weights = jnp.exp2(scores - peak)
        total = jnp.sum(weights, axis=0, keepdims=True)
        accum = lax.dot_general(
            value_new[rows, :],
            weights.astype(BF16),
            (((0,), (0,)), ((), ())),
            preferred_element_type=F32,
        )
        peak = jnp.concatenate([peak, jnp.full((1, half), NEGATIVE, F32)], axis=1)
        total = jnp.concatenate([total, jnp.zeros((1, half), F32)], axis=1)
        accum = jnp.concatenate([accum, jnp.zeros((HD, half), F32)], axis=1)
        count = lists[PAGES, i]

        def block(b, state):
            peak, total, accum = state
            codes = [lists[b * step + p, i] for p in range(step)]
            where = [code >> 7 for code in codes]
            keys = jnp.concatenate([got_k[w] for w in where], axis=0)
            values = jnp.concatenate([got_v[w] for w in where], axis=0)
            scores = lax.dot_general(
                keys, both, (((1,), (1,)), ((), ())), preferred_element_type=F32
            )
            scores = jnp.concatenate(
                [
                    jnp.where(
                        token < (codes[p] & 127),
                        scores[p * PAGE : (p + 1) * PAGE] * SCALE,
                        NEGATIVE,
                    )
                    for p in range(step)
                ],
                axis=0,
            )
            fresh = jnp.maximum(peak, jnp.max(scores, axis=0, keepdims=True))
            shrink = jnp.exp2(peak - fresh)
            weights = jnp.exp2(scores - fresh)
            total = total * shrink + jnp.sum(weights, axis=0, keepdims=True)
            accum = accum * shrink + lax.dot_general(
                values,
                weights.astype(BF16),
                (((0,), (0,)), ((), ())),
                preferred_element_type=F32,
            )
            return fresh, total, accum

        peak, total, accum = lax.fori_loop(
            0, (count + step - 1) >> 2, block, (peak, total, accum)
        )
        some = total > 0.0
        safe = jnp.where(some, total, 1.0)
        mixed = (accum / safe).astype(BF16)
        lse = jnp.where(some, peak + jnp.log(safe) * (1.0 / LN2), NEGATIVE)
        lse = jnp.broadcast_to(lse, (8, 2 * half))
        mixed_own[i] = mixed[:, :half]
        mixed_other[i] = mixed[:, half:]
        lse_own[i] = lse[:, :half]
        lse_other[i] = lse[:, half:]
        return carry

    lax.fori_loop(0, CONVS, one, 0)


def reduce_kernel(
    conv_ref,
    suffix_ref,
    mixed_own,
    mixed_other,
    lse_own,
    lse_other,
    w_out,
    out_ref,
    weights,
    mixed_got,
    lse_got,
    mixed,
    part,
    ring_a,
    ring_b,
    small_a,
    small_b,
    local_sem,
    pair_send,
    pair_recv,
    ring_send,
    ring_recv,
):
    group, tensor, y, core, x, z = place()
    pair_z = z + 1 - 2 * lax.rem(z, 2)
    load = pltpu.make_async_copy(w_out, weights, local_sem.at[0])
    load.start()
    x_up, x_down = lax.rem(x + 1, 4), lax.rem(x + 3, 4)
    z_up, z_down = lax.rem(z + 1, 4), lax.rem(z + 3, 4)
    x_far, z_far = lax.rem(x + 2, 4), lax.rem(z + 2, 4)
    to_x_up, to_x_down = x_up * 4 + z, x_down * 4 + z
    to_z_up, to_z_down = x * 4 + z_up, x * 4 + z_down
    barrier = pltpu.get_barrier_semaphore()
    for to in (to_x_up, to_x_down, to_z_up, to_z_down):
        pl.semaphore_signal(barrier, inc=1, device_id=(group, to), device_id_type=MESH)
    pl.semaphore_wait(barrier, 4)

    pair = x * 4 + pair_z
    mixed_copy = remote(mixed_other, mixed_got, pair_send.at[0], pair_recv.at[0], group, pair)
    lse_copy = remote(lse_other, lse_got, pair_send.at[1], pair_recv.at[1], group, pair)
    lse_copy.start()
    mixed_copy.start()
    lse_copy.wait()
    mixed_copy.wait()
    half = HEADS * SUF
    row_of = lane_iota((1, half)) & (SUF - 1)
    for i in range(CONVS):
        first, second = lse_own[i, 0:1, :], lse_got[i, 0:1, :]
        peak = jnp.maximum(first, second)
        first, second = jnp.exp2(first - peak), jnp.exp2(second - peak)
        scale = jnp.where(row_of < suffix_ref[conv_ref[group * CONVS + i]], 1.0, 0.0)
        scale = scale / (first + second)
        joined = mixed_own[i].astype(F32) * (first * scale) + mixed_got[i].astype(F32) * (
            second * scale
        )
        turned = jnp.transpose(joined).astype(BF16)
        for head in range(HEADS):
            mixed[i * SUF : (i + 1) * SUF, head * HD : (head + 1) * HD] = turned[
                head * SUF : (head + 1) * SUF, :
            ]
    load.wait()

    def project(bx, carry):
        for bz in range(4):
            columns = pl.ds(pl.multiple_of((bx * 4 + bz) * PART, PART), PART)
            part[bx, bz] = jnp.dot(
                mixed[...], weights[:, columns], preferred_element_type=F32
            ).astype(BF16)
        return carry

    lax.fori_loop(0, 4, project, 0)

    pending = []

    class Ring:
        def __init__(self, base, first_sem, pick, buffers, ups):
            self.base, self.sem, self.pick, self.buffers = base, first_sem, pick, buffers
            self.up, self.down, self.me, self.far, self.to_up, self.to_down = ups
            self.top, self.bottom = pl.ds(base, 64), pl.ds(base + 64, 64)

        def send(self, index, ref, to):
            sem = self.sem + index
            copy = remote(
                ref,
                self.buffers.at[index],
                ring_send.at[sem],
                ring_recv.at[sem],
                group,
                to,
            )
            copy.start()
            pending.append(copy)
            return copy

        def start(self):
            pick = self.pick
            self.c0 = self.send(0, pick(self.far, self.top), self.to_up)
            self.c1 = self.send(1, pick(self.far, self.bottom), self.to_down)
            self.c2 = self.send(2, pick(self.up, self.bottom), self.to_up)
            self.c3 = self.send(3, pick(self.down, self.top), self.to_down)

        def add(self, ref, *indices):
            total = ref[...].astype(F32)
            for index in indices:
                total = total + self.buffers[index].astype(F32)
            ref[...] = total.astype(BF16)

        def relay(self):
            pick = self.pick
            self.c0.wait_recv()
            self.add(pick(self.up, self.top), 0)
            self.c4 = self.send(4, pick(self.up, self.top), self.to_up)
            self.c1.wait_recv()
            self.add(pick(self.down, self.bottom), 1)
            self.c5 = self.send(5, pick(self.down, self.bottom), self.to_down)

        def finish(self):
            pick = self.pick
            self.c3.wait_recv()
            self.c4.wait_recv()
            self.add(pick(self.me, self.top), 3, 4)
            self.c2.wait_recv()
            self.c5.wait_recv()
            self.add(pick(self.me, self.bottom), 2, 5)

    along_x = (x_up, x_down, x, x_far, to_x_up, to_x_down)
    along_z = (z_up, z_down, z, z_far, to_z_up, to_z_down)
    big_a = Ring(0, 0, lambda j, rows: part.at[:, j, rows], ring_a, along_z)
    big_b = Ring(128, 6, lambda j, rows: part.at[j, :, rows], ring_b, along_x)
    end_a = Ring(0, 12, lambda j, rows: part.at[j, z, rows], small_a, along_x)
    end_b = Ring(128, 18, lambda j, rows: part.at[x, j, rows], small_b, along_z)
    big_a.start()
    big_b.start()
    big_a.relay()
    big_b.relay()
    big_a.finish()
    end_a.start()
    big_b.finish()
    end_b.start()
    end_a.relay()
    end_b.relay()
    end_a.finish()
    end_b.finish()
    out_ref[...] = part[x, z]
    for copy in pending:
        copy.wait_send()


def any_spec():
    return pl.BlockSpec(memory_space=pl.ANY)


def vmem_spec():
    return pl.BlockSpec(memory_space=pltpu.VMEM)


def smem_spec():
    return pl.BlockSpec(memory_space=pltpu.SMEM)


def shards(
    hidden_states,
    norm_gain,
    w_query,
    b_query,
    w_key,
    b_key,
    w_value,
    b_value,
    w_out,
    pool_keys,
    pool_values,
    conv_slots,
    page_table,
    prefix_len,
    suffix_len,
    new_dest,
):
    dma = pltpu.SemaphoreType.DMA
    freq = THETA ** (-(np.arange(HD // 2, dtype=np.float64) * 2.0 / HD))
    freq = jnp.asarray(np.concatenate([freq, freq])[None, :], F32)
    shape = jax.ShapeDtypeStruct
    got_k, got_v, query_own, query_other, key_new, value_new, lists, new_pages = pl.pallas_call(
        gather_kernel,
        out_shape=[
            shape((64, 2, PAGE, HD), BF16),
            shape((64, 2, PAGE, HD), BF16),
            shape((CONVS, HEADS * SUF, HD), BF16),
            shape((CONVS, HEADS * SUF, HD), BF16),
            shape((ROWS, HD), BF16),
            shape((ROWS, HD), BF16),
            shape((PAGES + 8, HD), I32),
            shape((TENSOR, SUF, HD), BF16),
        ],
        in_specs=[smem_spec()] * 4
        + [vmem_spec()]
        + [any_spec()] * 6
        + [vmem_spec()] * 5,
        out_specs=[
            any_spec(),
            any_spec(),
            vmem_spec(),
            any_spec(),
            vmem_spec(),
            vmem_spec(),
            vmem_spec(),
            any_spec(),
        ],
        scratch_shapes=[
            pltpu.VMEM((4, 4, ROWS, PART), BF16),
            pltpu.VMEM((WIDTH, HEADS * HD), BF16),
            pltpu.VMEM((WIDTH, HD // 2), BF16),
            pltpu.VMEM((WIDTH, HD // 2), BF16),
            pltpu.VMEM((ROWS, HEADS * HD), F32),
            pltpu.VMEM((ROWS, HD // 2), F32),
            pltpu.VMEM((ROWS, HD // 2), F32),
            pltpu.VMEM((ROWS, HD), BF16),
            pltpu.VMEM((ROWS, HD), BF16),
            pltpu.VMEM((GROUPS * CONVS, SUF, HD), BF16),
            pltpu.VMEM((TENSOR, SUF, HD), BF16),
            dma((8,)),
            dma((16,)),
            dma((16,)),
            dma((2, 64)),
            dma((2, 64)),
            dma((2,)),
            dma((2,)),
            dma((8,)),
            dma((8,)),
            dma((16,)),
            dma((16,)),
        ],
        compiler_params=pltpu.CompilerParams(
            collective_id=0, has_side_effects=True, vmem_limit_bytes=48 * 1024 * 1024
        ),
        name="gather",
    )(
        conv_slots,
        prefix_len,
        suffix_len,
        new_dest,
        page_table,
        hidden_states,
        pool_keys,
        pool_values,
        w_query,
        w_key,
        w_value,
        norm_gain.astype(F32).reshape(TENSOR, 1, PART),
        b_query.reshape(1, HEADS * HD),
        b_key.reshape(1, HD // 2),
        b_value.reshape(1, HD // 2),
        freq,
    )
    mixed_own, mixed_other, lse_own, lse_other = pl.pallas_call(
        attend_kernel,
        out_shape=[
            shape((CONVS, HD, HEADS * SUF), BF16),
            shape((CONVS, HD, HEADS * SUF), BF16),
            shape((CONVS, 8, HEADS * SUF), F32),
            shape((CONVS, 8, HEADS * SUF), F32),
        ],
        in_specs=[smem_spec()] + [vmem_spec()] * 6,
        out_specs=[vmem_spec()] * 4,
        compiler_params=pltpu.CompilerParams(vmem_limit_bytes=32 * 1024 * 1024),
        name="attend",
    )(
        lists,
        got_k.reshape(128, PAGE, HD),
        got_v.reshape(128, PAGE, HD),
        query_own,
        query_other,
        key_new,
        value_new,
    )
    attn_out = pl.pallas_call(
        reduce_kernel,
        out_shape=shape((ROWS, PART), BF16),
        in_specs=[smem_spec()] * 2 + [vmem_spec()] * 4 + [any_spec()],
        out_specs=vmem_spec(),
        scratch_shapes=[
            pltpu.VMEM((HEADS * HD, WIDTH), BF16),
            pltpu.VMEM((CONVS, HD, HEADS * SUF), BF16),
            pltpu.VMEM((CONVS, 8, HEADS * SUF), F32),
            pltpu.VMEM((ROWS, HEADS * HD), BF16),
            pltpu.VMEM((4, 4, ROWS, PART), BF16),
            pltpu.VMEM((6, 4, 64, PART), BF16),
            pltpu.VMEM((6, 4, 64, PART), BF16),
            pltpu.VMEM((6, 64, PART), BF16),
            pltpu.VMEM((6, 64, PART), BF16),
            dma((1,)),
            dma((2,)),
            dma((2,)),
            dma((24,)),
            dma((24,)),
        ],
        compiler_params=pltpu.CompilerParams(
            collective_id=1, has_side_effects=True, vmem_limit_bytes=40 * 1024 * 1024
        ),
        name="reduce",
    )(conv_slots, suffix_len, mixed_own, mixed_other, lse_own, lse_other, w_out)
    pages = new_pages.reshape(TENSOR // 2, 2, SUF, HD)
    return (attn_out, pages[None, :, 0], pages[None, :, 1])


def solution(mesh):
    in_specs = (
        P("group", "tensor"),
        P(),
        P(None, "tensor"),
        P("tensor"),
        P(None, "tensor"),
        P("tensor"),
        P(None, "tensor"),
        P("tensor"),
        P("tensor", None),
        P(("group", "tensor"), None, None, None),
        P(("group", "tensor"), None, None, None),
        P(),
        P(),
        P(),
        P(),
        P(),
    )
    out_specs = (
        P("group", "tensor"),
        P(("group", "tensor"), None, None, None),
        P(("group", "tensor"), None, None, None),
    )
    return jax.shard_map(shards, mesh=mesh, in_specs=in_specs, out_specs=out_specs, check_vma=False)
```

time: 385 us -> 196 us (0.51)
  waiting for transfers between devices: 212 us -> 0 us
  Pallas kernels: 0 us -> 184 us
  matrix products: 73.6 us -> 0 us
  other arithmetic: 28.6 us -> 0.72 us
  local copies, waits for them, and re-layouts: 37.5 us -> 10.2 us
  starting transfers between devices: 17.1 us -> 0 us
  between operations: 14 us -> 0.78 us
    pallas_call x0 -> x3, Pallas kernels: none -> 184 us  [the longest x1 130 us: shards(): pl.pallas_call(gather_kernel, out_shape=[shape((64, 2, PAGE, HD), BF16),...]
    dot_general x40 -> x0, matrix products: 73.6 us -> none  [the longest x17 21.7 us: attend(): jnp.einsum('hrb,bd->hrd', weights.astype(jnp.bfloat16), values, preferred...]
    all_gather x3 -> x0, waiting for transfers between devices: 58.7 us -> none  [the longest x1 58.7 us: shards(): features = lax.all_gather(hidden_states, 'tensor', axis=1, tiled=True)]
    all_to_all x2 -> x0, waiting for transfers between devices: 58.3 us -> none  [the longest x1 50.4 us: shards(): lax.all_to_all(arrange(pool_keys), ('group', 'tensor'), split_axis=0, con...]
    reduce_scatter x1 -> x0, waiting for transfers between devices: 55.1 us -> none  [shards(): lax.psum_scatter(partial_value.astype(jnp.bfloat16), 'tensor', scatter_di...]
    ppermute x2 -> x0, waiting for transfers between devices: 39.6 us -> none  [from_partner(): return lax.ppermute(value, axis, pairs)]
    reduce_sum x23 -> x0, other arithmetic: 19.5 us -> none  [the longest x17 14.9 us: attend(): total = total * shrink + jnp.sum(weights, axis=-1)]
    dynamic_slice x49 -> x0, local copies, waits for them, and re-layouts: 19.2 us -> none  [the longest x16 17.2 us: step_block(): lax.dynamic_slice_in_dim(values_src, start, block_pages, 0)]
  transfers between devices with their start and end apart: 8 -> 0, of which waited for: 6 -> 0; matrix products, arithmetic and copies ran while one was open for 33% -> 0% of each run, Pallas kernels for 0% -> 0%
where the time goes in v1:
time: 196 us
  Pallas kernels  184 us (94%)
  local copies, waits for them, and re-layouts  10.2 us (5%)
    pallas_call x1, Pallas kernels, shards(): pl.pallas_call(gather_kernel, out_shape=[shape((64, 2, PAGE, HD), BF16),...  130 us
    pallas_call x1, Pallas kernels, shards(): pl.pallas_call(reduce_kernel, out_shape=shape((ROWS, PART), BF16), in_spe...  43.8 us
    pallas_call x1, Pallas kernels, shards(): pl.pallas_call(attend_kernel, out_shape=[shape((CONVS, HD, HEADS * SUF),...  9.72 us
    unnamed x25, local copies, waits for them, and re-layouts  8.67 us

profile of v1, /device:TPU:0, one launch (start us, length us, event | category | flops | bytes accessed | tf_op | source)
XLA Modules:
  0.0 195.5 jit_solution(13378063204037691822)
XLA Ops:
  0.6 0.0 copy-start.10
  0.6 0.8 reshape.31.b_query
  1.4 0.7 reshape.37
  2.1 2.7 %copy.20.w_key = bf16[8192,64]{1,0:T(8,128)(2,1)} copy(bf16[8192,64]{0,1:T(8,128)(2,1)} %param.21) | data formatting | bytes 2097152 | tf_op args[4]
  4.9 0.0 copy-done.10
  4.9 0.0 copy-start.1
  4.9 0.0 copy-start.2
  4.9 0.0 copy-start.3
  4.9 0.0 copy-start.4
  4.9 0.0 copy-start.5
  4.9 0.0 copy-start.6
  4.9 0.0 copy-start.7
  4.9 0.0 copy-start.8
  5.0 0.0 copy-start.9
  5.0 1.8 copy.21.w_value
  6.8 0.0 copy-done.1
  6.8 0.0 copy-done.2
  6.8 0.0 copy-done.3
  6.8 0.0 copy-done.4
  6.8 0.0 copy-done.5
  6.8 0.0 copy-done.6
  6.8 0.0 copy-done.7
  6.8 0.0 copy-done.8
  6.8 0.0 copy-done.9
  6.8 130.3 %gather.1 = (bf16[64,2,64,128]{3,2,1,0:T(8,128)(2,1)S(1)}, bf16[64,2,64,128]{3,2,1,0:T(8,128)(2,1)S(1)}, bf16[4,256,128]{2,1,0:T(8,128)(2,1)S(1)}, bf16[4,256,12...) custom-call(s32[32]{0:T(128)S(1)} %copy-done.3, ...), custom_call_target="tpu_custom_call" | custom-call | tf_op jit(solution)/shard_map/gather/pallas_call | solution.py:711
  137.2 9.7 %attend.1 = (bf16[4,128,256]{2,1,0:T(8,128)(2,1)S(1)}, bf16[4,128,256]{2,1,0:T(8,128)(2,1)S(1)}, f32[4,8,256]{2,1,0:T(8,128)S(1)}, f32[4,8,256]{2,1,0:T(8,128)S(1)}) custom-call(s32[72,128]{1,0:T(8,128)S(1)} %get-tuple-element.15.lists, bf16[128,64,128]{2,1,0:T(8,128)(2,1)S(1)} %bitcast.14, bf16[128,64,128]{2,1,0:T(8,128)(2,1)S(1)} %bitcast.15, ...), custom_call_target="tpu_custom_call" | custom-call | tf_op jit(solution)/shard_map/attend/pallas_call | solution.py:783
  146.9 0.0 copy-start
  146.9 3.4 %copy-done = bf16[512,8192]{1,0:T(8,128)(2,1)S(1)} copy-done((bf16[512,8192]{1,0:T(8,128)(2,1)S(1)}, bf16[512,8192]{1,0:T(8,128)(2,1)}, u32[]{:S(2)}) %copy-start) | copy-done | bytes 8388632
  150.3 43.8 %reduce.1 = bf16[256,512]{1,0:T(8,128)(2,1)S(1)} custom-call(s32[32]{0:T(128)S(1)} %copy-done.3, s32[32]{0:T(128)S(1)} %copy-done.4, bf16[4,128,256]{2,1,0:T(8,128)(2,1)S(1)} %get-tuple-element.22.mixed_own, bf16[4,128,256]{2,1,0:T(8,128)(2,1)S(1)} %get-tuple-element.23.mixed_other, f32[4,8,256]{2,1,0:T(8,128)S(1)} %get-tuple-element.24.lse_own, ...), custom_call_target="tpu_custom_call" | custom-call | tf_op jit(solution)/shard_map/reduce/pallas_call | solution.py:804
  194.1 0.7 slice_bitcast_fusion
  194.8 0.7 copy.27
Async XLA Ops:
  0.6 4.2 %copy-start.10 = (bf16[8192,64]{0,1:T(8,128)(2,1)S(1)}, bf16[8192,64]{0,1:T(8,128)(2,1)}, u32[]{:S(2)}) copy-start(bf16[8192,64]{0,1:T(8,128)(2,1)} %param.23) | copy-start | bytes 3145732
  4.9 1.9 copy-start.1
  4.9 1.9 copy-start.2
  4.9 1.9 copy-start.3
  4.9 1.9 copy-start.4
  4.9 1.9 copy-start.5
  4.9 1.9 copy-start.6
  4.9 1.9 copy-start.7
  4.9 1.9 copy-start.8
  5.0 1.9 copy-start.9
  146.9 3.4 %copy-start = (bf16[512,8192]{1,0:T(8,128)(2,1)S(1)}, bf16[512,8192]{1,0:T(8,128)(2,1)}, u32[]{:S(2)}) copy-start(bf16[512,8192]{1,0:T(8,128)(2,1)} %w_out.1) | copy-start | bytes 25165828

commit v2 on v1

v2 whole, which is shorter than its diff:
```python
import jax
import jax.numpy as jnp
import numpy as np
from jax import lax
from jax.experimental import pallas as pl
from jax.experimental.pallas import tpu as pltpu
from jax.sharding import PartitionSpec as P

HD = 128
SUF = 64
CONVS = 4
ROWS = CONVS * SUF
GROUPS = 8
TENSOR = 16
WIDTH = 8192
PART = WIDTH // TENSOR
PAGES = 64
PAGE = 64
HEADS = 4
THETA = 1000000.0
EPSILON = 1e-06
NEGATIVE = -1e30
SCALE = HD**-0.5 * 1.4426950408889634
LN2 = 0.6931471805599453
MESH = pl.DeviceIdType.MESH
BF16 = jnp.bfloat16
F32 = jnp.float32
I32 = jnp.int32


def remote(src, dst, send_sem, recv_sem, group, tensor):
    return pltpu.make_async_remote_copy(
        src_ref=src,
        dst_ref=dst,
        send_sem=send_sem,
        recv_sem=recv_sem,
        device_id=(group, tensor),
        device_id_type=MESH,
    )


def place():
    group = lax.axis_index("group")
    tensor = lax.axis_index("tensor")
    return (
        group,
        tensor,
        lax.div(group, 2),
        lax.rem(group, 2),
        lax.div(tensor, 4),
        lax.rem(tensor, 4),
    )


def lane_iota(shape):
    return lax.broadcasted_iota(I32, shape, len(shape) - 1)


def row_iota(shape):
    return lax.broadcasted_iota(I32, shape, len(shape) - 2)


def gather_kernel(
    conv_ref,
    prefix_ref,
    suffix_ref,
    dest_ref,
    table_ref,
    hidden,
    pool_k,
    pool_v,
    w_query,
    w_key,
    w_value,
    gain_ref,
    b_query,
    b_key,
    b_value,
    freq_ref,
    got_k,
    got_v,
    queries,
    key_new,
    value_new,
    lists,
    new_pages,
    feat,
    wq,
    wkv,
    acc_q,
    acc_kv,
    squares,
    stage_k,
    stage_v,
    query_own,
    kv_own,
    kv_other,
    new_all,
    new_send,
    load_sem,
    keep_sem,
    feat_send,
    feat_recv,
    y_send,
    y_recv,
    x_send,
    x_recv,
    pair_send,
    pair_recv,
    group_send,
    group_recv,
    page_send,
    page_recv,
):
    group, tensor, y, core, x, z = place()
    parity = lax.rem(z, 2)
    partner_z = [z, z + 1 - 2 * parity, lax.rem(z + 2, 4), 3 - z]
    own = pltpu.make_async_copy(hidden, feat.at[x, z], load_sem.at[0])
    own.start()
    loads = [
        pltpu.make_async_copy(w_query, wq, load_sem.at[1]),
        pltpu.make_async_copy(w_key, wkv.at[pl.ds(0, HD // 2)], load_sem.at[2]),
        pltpu.make_async_copy(w_value, wkv.at[pl.ds(HD // 2, HD // 2)], load_sem.at[3]),
    ]
    for load in loads:
        load.start()

    def group_at(shift):
        to_y = lax.rem(y + shift // 2, 4)
        to_core = lax.rem(core + shift % 2, 2)
        return to_y * 2 + to_core

    barrier = pltpu.get_barrier_semaphore()
    for shift in range(1, GROUPS):
        pl.semaphore_signal(
            barrier, inc=1, device_id=(group_at(shift), tensor), device_id_type=MESH
        )

    def greet(off, carry):
        to = lax.rem(tensor + off, TENSOR)
        pl.semaphore_signal(barrier, inc=1, device_id=(group, to), device_id_type=MESH)
        return carry

    lax.fori_loop(1, TENSOR, greet, 0)
    pl.semaphore_wait(barrier, GROUPS - 1 + TENSOR - 1)

    own.wait()
    x_at = [lax.rem(x + shift, 4) for shift in range(4)]
    z_up, z_far, z_down = (lax.rem(z + shift, 4) for shift in (1, 2, 3))
    to_x_up, to_x_down = x_at[1] * 4 + z, x_at[3] * 4 + z
    to_z_up, to_z_down = x * 4 + z_up, x * 4 + z_down
    half_rows = ROWS // 2
    low_rows, high_rows = pl.ds(0, half_rows), pl.ds(half_rows, half_rows)
    sent = []
    kept = []

    def pass_on(index, ref, to):
        copy = remote(ref, ref, feat_send.at[index], feat_recv.at[index], group, to)
        copy.start()
        sent.append(copy)
        return copy

    def spread(block, shift):
        ref = feat.at[x_at[shift], z]
        return (
            pass_on(4 + 4 * block, ref, to_z_up),
            pass_on(5 + 4 * block, ref, to_z_down),
        )

    def spread_on(block, shift, copies):
        copies[0].wait_recv()
        first = pass_on(6 + 4 * block, feat.at[x_at[shift], z_down, low_rows], to_z_up)
        copies[1].wait_recv()
        second = pass_on(7 + 4 * block, feat.at[x_at[shift], z_up, high_rows], to_z_down)
        return first, second

    pools, stages, gots = (pool_k, pool_v), (stage_k, stage_v), (got_k, got_v)

    def y_copy(kind, shift):
        to_group = group_at(shift)
        return remote(
            pools[kind].at[pl.ds(2 * to_group, 2)],
            stages[kind].at[shift],
            y_send.at[kind, shift],
            y_recv.at[kind, shift],
            to_group,
            tensor,
        )

    def x_copies(kind, shift):
        for step in (1, 3, 2, 0):
            heads = pl.ds(2 * x_at[step], 2)
            if shift == 0:
                source = pools[kind].at[pl.ds(2 * group, 2), heads]
            else:
                source = stages[kind].at[shift, :, heads]
            target = gots[kind].at[step, shift]
            if step == 0:
                copy = pltpu.make_async_copy(source, target, keep_sem.at[kind, shift])
                copy.start()
                kept.append(copy)
            else:
                copy = remote(
                    source,
                    target,
                    x_send.at[kind, shift, step],
                    x_recv.at[kind, shift, step],
                    group,
                    x_at[step] * 4 + z,
                )
                copy.start()
                pages_out.append(copy)

    pages_out = []
    y_out = []
    y_items = [
        (kind, shifts) for shifts in ((2, 6), (3, 7), (4,), (5,)) for kind in range(2)
    ]
    y_running = {}

    def y_start(item):
        if item < len(y_items):
            kind, shifts = y_items[item]
            y_running[item] = [y_copy(kind, shift) for shift in shifts]
            for copy in y_running[item]:
                copy.start()
                y_out.append(copy)

    def y_step(item):
        kind, shifts = y_items[item]
        for copy in y_running[item]:
            copy.wait_recv()
        y_start(item + 2)
        for shift in shifts:
            x_copies(kind, shift)

    f0 = pass_on(0, feat.at[x, z], to_x_up)
    f1 = pass_on(1, feat.at[x, z], to_x_down)
    across = [y_copy(0, 1), y_copy(1, 1)]
    for copy in across:
        copy.start()
        y_out.append(copy)
    y_start(0)
    y_start(1)
    s0 = spread(0, 0)
    x_copies(0, 0)
    x_copies(1, 0)
    f0.wait_recv()
    f2 = pass_on(2, feat.at[x_at[3], z, low_rows], to_x_up)
    s1 = spread(1, 3)
    f1.wait_recv()
    f3 = pass_on(3, feat.at[x_at[1], z, high_rows], to_x_down)
    s2 = spread(2, 1)
    for kind in range(2):
        across[kind].wait_recv()
        x_copies(kind, 1)

    prefix = [prefix_ref[conv_ref[group * CONVS + i]] for i in range(CONVS)]
    suffix = [suffix_ref[conv_ref[group * CONVS + i]] for i in range(CONVS)]

    offsets = row_iota((SUF, HD))
    positions = jnp.concatenate([offsets + prefix[i] for i in range(CONVS)], axis=0)
    angle = positions.astype(F32) * freq_ref[...]
    cosine = jnp.cos(angle)
    sine = jnp.sin(angle)
    sine = jnp.where(lane_iota((ROWS, HD)) < HD // 2, -sine, sine)

    y_step(0)
    r0 = spread_on(0, 0, s0)

    page_ids = lane_iota((1, PAGES))
    below = (row_iota((PAGES, PAGES)) < lane_iota((PAGES, PAGES))).astype(F32)
    lane = lane_iota((PAGES, HD))
    table = jnp.zeros((PAGES, HD), F32)
    counts = jnp.zeros((8, HD), F32)
    for i in range(CONVS):
        entry = table_ref[pl.ds(conv_ref[group * CONVS + i], 1), :]
        source = entry >> 4
        source_y, source_core = source >> 5, (source >> 4) & 1
        source_x, source_z = (source >> 2) & 3, source & 3
        live = jnp.clip(prefix[i] - page_ids * PAGE, 0, PAGE)
        here = (source_z == z) & (live > 0)
        where = ((x - source_x) & 3) * GROUPS
        where = where + ((y - source_y) & 3) * 2 + ((core - source_core) & 1)
        value = ((where * 2 + (entry & 1)) * 128 + live).astype(F32)
        here_f = here.astype(F32)
        order = jnp.dot(
            jnp.broadcast_to(here_f, (8, PAGES)), below, preferred_element_type=F32
        )[0:1, :]
        match = (order == row_iota((PAGES, PAGES)).astype(F32)) & (
            jnp.broadcast_to(here_f, (PAGES, PAGES)) > 0.5
        )
        column = jnp.sum(jnp.where(match, value, 0.0), axis=1, keepdims=True)
        table = jnp.where(lane == i, column, table)
        counts = jnp.where(
            lane_iota((8, HD)) == i, jnp.sum(here_f, axis=1, keepdims=True), counts
        )
    counts = jnp.where(
        lane_iota((8, HD)) == CONVS, lax.div(z, 2).astype(F32), counts
    )
    lists[pl.ds(0, PAGES), :] = table.astype(I32)
    lists[pl.ds(PAGES, 8), :] = counts.astype(I32)

    f2.wait_recv()
    f3.wait_recv()
    s3 = spread(3, 2)
    for load in loads:
        load.wait()
    acc_q[...] = jnp.zeros_like(acc_q)
    acc_kv[...] = jnp.zeros_like(acc_kv)
    squares[...] = jnp.zeros_like(squares)

    def project(bz):
        def one(bx, carry):
            block = bx * 4 + bz
            rows = pl.ds(pl.multiple_of(block * PART, PART), PART)
            wide = feat[bx, bz].astype(F32)
            scaled = (wide * gain_ref[block]).astype(BF16)
            acc_q[...] += jnp.dot(scaled, wq[rows, :], preferred_element_type=F32)
            acc_kv[...] += lax.dot_general(
                scaled,
                wkv[:, rows],
                (((1,), (1,)), ((), ())),
                preferred_element_type=F32,
            )
            wide = wide * wide
            total = squares[...]
            for part in range(PART // HD):
                total = total + wide[:, part * HD : (part + 1) * HD]
            squares[...] = total
            return carry

        lax.fori_loop(0, 4, one, 0)

    project(z)
    y_step(1)
    r1 = spread_on(1, 3, s1)
    r2 = spread_on(2, 1, s2)
    y_step(2)
    r3 = spread_on(3, 2, s3)
    project(z_up)
    y_step(3)
    project(z_down)
    y_step(4)
    for copies in (r0, r1, r2, r3):
        for copy in copies:
            copy.wait_recv()
    project(z_far)
    mean = jnp.sum(squares[...], axis=1, keepdims=True) * (1.0 / WIDTH)
    factor = lax.rsqrt(mean + EPSILON)
    bias = jnp.concatenate([b_key[...], b_value[...]], axis=1).astype(F32)
    kv_own[...] = (acc_kv[...] * factor + bias).astype(BF16)
    kv_copy = remote(
        kv_own,
        kv_other,
        pair_send.at[0],
        pair_recv.at[0],
        group,
        x * 4 + partner_z[1],
    )
    kv_copy.start()

    def rotate(values):
        return values * cosine + pltpu.roll(values, HD // 2, 1) * sine

    for head in range(HEADS):
        columns = slice(head * HD, (head + 1) * HD)
        values = acc_q[:, columns] * factor + b_query[:, columns].astype(F32)
        values = rotate(values).astype(BF16)
        for i in range(CONVS):
            query_own[i, head * SUF : (head + 1) * SUF, :] = values[i * SUF : (i + 1) * SUF, :]
    query_out = [
        remote(
            query_own,
            queries.at[r],
            pair_send.at[r],
            pair_recv.at[r],
            group,
            x * 4 + partner_z[r],
        )
        for r in (1, 2, 3)
    ]
    for copy in query_out:
        copy.start()
    query_keep = pltpu.make_async_copy(query_own, queries.at[0], load_sem.at[4])
    query_keep.start()
    y_step(5)

    kv_copy.wait_recv()
    mine = kv_own[...].astype(F32)
    theirs = kv_other[...].astype(F32)
    even = jnp.where(parity == 0, mine, theirs)
    odd = jnp.where(parity == 0, theirs, mine)
    low = lane_iota((ROWS, HD)) < HD // 2
    keys = jnp.where(low, even, pltpu.roll(odd, HD // 2, 1))
    keys = rotate(keys)
    values = jnp.where(low, pltpu.roll(even, HD // 2, 1), odd)
    key_new[...] = keys.astype(BF16)
    value_new[...] = values.astype(BF16)

    page = jnp.where(parity == 0, keys.astype(BF16).astype(F32), values)
    live_row = jnp.concatenate([offsets < suffix[i] for i in range(CONVS)], axis=0)
    page = jnp.where(live_row, page, 0.0).astype(BF16)
    new_all[pl.ds(group * CONVS, CONVS)] = page.reshape(CONVS, SUF, HD)
    new_ref = new_all.at[pl.ds(group * CONVS, CONVS)]
    group_out = [
        remote(
            new_ref,
            new_ref,
            group_send.at[shift],
            group_recv.at[shift],
            group_at(shift),
            tensor,
        )
        for shift in range(1, GROUPS)
    ]
    for copy in group_out:
        copy.start()
    y_step(6)
    for copy in group_out:
        copy.wait_recv()

    def choose(to, carry):
        target = group * TENSOR + to
        index = jnp.int32(0)
        found = jnp.float32(0)
        for slot in range(GROUPS * CONVS):
            hit = dest_ref[conv_ref[slot]] == target
            index = jnp.where(hit, slot, index)
            found = jnp.where(hit, 1.0, found)
        new_send[to] = (new_all[index].astype(F32) * found).astype(BF16)
        return carry

    lax.fori_loop(0, TENSOR, choose, 0)
    mine_copy = pltpu.make_async_copy(
        new_send.at[tensor], new_pages.at[tensor], load_sem.at[5]
    )
    mine_copy.start()

    def page_copy(off):
        to = lax.rem(tensor + off, TENSOR)
        return remote(
            new_send.at[to],
            new_pages.at[tensor],
            page_send.at[off],
            page_recv.at[off],
            group,
            to,
        )

    def page_start(off, carry):
        page_copy(off).start()
        return carry

    lax.fori_loop(1, TENSOR, page_start, 0)
    y_step(7)

    mine_copy.wait()
    query_keep.wait()
    kv_copy.wait_send()
    for copy in query_out:
        copy.wait()
    for copy in sent + y_out + group_out:
        copy.wait_send()

    def page_end(off, carry):
        page_copy(off).wait()
        return carry

    lax.fori_loop(1, TENSOR, page_end, 0)
    for copy in kept + pages_out:
        copy.wait()


def attend_kernel(lists, got_k, got_v, queries, key_new, value_new, mixed_ref, lse_ref):
    half = HEADS * SUF
    token = row_iota((PAGE, 2 * half))
    causal = row_iota((SUF, half)) <= (lane_iota((SUF, half)) & (SUF - 1))
    step = 4
    own_head = lists[PAGES, CONVS]
    heads = (own_head, 1 - own_head)

    def one(i, carry):
        first = queries[0, i]
        query = [
            jnp.concatenate([first, queries[1, i]], axis=0),
            jnp.concatenate([queries[2, i], queries[3, i]], axis=0),
        ]
        rows = pl.ds(pl.multiple_of(i * SUF, SUF), SUF)
        scores = lax.dot_general(
            key_new[rows, :], first, (((1,), (1,)), ((), ())), preferred_element_type=F32
        )
        scores = jnp.where(causal, scores * SCALE, NEGATIVE)
        peak = jnp.max(scores, axis=0, keepdims=True)
        weights = jnp.exp2(scores - peak)
        total = jnp.sum(weights, axis=0, keepdims=True)
        accum = lax.dot_general(
            value_new[rows, :],
            weights.astype(BF16),
            (((0,), (0,)), ((), ())),
            preferred_element_type=F32,
        )
        peak = jnp.concatenate([peak, jnp.full((1, half), NEGATIVE, F32)], axis=1)
        total = jnp.concatenate([total, jnp.zeros((1, half), F32)], axis=1)
        accum = jnp.concatenate([accum, jnp.zeros((HD, half), F32)], axis=1)
        empty = (
            jnp.full((1, 2 * half), NEGATIVE, F32),
            jnp.zeros((1, 2 * half), F32),
            jnp.zeros((HD, 2 * half), F32),
        )
        count = lists[PAGES, i]

        def block(b, state):
            codes = [lists[b * step + p, i] for p in range(step)]
            scores = []
            for slot in range(2):
                keys = jnp.concatenate([got_k[code >> 7, heads[slot]] for code in codes], axis=0)
                scores.append(
                    lax.dot_general(
                        keys,
                        query[slot],
                        (((1,), (1,)), ((), ())),
                        preferred_element_type=F32,
                    )
                )
            out = []
            for slot in range(2):
                peak, total, accum = state[slot]
                values = jnp.concatenate(
                    [got_v[code >> 7, heads[slot]] for code in codes], axis=0
                )
                score = jnp.concatenate(
                    [
                        jnp.where(
                            token < (codes[p] & 127),
                            scores[slot][p * PAGE : (p + 1) * PAGE] * SCALE,
                            NEGATIVE,
                        )
                        for p in range(step)
                    ],
                    axis=0,
                )
                fresh = jnp.maximum(peak, jnp.max(score, axis=0, keepdims=True))
                shrink = jnp.exp2(peak - fresh)
                weights = jnp.exp2(score - fresh)
                total = total * shrink + jnp.sum(weights, axis=0, keepdims=True)
                accum = accum * shrink + lax.dot_general(
                    values,
                    weights.astype(BF16),
                    (((0,), (0,)), ((), ())),
                    preferred_element_type=F32,
                )
                out.append((fresh, total, accum))
            return tuple(out)

        state = lax.fori_loop(
            0, (count + step - 1) >> 2, block, ((peak, total, accum), empty)
        )
        for slot in range(2):
            peak, total, accum = state[slot]
            some = total > 0.0
            safe = jnp.where(some, total, 1.0)
            mixed = (accum / safe).astype(BF16)
            lse = jnp.where(some, peak + jnp.log(safe) * (1.0 / LN2), NEGATIVE)
            lse = jnp.broadcast_to(lse, (8, 2 * half))
            for side in range(2):
                columns = slice(side * half, (side + 1) * half)
                mixed_ref[2 * slot + side, i] = mixed[:, columns]
                lse_ref[2 * slot + side, i] = lse[:, columns]
        return carry

    lax.fori_loop(0, CONVS, one, 0)


X_FIRST = (True, True, False, True)


def reduce_kernel(
    conv_ref,
    suffix_ref,
    mixed_ref,
    lse_ref,
    w_out,
    out_ref,
    weights,
    mixed_got,
    lse_got,
    mixed,
    part,
    big,
    small,
    load_sem,
    mixed_send,
    mixed_recv,
    lse_send,
    lse_recv,
    ring_send,
    ring_recv,
):
    group, tensor, y, core, x, z = place()
    partner_z = [z, z + 1 - 2 * lax.rem(z, 2), lax.rem(z + 2, 4), 3 - z]
    load = pltpu.make_async_copy(w_out, weights, load_sem.at[0])
    load.start()
    x_up, x_far, x_down = (lax.rem(x + shift, 4) for shift in (1, 2, 3))
    z_up, z_far, z_down = (lax.rem(z + shift, 4) for shift in (1, 2, 3))
    to_x_up, to_x_down = x_up * 4 + z, x_down * 4 + z
    to_z_up, to_z_down = x * 4 + z_up, x * 4 + z_down
    barrier = pltpu.get_barrier_semaphore()
    for to in (to_x_up, to_x_down, to_z_up, to_z_down, x * 4 + z_far):
        pl.semaphore_signal(barrier, inc=1, device_id=(group, to), device_id_type=MESH)
    pl.semaphore_wait(barrier, 5)

    lse_out = [
        remote(
            lse_ref.at[r],
            lse_got.at[r],
            lse_send.at[r],
            lse_recv.at[r],
            group,
            x * 4 + partner_z[r],
        )
        for r in (1, 2, 3)
    ]
    mixed_out = [
        [
            remote(
                mixed_ref.at[r, i],
                mixed_got.at[r, i],
                mixed_send.at[r, i],
                mixed_recv.at[r, i],
                group,
                x * 4 + partner_z[r],
            )
            for r in (1, 2, 3)
        ]
        for i in range(CONVS)
    ]
    for copy in lse_out + mixed_out[0] + mixed_out[1]:
        copy.start()
    row_of = lane_iota((1, HEADS * SUF)) & (SUF - 1)
    pending = []

    def combine(i):
        if i == 0:
            for copy in lse_out:
                copy.wait_recv()
        for copy in mixed_out[i]:
            copy.wait_recv()
        if i + 2 < CONVS:
            for copy in mixed_out[i + 2]:
                copy.start()
        logs = [lse_ref[0, i, 0:1, :]] + [lse_got[r, i, 0:1, :] for r in (1, 2, 3)]
        peak = jnp.maximum(jnp.maximum(logs[0], logs[1]), jnp.maximum(logs[2], logs[3]))
        shares = [jnp.exp2(log - peak) for log in logs]
        scale = jnp.where(row_of < suffix_ref[conv_ref[group * CONVS + i]], 1.0, 0.0)
        scale = scale / (shares[0] + shares[1] + shares[2] + shares[3])
        joined = mixed_ref[0, i].astype(F32) * (shares[0] * scale)
        for r in (1, 2, 3):
            joined = joined + mixed_got[r, i].astype(F32) * (shares[r] * scale)
        turned = jnp.transpose(joined).astype(BF16)
        for head in range(HEADS):
            mixed[i, :, head * HD : (head + 1) * HD] = turned[
                head * SUF : (head + 1) * SUF, :
            ]

    class Ring:
        def __init__(self, conv, first, pick, buffers, way):
            self.conv, self.first, self.pick, self.buffers = conv, first, pick, buffers
            self.up, self.down, self.me, self.far, self.to_up, self.to_down = way
            self.top = pl.ds(conv * SUF, SUF // 2)
            self.bottom = pl.ds(conv * SUF + SUF // 2, SUF // 2)

        def send(self, index, ref, to):
            sem = self.first + index
            copy = remote(
                ref,
                self.buffers.at[self.conv, index],
                ring_send.at[sem],
                ring_recv.at[sem],
                group,
                to,
            )
            copy.start()
            pending.append(copy)
            return copy

        def start(self, ready):
            pick = self.pick
            ready(self.far)
            self.c0 = self.send(0, pick(self.far, self.top), self.to_up)
            self.c1 = self.send(1, pick(self.far, self.bottom), self.to_down)
            ready(self.up)
            self.c2 = self.send(2, pick(self.up, self.bottom), self.to_up)
            ready(self.down)
            self.c3 = self.send(3, pick(self.down, self.top), self.to_down)
            ready(self.me)

        def add(self, ref, *indices):
            total = ref[...].astype(F32)
            for index in indices:
                total = total + self.buffers[self.conv, index].astype(F32)
            ref[...] = total.astype(BF16)

        def relay(self):
            pick = self.pick
            self.c0.wait_recv()
            self.add(pick(self.up, self.top), 0)
            self.c4 = self.send(4, pick(self.up, self.top), self.to_up)
            self.c1.wait_recv()
            self.add(pick(self.down, self.bottom), 1)
            self.c5 = self.send(5, pick(self.down, self.bottom), self.to_down)

        def finish(self):
            pick = self.pick
            self.c3.wait_recv()
            self.c4.wait_recv()
            self.add(pick(self.me, self.top), 3, 4)
            self.c2.wait_recv()
            self.c5.wait_recv()
            self.add(pick(self.me, self.bottom), 2, 5)

    along_x = (x_up, x_down, x, x_far, to_x_up, to_x_down)
    along_z = (z_up, z_down, z, z_far, to_z_up, to_z_down)
    firsts, seconds = [], []
    for i in range(CONVS):
        if X_FIRST[i]:
            firsts.append(Ring(i, 12 * i, lambda j, rows: part.at[j, :, rows], big, along_x))
            seconds.append(
                Ring(i, 12 * i + 6, lambda j, rows: part.at[x, j, rows], small, along_z)
            )
        else:
            firsts.append(Ring(i, 12 * i, lambda j, rows: part.at[:, j, rows], big, along_z))
            seconds.append(
                Ring(i, 12 * i + 6, lambda j, rows: part.at[j, z, rows], small, along_x)
            )

    def begin(i):
        combine(i)
        if i == 0:
            load.wait()
        rows = slice(i * SUF, (i + 1) * SUF)

        def ready(j):
            def one(k, carry):
                bx, bz = (j, k) if X_FIRST[i] else (k, j)
                columns = pl.ds(pl.multiple_of((bx * 4 + bz) * PART, PART), PART)
                part[bx, bz, rows] = jnp.dot(
                    mixed[i], weights[:, columns], preferred_element_type=F32
                ).astype(BF16)
                return carry

            lax.fori_loop(0, 4, one, 0)

        firsts[i].start(ready)

    def turn(i):
        firsts[i].finish()
        seconds[i].start(lambda j: None)

    begin(0)
    begin(1)
    firsts[0].relay()
    begin(2)
    firsts[1].relay()
    turn(0)
    begin(3)
    firsts[2].relay()
    turn(1)
    seconds[0].relay()
    firsts[3].relay()
    turn(2)
    seconds[1].relay()
    seconds[0].finish()
    turn(3)
    seconds[2].relay()
    seconds[1].finish()
    seconds[3].relay()
    seconds[2].finish()
    seconds[3].finish()
    out_ref[...] = part[x, z]
    for copy in lse_out + mixed_out[0] + mixed_out[1] + mixed_out[2] + mixed_out[3] + pending:
        copy.wait_send()


def any_spec():
    return pl.BlockSpec(memory_space=pl.ANY)


def vmem_spec():
    return pl.BlockSpec(memory_space=pltpu.VMEM)


def smem_spec():
    return pl.BlockSpec(memory_space=pltpu.SMEM)


def shards(
    hidden_states,
    norm_gain,
    w_query,
    b_query,
    w_key,
    b_key,
    w_value,
    b_value,
    w_out,
    pool_keys,
    pool_values,
    conv_slots,
    page_table,
    prefix_len,
    suffix_len,
    new_dest,
):
    dma = pltpu.SemaphoreType.DMA
    freq = THETA ** (-(np.arange(HD // 2, dtype=np.float64) * 2.0 / HD))
    freq = jnp.asarray(np.concatenate([freq, freq])[None, :], F32)
    shape = jax.ShapeDtypeStruct
    got_k, got_v, queries, key_new, value_new, lists, new_pages = pl.pallas_call(
        gather_kernel,
        out_shape=[
            shape((4, GROUPS, 2, 2, PAGE, HD), BF16),
            shape((4, GROUPS, 2, 2, PAGE, HD), BF16),
            shape((4, CONVS, HEADS * SUF, HD), BF16),
            shape((ROWS, HD), BF16),
            shape((ROWS, HD), BF16),
            shape((PAGES + 8, HD), I32),
            shape((TENSOR, SUF, HD), BF16),
        ],
        in_specs=[smem_spec()] * 4
        + [vmem_spec()]
        + [any_spec()] * 6
        + [vmem_spec()] * 5,
        out_specs=[any_spec()] * 3 + [vmem_spec()] * 3 + [any_spec()],
        scratch_shapes=[
            pltpu.VMEM((4, 4, ROWS, PART), BF16),
            pltpu.VMEM((WIDTH, HEADS * HD), BF16),
            pltpu.VMEM((HD, WIDTH), BF16),
            pltpu.VMEM((ROWS, HEADS * HD), F32),
            pltpu.VMEM((ROWS, HD), F32),
            pltpu.VMEM((ROWS, HD), F32),
            pltpu.VMEM((GROUPS, 2, 8, PAGE, HD), BF16),
            pltpu.VMEM((GROUPS, 2, 8, PAGE, HD), BF16),
            pltpu.VMEM((CONVS, HEADS * SUF, HD), BF16),
            pltpu.VMEM((ROWS, HD), BF16),
            pltpu.VMEM((ROWS, HD), BF16),
            pltpu.VMEM((GROUPS * CONVS, SUF, HD), BF16),
            pltpu.VMEM((TENSOR, SUF, HD), BF16),
            dma((8,)),
            dma((2, GROUPS)),
            dma((20,)),
            dma((20,)),
            dma((2, GROUPS)),
            dma((2, GROUPS)),
            dma((2, GROUPS, 4)),
            dma((2, GROUPS, 4)),
            dma((4,)),
            dma((4,)),
            dma((GROUPS,)),
            dma((GROUPS,)),
            dma((TENSOR,)),
            dma((TENSOR,)),
        ],
        compiler_params=pltpu.CompilerParams(
            collective_id=0, has_side_effects=True, vmem_limit_bytes=60 * 1024 * 1024
        ),
        name="gather",
    )(
        conv_slots,
        prefix_len,
        suffix_len,
        new_dest,
        page_table,
        hidden_states,
        pool_keys,
        pool_values,
        w_query,
        w_key.T,
        w_value.T,
        norm_gain.astype(F32).reshape(TENSOR, 1, PART),
        b_query.reshape(1, HEADS * HD),
        b_key.reshape(1, HD // 2),
        b_value.reshape(1, HD // 2),
        freq,
    )
    mixed, lse = pl.pallas_call(
        attend_kernel,
        out_shape=[
            shape((4, CONVS, HD, HEADS * SUF), BF16),
            shape((4, CONVS, 8, HEADS * SUF), F32),
        ],
        in_specs=[smem_spec()] + [vmem_spec()] * 5,
        out_specs=[vmem_spec()] * 2,
        compiler_params=pltpu.CompilerParams(vmem_limit_bytes=60 * 1024 * 1024),
        name="attend",
    )(
        lists,
        got_k.reshape(PAGES, 2, PAGE, HD),
        got_v.reshape(PAGES, 2, PAGE, HD),
        queries,
        key_new,
        value_new,
    )
    attn_out = pl.pallas_call(
        reduce_kernel,
        out_shape=shape((ROWS, PART), BF16),
        in_specs=[smem_spec()] * 2 + [vmem_spec()] * 2 + [any_spec()],
        out_specs=vmem_spec(),
        scratch_shapes=[
            pltpu.VMEM((HEADS * HD, WIDTH), BF16),
            pltpu.VMEM((4, CONVS, HD, HEADS * SUF), BF16),
            pltpu.VMEM((4, CONVS, 8, HEADS * SUF), F32),
            pltpu.VMEM((CONVS, SUF, HEADS * HD), BF16),
            pltpu.VMEM((4, 4, ROWS, PART), BF16),
            pltpu.VMEM((CONVS, 6, 4, SUF // 2, PART), BF16),
            pltpu.VMEM((CONVS, 6, SUF // 2, PART), BF16),
            dma((1,)),
            dma((4, CONVS)),
            dma((4, CONVS)),
            dma((4,)),
            dma((4,)),
            dma((12 * CONVS,)),
            dma((12 * CONVS,)),
        ],
        compiler_params=pltpu.CompilerParams(
            collective_id=1, has_side_effects=True, vmem_limit_bytes=60 * 1024 * 1024
        ),
        name="reduce",
    )(conv_slots, suffix_len, mixed, lse, w_out)
    pages = new_pages.reshape(TENSOR // 2, 2, SUF, HD)
    return (attn_out, pages[None, :, 0], pages[None, :, 1])


def solution(mesh):
    in_specs = (
        P("group", "tensor"),
        P(),
        P(None, "tensor"),
        P("tensor"),
        P(None, "tensor"),
        P("tensor"),
        P(None, "tensor"),
        P("tensor"),
        P("tensor", None),
        P(("group", "tensor"), None, None, None),
        P(("group", "tensor"), None, None, None),
        P(),
        P(),
        P(),
        P(),
        P(),
    )
    out_specs = (
        P("group", "tensor"),
        P(("group", "tensor"), None, None, None),
        P(("group", "tensor"), None, None, None),
    )
    return jax.shard_map(shards, mesh=mesh, in_specs=in_specs, out_specs=out_specs, check_vma=False)
```

time: 196 us -> 144 us (0.73)
  the two profiles are of different devices: /device:TPU:0 before, /device:TPU:8 now
where the time goes in v2:
time: 144 us
  Pallas kernels  138 us (96%)
  local copies, waits for them, and re-layouts  3.65 us (3%)
    pallas_call x1, Pallas kernels, shards(): pl.pallas_call(gather_kernel, out_shape=[shape((4, GROUPS, 2, 2, PAGE, HD...  75.8 us
    pallas_call x1, Pallas kernels, shards(): pl.pallas_call(reduce_kernel, out_shape=shape((ROWS, PART), BF16), in_spe...  51.6 us
    pallas_call x1, Pallas kernels, shards(): pl.pallas_call(attend_kernel, out_shape=[shape((4, CONVS, HD, HEADS * SUF...  11.1 us

profile of v2, /device:TPU:8, one launch (start us, length us, event | category | flops | bytes accessed | tf_op | source)
XLA Modules:
  0.0 144.1 jit_solution(11010296312332137532)
XLA Ops:
  0.6 1.3 reshape.31.b_query
  1.9 1.3 reshape.37
  3.2 75.8 %gather.1 = (bf16[4,8,2,2,64,128]{5,4,3,2,1,0:T(8,128)(2,1)}, bf16[4,8,2,2,64,128]{5,4,3,2,1,0:T(8,128)(2,1)}, bf16[4,4,256,128]{3,2,1,0:T(8,128)(2,1)}, bf16[25...) custom-call(s32[32]{0:T(128)} %conv_ref.3, s32[32]{0:T(128)} %prefix_ref.1, ...), custom_call_target="tpu_custom_call" | custom-call | tf_op jit(solution)/shard_map/gather/pallas_call | solution.py:819
  79.1 11.1 %attend.1 = (bf16[4,4,128,256]{3,2,1,0:T(8,128)(2,1)}, f32[4,4,8,256]{3,2,1,0:T(8,128)}) custom-call(s32[72,128]{1,0:T(8,128)} %get-tuple-element.12.lists, bf16[64,2,64,128]{3,2,1,0:T(8,128)(2,1)} %bitcast.16, bf16[64,2,64,128]{3,2,1,0:T(8,128)(2,1)} %bitcast.17, bf16[4,4,256,128]{3,2,1,0:T(8,128)(2,1)} %get-tuple-element.15.queries, ...), custom_call_target="tpu_custom_call" | custom-call | tf_op jit(solution)/shard_map/attend/pallas_call | solution.py:886
  90.1 0.0 copy-start
  90.1 51.6 %reduce.1 = bf16[256,512]{1,0:T(8,128)(2,1)} custom-call(s32[32]{0:T(128)} %conv_ref.3, s32[32]{0:T(128)} %suffix_ref.3, bf16[4,4,128,256]{3,2,1,0:T(8,128)(2,1)} %get-tuple-element.18.mixed_ref, f32[4,4,8,256]{3,2,1,0:T(8,128)} %get-tuple-element.19.lse_ref, bf16[512,8192]{1,0:T(8,128)(2,1)} %w_out.1), custom_call_target="tpu_custom_call" | custom-call | tf_op jit(solution)/shard_map/reduce/pallas_call | solution.py:904
  141.7 0.0 copy-done
  141.7 0.7 slice_bitcast_fusion
  142.4 1.7 %copy.25 = bf16[256,512]{1,0:T(8,128)(2,1)} copy(bf16[256,512]{1,0:T(8,128)(2,1)} %reduce.1) | data formatting | bytes 524288
Async XLA Ops:
  90.1 51.6 %copy-start = (bf16[16,64,128]{2,1,0:T(8,128)(2,1)S(1)}, bf16[16,64,128]{2,1,0:T(8,128)(2,1)}, u32[]{:S(2)}) copy-start(bf16[16,64,128]{2,1,0:T(8,128)(2,1)} %get-tuple-element.20) | copy-start | bytes 786436

commit v3 on v2

--- a/solution.py
+++ b/solution.py
@@ -97,6 +97,8 @@
     kv_other,
     new_all,
     new_send,
+    chosen,
+    gain,
     load_sem,
     keep_sem,
     feat_send,
@@ -105,6 +107,8 @@
     y_recv,
     x_send,
     x_recv,
+    v_send,
+    v_recv,
     pair_send,
     pair_recv,
     group_send,
@@ -151,8 +155,7 @@
     to_z_up, to_z_down = x * 4 + z_up, x * 4 + z_down
     half_rows = ROWS // 2
     low_rows, high_rows = pl.ds(0, half_rows), pl.ds(half_rows, half_rows)
-    sent = []
-    kept = []
+    sent, kept = [], []
 
     def pass_on(index, ref, to):
         copy = remote(ref, ref, feat_send.at[index], feat_recv.at[index], group, to)
@@ -174,86 +177,103 @@
         second = pass_on(7 + 4 * block, feat.at[x_at[shift], z_up, high_rows], to_z_down)
         return first, second
 
-    pools, stages, gots = (pool_k, pool_v), (stage_k, stage_v), (got_k, got_v)
-
-    def y_copy(kind, shift):
-        to_group = group_at(shift)
-        return remote(
-            pools[kind].at[pl.ds(2 * to_group, 2)],
-            stages[kind].at[shift],
-            y_send.at[kind, shift],
-            y_recv.at[kind, shift],
-            to_group,
+    pages_out = []
+
+    def push(source, target, send_sem, recv_sem, to_group, to):
+        copy = remote(source, target, send_sem, recv_sem, to_group, to)
+        copy.start()
+        pages_out.append(copy)
+        return copy
+
+    def keep(source, target, sem):
+        copy = pltpu.make_async_copy(source, target, sem)
+        copy.start()
+        kept.append(copy)
+
+    def slots(shift):
+        return pl.ds(2 * group_at(shift), 2)
+
+    def heads(step):
+        return pl.ds(2 * x_at[step], 2)
+
+    def keys_first(shift):
+        return push(
+            pool_k.at[slots(shift)],
+            stage_k.at[shift],
+            y_send.at[0, shift],
+            y_recv.at[0, shift],
+            group_at(shift),
             tensor,
         )
 
-    def x_copies(kind, shift):
+    def keys_second(shift):
         for step in (1, 3, 2, 0):
-            heads = pl.ds(2 * x_at[step], 2)
             if shift == 0:
-                source = pools[kind].at[pl.ds(2 * group, 2), heads]
+                source = pool_k.at[slots(0), heads(step)]
             else:
-                source = stages[kind].at[shift, :, heads]
-            target = gots[kind].at[step, shift]
+                source = stage_k.at[shift, :, heads(step)]
+            target = got_k.at[step, shift]
             if step == 0:
-                copy = pltpu.make_async_copy(source, target, keep_sem.at[kind, shift])
-                copy.start()
-                kept.append(copy)
+                keep(source, target, keep_sem.at[0, shift])
             else:
-                copy = remote(
-                    source,
-                    target,
-                    x_send.at[kind, shift, step],
-                    x_recv.at[kind, shift, step],
-                    group,
-                    x_at[step] * 4 + z,
+                keys_last.append(
+                    push(
+                        source,
+                        target,
+                        x_send.at[0, shift, step],
+                        x_recv.at[0, shift, step],
+                        group,
+                        x_at[step] * 4 + z,
+                    )
                 )
-                copy.start()
-                pages_out.append(copy)
-
-    pages_out = []
-    y_out = []
-    y_items = [
-        (kind, shifts) for shifts in ((2, 6), (3, 7), (4,), (5,)) for kind in range(2)
-    ]
-    y_running = {}
-
-    def y_start(item):
-        if item < len(y_items):
-            kind, shifts = y_items[item]
-            y_running[item] = [y_copy(kind, shift) for shift in shifts]
-            for copy in y_running[item]:
-                copy.start()
-                y_out.append(copy)
-
-    def y_step(item):
-        kind, shifts = y_items[item]
-        for copy in y_running[item]:
-            copy.wait_recv()
-        y_start(item + 2)
-        for shift in shifts:
-            x_copies(kind, shift)
-
+
+    def values_first(step):
+        return push(
+            pool_v.at[:, heads(step)],
+            stage_v.at[step],
+            v_send.at[step],
+            v_recv.at[step],
+            group,
+            x_at[step] * 4 + z,
+        )
+
+    def values_second(step):
+        for shift in (1, 2, 6, 3, 7, 4, 5, 0):
+            if step == 0:
+                source = pool_v.at[slots(shift), heads(0)]
+            else:
+                source = stage_v.at[step, slots(shift)]
+            target = got_v.at[step, shift]
+            if shift == 0:
+                keep(source, target, keep_sem.at[1, step])
+            else:
+                keys_last.append(
+                    push(
+                        source,
+                        target,
+                        x_send.at[1, shift, step],
+                        x_recv.at[1, shift, step],
+                        group_at(shift),
+                        tensor,
+                    )
+                )
+
+    keys_last = []
     f0 = pass_on(0, feat.at[x, z], to_x_up)
     f1 = pass_on(1, feat.at[x, z], to_x_down)
-    across = [y_copy(0, 1), y_copy(1, 1)]
-    for copy in across:
-        copy.start()
-        y_out.append(copy)
-    y_start(0)
-    y_start(1)
     s0 = spread(0, 0)
-    x_copies(0, 0)
-    x_copies(1, 0)
+    key_first = {shift: keys_first(shift) for shift in (1, 2, 6, 3, 7, 4, 5)}
+    value_first = {step: values_first(step) for step in (1, 3, 2)}
+    keys_second(0)
+    values_second(0)
     f0.wait_recv()
     f2 = pass_on(2, feat.at[x_at[3], z, low_rows], to_x_up)
     s1 = spread(1, 3)
     f1.wait_recv()
     f3 = pass_on(3, feat.at[x_at[1], z, high_rows], to_x_down)
     s2 = spread(2, 1)
-    for kind in range(2):
-        across[kind].wait_recv()
-        x_copies(kind, 1)
+    key_first[1].wait_recv()
+    keys_second(1)
 
     prefix = [prefix_ref[conv_ref[group * CONVS + i]] for i in range(CONVS)]
     suffix = [suffix_ref[conv_ref[group * CONVS + i]] for i in range(CONVS)]
@@ -265,7 +285,6 @@
     sine = jnp.sin(angle)
     sine = jnp.where(lane_iota((ROWS, HD)) < HD // 2, -sine, sine)
 
-    y_step(0)
     r0 = spread_on(0, 0, s0)
 
     page_ids = lane_iota((1, PAGES))
@@ -301,11 +320,25 @@
     lists[pl.ds(0, PAGES), :] = table.astype(I32)
     lists[pl.ds(PAGES, 8), :] = counts.astype(I32)
 
+    def find(to, carry):
+        target = group * TENSOR + to
+        index = jnp.int32(0)
+        found = jnp.int32(0)
+        for slot in range(GROUPS * CONVS):
+            hit = dest_ref[conv_ref[slot]] == target
+            index = jnp.where(hit, slot, index)
+            found = jnp.where(hit, 1, found)
+        chosen[0, to] = index
+        chosen[1, to] = found
+        return carry
+
     f2.wait_recv()
     f3.wait_recv()
     s3 = spread(3, 2)
     for load in loads:
         load.wait()
+    gain[...] = gain_ref[...].astype(F32).reshape(1, WIDTH)
+    query_bias = b_query[...].astype(F32).reshape(1, HEADS * HD)
     acc_q[...] = jnp.zeros_like(acc_q)
     acc_kv[...] = jnp.zeros_like(acc_kv)
     squares[...] = jnp.zeros_like(squares)
@@ -315,7 +348,7 @@
             block = bx * 4 + bz
             rows = pl.ds(pl.multiple_of(block * PART, PART), PART)
             wide = feat[bx, bz].astype(F32)
-            scaled = (wide * gain_ref[block]).astype(BF16)
+            scaled = (wide * gain[:, rows]).astype(BF16)
             acc_q[...] += jnp.dot(scaled, wq[rows, :], preferred_element_type=F32)
             acc_kv[...] += lax.dot_general(
                 scaled,
@@ -333,22 +366,27 @@
         lax.fori_loop(0, 4, one, 0)
 
     project(z)
-    y_step(1)
+    lax.fori_loop(0, TENSOR, find, 0)
     r1 = spread_on(1, 3, s1)
     r2 = spread_on(2, 1, s2)
-    y_step(2)
     r3 = spread_on(3, 2, s3)
+    for shift in (2, 6, 3, 7, 4, 5):
+        key_first[shift].wait_recv()
+        keys_second(shift)
+    for step in (1, 3, 2):
+        value_first[step].wait_recv()
+        values_second(step)
     project(z_up)
-    y_step(3)
     project(z_down)
-    y_step(4)
     for copies in (r0, r1, r2, r3):
         for copy in copies:
             copy.wait_recv()
     project(z_far)
     mean = jnp.sum(squares[...], axis=1, keepdims=True) * (1.0 / WIDTH)
     factor = lax.rsqrt(mean + EPSILON)
-    bias = jnp.concatenate([b_key[...], b_value[...]], axis=1).astype(F32)
+    bias = jnp.concatenate(
+        [ref[...].astype(F32).reshape(1, HD // 2) for ref in (b_key, b_value)], axis=1
+    )
     kv_own[...] = (acc_kv[...] * factor + bias).astype(BF16)
     kv_copy = remote(
         kv_own,
@@ -365,7 +403,7 @@
 
     for head in range(HEADS):
         columns = slice(head * HD, (head + 1) * HD)
-        values = acc_q[:, columns] * factor + b_query[:, columns].astype(F32)
+        values = acc_q[:, columns] * factor + query_bias[:, columns]
         values = rotate(values).astype(BF16)
         for i in range(CONVS):
             query_own[i, head * SUF : (head + 1) * SUF, :] = values[i * SUF : (i + 1) * SUF, :]
@@ -384,7 +422,6 @@
         copy.start()
     query_keep = pltpu.make_async_copy(query_own, queries.at[0], load_sem.at[4])
     query_keep.start()
-    y_step(5)
 
     kv_copy.wait_recv()
     mine = kv_own[...].astype(F32)
@@ -416,19 +453,12 @@
     ]
     for copy in group_out:
         copy.start()
-    y_step(6)
     for copy in group_out:
         copy.wait_recv()
 
     def choose(to, carry):
-        target = group * TENSOR + to
-        index = jnp.int32(0)
-        found = jnp.float32(0)
-        for slot in range(GROUPS * CONVS):
-            hit = dest_ref[conv_ref[slot]] == target
-            index = jnp.where(hit, slot, index)
-            found = jnp.where(hit, 1.0, found)
-        new_send[to] = (new_all[index].astype(F32) * found).astype(BF16)
+        page = new_all[chosen[0, to]].astype(F32)
+        new_send[to] = (page * chosen[1, to].astype(F32)).astype(BF16)
         return carry
 
     lax.fori_loop(0, TENSOR, choose, 0)
@@ -453,14 +483,13 @@
         return carry
 
     lax.fori_loop(1, TENSOR, page_start, 0)
-    y_step(7)
 
     mine_copy.wait()
     query_keep.wait()
     kv_copy.wait_send()
     for copy in query_out:
         copy.wait()
-    for copy in sent + y_out + group_out:
+    for copy in sent + pages_out + group_out:
         copy.wait_send()
 
     def page_end(off, carry):
@@ -468,8 +497,10 @@
         return carry
 
     lax.fori_loop(1, TENSOR, page_end, 0)
-    for copy in kept + pages_out:
+    for copy in kept:
         copy.wait()
+    for copy in keys_last:
+        copy.wait_recv()
 
 
 def attend_kernel(lists, got_k, got_v, queries, key_new, value_new, mixed_ref, lse_ref):
@@ -560,7 +591,7 @@
             peak, total, accum = state[slot]
             some = total > 0.0
             safe = jnp.where(some, total, 1.0)
-            mixed = (accum / safe).astype(BF16)
+            mixed = (accum * (1.0 / safe)).astype(BF16)
             lse = jnp.where(some, peak + jnp.log(safe) * (1.0 / LN2), NEGATIVE)
             lse = jnp.broadcast_to(lse, (8, 2 * half))
             for side in range(2):
@@ -570,9 +601,6 @@
         return carry
 
     lax.fori_loop(0, CONVS, one, 0)
-
-
-X_FIRST = (True, True, False, True)
 
 
 def reduce_kernel(
@@ -659,22 +687,22 @@
             joined = joined + mixed_got[r, i].astype(F32) * (shares[r] * scale)
         turned = jnp.transpose(joined).astype(BF16)
         for head in range(HEADS):
-            mixed[i, :, head * HD : (head + 1) * HD] = turned[
+            mixed[i * SUF : (i + 1) * SUF, head * HD : (head + 1) * HD] = turned[
                 head * SUF : (head + 1) * SUF, :
             ]
 
     class Ring:
-        def __init__(self, conv, first, pick, buffers, way):
-            self.conv, self.first, self.pick, self.buffers = conv, first, pick, buffers
+        def __init__(self, side, first, pick, buffers, way):
+            self.side, self.first, self.pick, self.buffers = side, first, pick, buffers
             self.up, self.down, self.me, self.far, self.to_up, self.to_down = way
-            self.top = pl.ds(conv * SUF, SUF // 2)
-            self.bottom = pl.ds(conv * SUF + SUF // 2, SUF // 2)
+            self.top = pl.ds(side * 2 * SUF, SUF)
+            self.bottom = pl.ds(side * 2 * SUF + SUF, SUF)
 
         def send(self, index, ref, to):
             sem = self.first + index
             copy = remote(
                 ref,
-                self.buffers.at[self.conv, index],
+                self.buffers.at[self.side, index],
                 ring_send.at[sem],
                 ring_recv.at[sem],
                 group,
@@ -698,7 +726,7 @@
         def add(self, ref, *indices):
             total = ref[...].astype(F32)
             for index in indices:
-                total = total + self.buffers[self.conv, index].astype(F32)
+                total = total + self.buffers[self.side, index].astype(F32)
             ref[...] = total.astype(BF16)
 
         def relay(self):
@@ -721,62 +749,49 @@
 
     along_x = (x_up, x_down, x, x_far, to_x_up, to_x_down)
     along_z = (z_up, z_down, z, z_far, to_z_up, to_z_down)
-    firsts, seconds = [], []
-    for i in range(CONVS):
-        if X_FIRST[i]:
-            firsts.append(Ring(i, 12 * i, lambda j, rows: part.at[j, :, rows], big, along_x))
-            seconds.append(
-                Ring(i, 12 * i + 6, lambda j, rows: part.at[x, j, rows], small, along_z)
-            )
-        else:
-            firsts.append(Ring(i, 12 * i, lambda j, rows: part.at[:, j, rows], big, along_z))
-            seconds.append(
-                Ring(i, 12 * i + 6, lambda j, rows: part.at[j, z, rows], small, along_x)
-            )
-
-    def begin(i):
-        combine(i)
-        if i == 0:
+    firsts = (
+        Ring(0, 0, lambda j, rows: part.at[j, :, rows], big, along_x),
+        Ring(1, 6, lambda j, rows: part.at[:, j, rows], big, along_z),
+    )
+    seconds = (
+        Ring(0, 12, lambda j, rows: part.at[x, j, rows], small, along_z),
+        Ring(1, 18, lambda j, rows: part.at[j, z, rows], small, along_x),
+    )
+
+    def begin(side):
+        combine(2 * side)
+        combine(2 * side + 1)
+        if side == 0:
             load.wait()
-        rows = slice(i * SUF, (i + 1) * SUF)
+        rows = slice(side * 2 * SUF, (side + 1) * 2 * SUF)
 
         def ready(j):
             def one(k, carry):
-                bx, bz = (j, k) if X_FIRST[i] else (k, j)
+                bx, bz = (j, k) if side == 0 else (k, j)
                 columns = pl.ds(pl.multiple_of((bx * 4 + bz) * PART, PART), PART)
                 part[bx, bz, rows] = jnp.dot(
-                    mixed[i], weights[:, columns], preferred_element_type=F32
+                    mixed[rows], weights[:, columns], preferred_element_type=F32
                 ).astype(BF16)
                 return carry
 
             lax.fori_loop(0, 4, one, 0)
 
-        firsts[i].start(ready)
-
-    def turn(i):
-        firsts[i].finish()
-        seconds[i].start(lambda j: None)
+        firsts[side].start(ready)
+
+    def turn(side):
+        firsts[side].finish()
+        seconds[side].start(lambda j: None)
 
     begin(0)
     begin(1)
     firsts[0].relay()
-    begin(2)
     firsts[1].relay()
     turn(0)
-    begin(3)
-    firsts[2].relay()
     turn(1)
     seconds[0].relay()
-    firsts[3].relay()
-    turn(2)
     seconds[1].relay()
     seconds[0].finish()
-    turn(3)
-    seconds[2].relay()
     seconds[1].finish()
-    seconds[3].relay()
-    seconds[2].finish()
-    seconds[3].finish()
     out_ref[...] = part[x, z]
     for copy in lse_out + mixed_out[0] + mixed_out[1] + mixed_out[2] + mixed_out[3] + pending:
         copy.wait_send()
@@ -840,12 +855,14 @@
             pltpu.VMEM((ROWS, HD), F32),
             pltpu.VMEM((ROWS, HD), F32),
             pltpu.VMEM((GROUPS, 2, 8, PAGE, HD), BF16),
-            pltpu.VMEM((GROUPS, 2, 8, PAGE, HD), BF16),
+            pltpu.VMEM((4, 2 * GROUPS, 2, PAGE, HD), BF16),
             pltpu.VMEM((CONVS, HEADS * SUF, HD), BF16),
             pltpu.VMEM((ROWS, HD), BF16),
             pltpu.VMEM((ROWS, HD), BF16),
             pltpu.VMEM((GROUPS * CONVS, SUF, HD), BF16),
             pltpu.VMEM((TENSOR, SUF, HD), BF16),
+            pltpu.SMEM((2, TENSOR), I32),
+            pltpu.VMEM((1, WIDTH), F32),
             dma((8,)),
             dma((2, GROUPS)),
             dma((20,)),
@@ -854,6 +871,8 @@
             dma((2, GROUPS)),
             dma((2, GROUPS, 4)),
             dma((2, GROUPS, 4)),
+            dma((4,)),
+            dma((4,)),
             dma((4,)),
             dma((4,)),
             dma((GROUPS,)),
@@ -877,10 +896,10 @@
         w_query,
         w_key.T,
         w_value.T,
-        norm_gain.astype(F32).reshape(TENSOR, 1, PART),
-        b_query.reshape(1, HEADS * HD),
-        b_key.reshape(1, HD // 2),
-        b_value.reshape(1, HD // 2),
+        norm_gain,
+        b_query,
+        b_key,
+        b_value,
         freq,
     )
     mixed, lse = pl.pallas_call(
@@ -910,17 +929,17 @@
             pltpu.VMEM((HEADS * HD, WIDTH), BF16),
             pltpu.VMEM((4, CONVS, HD, HEADS * SUF), BF16),
             pltpu.VMEM((4, CONVS, 8, HEADS * SUF), F32),
-            pltpu.VMEM((CONVS, SUF, HEADS * HD), BF16),
+            pltpu.VMEM((ROWS, HEADS * HD), BF16),
             pltpu.VMEM((4, 4, ROWS, PART), BF16),
-            pltpu.VMEM((CONVS, 6, 4, SUF // 2, PART), BF16),
-            pltpu.VMEM((CONVS, 6, SUF // 2, PART), BF16),
+            pltpu.VMEM((2, 6, 4, SUF, PART), BF16),
+            pltpu.VMEM((2, 6, SUF, PART), BF16),
             dma((1,)),
             dma((4, CONVS)),
             dma((4, CONVS)),
             dma((4,)),
             dma((4,)),
-            dma((12 * CONVS,)),
-            dma((12 * CONVS,)),
+            dma((24,)),
+            dma((24,)),
         ],
         compiler_params=pltpu.CompilerParams(
             collective_id=1, has_side_effects=True, vmem_limit_bytes=60 * 1024 * 1024

time: 144 us -> 148 us (1.028)
  the two profiles are of different devices: /device:TPU:8 before, /device:TPU:0 now
where the time goes in v3:
time: 148 us
  Pallas kernels  145 us (98%)
  local copies, waits for them, and re-layouts  2.39 us (2%)
    pallas_call x1, Pallas kernels, shards(): pl.pallas_call(gather_kernel, out_shape=[shape((4, GROUPS, 2, 2, PAGE, HD...  83.2 us
    pallas_call x1, Pallas kernels, shards(): pl.pallas_call(reduce_kernel, out_shape=shape((ROWS, PART), BF16), in_spe...  50.7 us
    pallas_call x1, Pallas kernels, shards(): pl.pallas_call(attend_kernel, out_shape=[shape((4, CONVS, HD, HEADS * SUF...  11.1 us

profile of v3, /device:TPU:0, one launch (start us, length us, event | category | flops | bytes accessed | tf_op | source)
XLA Modules:
  0.0 148.1 jit_solution(3428151731429277188)
XLA Ops:
  0.6 83.2 %gather.1 = (bf16[4,8,2,2,64,128]{5,4,3,2,1,0:T(8,128)(2,1)}, bf16[4,8,2,2,64,128]{5,4,3,2,1,0:T(8,128)(2,1)}, bf16[4,4,256,128]{3,2,1,0:T(8,128)(2,1)}, bf16[25...) custom-call(s32[32]{0:T(128)} %conv_ref.3, s32[32]{0:T(128)} %prefix_ref.1, ...), custom_call_target="tpu_custom_call" | custom-call | tf_op jit(solution)/shard_map/gather/pallas_call | solution.py:834
  83.9 11.1 %attend.1 = (bf16[4,4,128,256]{3,2,1,0:T(8,128)(2,1)}, f32[4,4,8,256]{3,2,1,0:T(8,128)}) custom-call(s32[72,128]{1,0:T(8,128)} %get-tuple-element.12.lists, bf16[64,2,64,128]{3,2,1,0:T(8,128)(2,1)} %bitcast.13, bf16[64,2,64,128]{3,2,1,0:T(8,128)(2,1)} %bitcast.14, bf16[4,4,256,128]{3,2,1,0:T(8,128)(2,1)} %get-tuple-element.15.queries, ...), custom_call_target="tpu_custom_call" | custom-call | tf_op jit(solution)/shard_map/attend/pallas_call | solution.py:905
  94.9 0.0 copy-start
  94.9 50.7 %reduce.1 = bf16[256,512]{1,0:T(8,128)(2,1)} custom-call(s32[32]{0:T(128)} %conv_ref.3, s32[32]{0:T(128)} %suffix_ref.3, bf16[4,4,128,256]{3,2,1,0:T(8,128)(2,1)} %get-tuple-element.18.mixed_ref, f32[4,4,8,256]{3,2,1,0:T(8,128)} %get-tuple-element.19.lse_ref, bf16[512,8192]{1,0:T(8,128)(2,1)} %w_out.1), custom_call_target="tpu_custom_call" | custom-call | tf_op jit(solution)/shard_map/reduce/pallas_call | solution.py:923
  145.7 0.0 copy-done
  145.7 0.7 slice_bitcast_fusion
  146.4 1.7 %copy.25 = bf16[256,512]{1,0:T(8,128)(2,1)} copy(bf16[256,512]{1,0:T(8,128)(2,1)} %reduce.1) | data formatting | bytes 524288
Async XLA Ops:
  94.9 50.8 %copy-start = (bf16[16,64,128]{2,1,0:T(8,128)(2,1)S(1)}, bf16[16,64,128]{2,1,0:T(8,128)(2,1)}, u32[]{:S(2)}) copy-start(bf16[16,64,128]{2,1,0:T(8,128)(2,1)} %get-tuple-element.20) | copy-start | bytes 786436

commit v4 on v3

--- a/solution.py
+++ b/solution.py
@@ -21,6 +21,9 @@
 EPSILON = 1e-06
 NEGATIVE = -1e30
 SCALE = HD**-0.5 * 1.4426950408889634
+STEP = 4
+BLOCKS = (PAGES + CONVS * (STEP - 1)) // STEP
+LIST = 80
 LN2 = 0.6931471805599453
 MESH = pl.DeviceIdType.MESH
 BF16 = jnp.bfloat16
@@ -263,18 +266,12 @@
     f1 = pass_on(1, feat.at[x, z], to_x_down)
     s0 = spread(0, 0)
     key_first = {shift: keys_first(shift) for shift in (1, 2, 6, 3, 7, 4, 5)}
-    value_first = {step: values_first(step) for step in (1, 3, 2)}
-    keys_second(0)
-    values_second(0)
     f0.wait_recv()
     f2 = pass_on(2, feat.at[x_at[3], z, low_rows], to_x_up)
     s1 = spread(1, 3)
     f1.wait_recv()
     f3 = pass_on(3, feat.at[x_at[1], z, high_rows], to_x_down)
     s2 = spread(2, 1)
-    key_first[1].wait_recv()
-    keys_second(1)
-
     prefix = [prefix_ref[conv_ref[group * CONVS + i]] for i in range(CONVS)]
     suffix = [suffix_ref[conv_ref[group * CONVS + i]] for i in range(CONVS)]
 
@@ -285,13 +282,27 @@
     sine = jnp.sin(angle)
     sine = jnp.where(lane_iota((ROWS, HD)) < HD // 2, -sine, sine)
 
+    f2.wait_recv()
+    f3.wait_recv()
+    s3 = spread(3, 2)
+    value_first = {step: values_first(step) for step in (1, 3, 2)}
+    keys_second(0)
+    values_second(0)
+    key_first[1].wait_recv()
+    keys_second(1)
     r0 = spread_on(0, 0, s0)
 
     page_ids = lane_iota((1, PAGES))
     below = (row_iota((PAGES, PAGES)) < lane_iota((PAGES, PAGES))).astype(F32)
-    lane = lane_iota((PAGES, HD))
-    table = jnp.zeros((PAGES, HD), F32)
-    counts = jnp.zeros((8, HD), F32)
+    lane = lane_iota((LIST, HD))
+    place_id = row_iota((LIST, PAGES)).astype(F32)
+    row_id = row_iota((LIST, 1)).astype(F32)
+    codes = jnp.zeros((LIST, 1), F32)
+    block_conv = jnp.zeros((LIST, 1), F32)
+    block_first = jnp.zeros((LIST, 1), F32)
+    last_block = jnp.zeros((LIST, 1), F32)
+    has_block = jnp.zeros((LIST, 1), F32)
+    begin = jnp.zeros((1, 1), F32)
     for i in range(CONVS):
         entry = table_ref[pl.ds(conv_ref[group * CONVS + i], 1), :]
         source = entry >> 4
@@ -306,19 +317,22 @@
         order = jnp.dot(
             jnp.broadcast_to(here_f, (8, PAGES)), below, preferred_element_type=F32
         )[0:1, :]
-        match = (order == row_iota((PAGES, PAGES)).astype(F32)) & (
-            jnp.broadcast_to(here_f, (PAGES, PAGES)) > 0.5
-        )
-        column = jnp.sum(jnp.where(match, value, 0.0), axis=1, keepdims=True)
-        table = jnp.where(lane == i, column, table)
-        counts = jnp.where(
-            lane_iota((8, HD)) == i, jnp.sum(here_f, axis=1, keepdims=True), counts
-        )
-    counts = jnp.where(
-        lane_iota((8, HD)) == CONVS, lax.div(z, 2).astype(F32), counts
-    )
-    lists[pl.ds(0, PAGES), :] = table.astype(I32)
-    lists[pl.ds(PAGES, 8), :] = counts.astype(I32)
+        count = jnp.sum(here_f, axis=1, keepdims=True)
+        blocks = jnp.floor((count + (STEP - 1)) * (1.0 / STEP))
+        match = (order + begin * STEP == place_id) & (
+            jnp.broadcast_to(here_f, (LIST, PAGES)) > 0.5
+        )
+        codes = codes + jnp.sum(jnp.where(match, value, 0.0), axis=1, keepdims=True)
+        block_first = jnp.where(row_id == begin, 1.0, block_first)
+        begin = begin + blocks
+        if i < CONVS - 1:
+            block_conv = block_conv + jnp.where(row_id >= begin, 1.0, 0.0)
+        last_block = jnp.where(row_id == i, jnp.maximum(begin - 1.0, 0.0), last_block)
+        has_block = jnp.where(row_id == i, jnp.minimum(count, 1.0), has_block)
+    table = jnp.zeros((LIST, HD), F32)
+    for column, data in enumerate((codes, block_conv, block_first, last_block, has_block)):
+        table = jnp.where(lane == column, data, table)
+    lists[...] = table.astype(I32)
 
     def find(to, carry):
         target = group * TENSOR + to
@@ -332,9 +346,6 @@
         chosen[1, to] = found
         return carry
 
-    f2.wait_recv()
-    f3.wait_recv()
-    s3 = spread(3, 2)
     for load in loads:
         load.wait()
     gain[...] = gain_ref[...].astype(F32).reshape(1, WIDTH)
@@ -369,15 +380,15 @@
     lax.fori_loop(0, TENSOR, find, 0)
     r1 = spread_on(1, 3, s1)
     r2 = spread_on(2, 1, s2)
-    r3 = spread_on(3, 2, s3)
     for shift in (2, 6, 3, 7, 4, 5):
         key_first[shift].wait_recv()
         keys_second(shift)
+    r3 = spread_on(3, 2, s3)
+    project(z_up)
+    project(z_down)
     for step in (1, 3, 2):
         value_first[step].wait_recv()
         values_second(step)
-    project(z_up)
-    project(z_down)
     for copies in (r0, r1, r2, r3):
         for copy in copies:
             copy.wait_recv()
@@ -503,114 +514,27 @@
         copy.wait_recv()
 
 
-def attend_kernel(lists, got_k, got_v, queries, key_new, value_new, mixed_ref, lse_ref):
-    half = HEADS * SUF
-    token = row_iota((PAGE, 2 * half))
-    causal = row_iota((SUF, half)) <= (lane_iota((SUF, half)) & (SUF - 1))
-    step = 4
-    own_head = lists[PAGES, CONVS]
-    heads = (own_head, 1 - own_head)
-
-    def one(i, carry):
-        first = queries[0, i]
-        query = [
-            jnp.concatenate([first, queries[1, i]], axis=0),
-            jnp.concatenate([queries[2, i], queries[3, i]], axis=0),
-        ]
-        rows = pl.ds(pl.multiple_of(i * SUF, SUF), SUF)
-        scores = lax.dot_general(
-            key_new[rows, :], first, (((1,), (1,)), ((), ())), preferred_element_type=F32
-        )
-        scores = jnp.where(causal, scores * SCALE, NEGATIVE)
-        peak = jnp.max(scores, axis=0, keepdims=True)
-        weights = jnp.exp2(scores - peak)
-        total = jnp.sum(weights, axis=0, keepdims=True)
-        accum = lax.dot_general(
-            value_new[rows, :],
-            weights.astype(BF16),
-            (((0,), (0,)), ((), ())),
-            preferred_element_type=F32,
-        )
-        peak = jnp.concatenate([peak, jnp.full((1, half), NEGATIVE, F32)], axis=1)
-        total = jnp.concatenate([total, jnp.zeros((1, half), F32)], axis=1)
-        accum = jnp.concatenate([accum, jnp.zeros((HD, half), F32)], axis=1)
-        empty = (
-            jnp.full((1, 2 * half), NEGATIVE, F32),
-            jnp.zeros((1, 2 * half), F32),
-            jnp.zeros((HD, 2 * half), F32),
-        )
-        count = lists[PAGES, i]
-
-        def block(b, state):
-            codes = [lists[b * step + p, i] for p in range(step)]
-            scores = []
-            for slot in range(2):
-                keys = jnp.concatenate([got_k[code >> 7, heads[slot]] for code in codes], axis=0)
-                scores.append(
-                    lax.dot_general(
-                        keys,
-                        query[slot],
-                        (((1,), (1,)), ((), ())),
-                        preferred_element_type=F32,
-                    )
-                )
-            out = []
-            for slot in range(2):
-                peak, total, accum = state[slot]
-                values = jnp.concatenate(
-                    [got_v[code >> 7, heads[slot]] for code in codes], axis=0
-                )
-                score = jnp.concatenate(
-                    [
-                        jnp.where(
-                            token < (codes[p] & 127),
-                            scores[slot][p * PAGE : (p + 1) * PAGE] * SCALE,
-                            NEGATIVE,
-                        )
-                        for p in range(step)
-                    ],
-                    axis=0,
-                )
-                fresh = jnp.maximum(peak, jnp.max(score, axis=0, keepdims=True))
-                shrink = jnp.exp2(peak - fresh)
-                weights = jnp.exp2(score - fresh)
-                total = total * shrink + jnp.sum(weights, axis=0, keepdims=True)
-                accum = accum * shrink + lax.dot_general(
-                    values,
-                    weights.astype(BF16),
-                    (((0,), (0,)), ((), ())),
-                    preferred_element_type=F32,
-                )
-                out.append((fresh, total, accum))
-            return tuple(out)
-
-        state = lax.fori_loop(
-            0, (count + step - 1) >> 2, block, ((peak, total, accum), empty)
-        )
-        for slot in range(2):
-            peak, total, accum = state[slot]
-            some = total > 0.0
-            safe = jnp.where(some, total, 1.0)
-            mixed = (accum * (1.0 / safe)).astype(BF16)
-            lse = jnp.where(some, peak + jnp.log(safe) * (1.0 / LN2), NEGATIVE)
-            lse = jnp.broadcast_to(lse, (8, 2 * half))
-            for side in range(2):
-                columns = slice(side * half, (side + 1) * half)
-                mixed_ref[2 * slot + side, i] = mixed[:, columns]
-                lse_ref[2 * slot + side, i] = lse[:, columns]
-        return carry
-
-    lax.fori_loop(0, CONVS, one, 0)
-
-
-def reduce_kernel(
+def attend_kernel(
+    lists,
     conv_ref,
     suffix_ref,
-    mixed_ref,
-    lse_ref,
+    key_new,
+    value_new,
+    queries_hbm,
+    got_k_hbm,
+    got_v_hbm,
     w_out,
     out_ref,
+    queries,
+    got_k,
+    got_v,
     weights,
+    accums,
+    stats,
+    own_accum,
+    own_stats,
+    mixed_out,
+    lse_out,
     mixed_got,
     lse_got,
     mixed,
@@ -627,8 +551,12 @@
 ):
     group, tensor, y, core, x, z = place()
     partner_z = [z, z + 1 - 2 * lax.rem(z, 2), lax.rem(z + 2, 4), 3 - z]
-    load = pltpu.make_async_copy(w_out, weights, load_sem.at[0])
-    load.start()
+    load_query = pltpu.make_async_copy(queries_hbm, queries, load_sem.at[0])
+    load_k = pltpu.make_async_copy(got_k_hbm, got_k, load_sem.at[1])
+    load_v = pltpu.make_async_copy(got_v_hbm, got_v, load_sem.at[2])
+    load = pltpu.make_async_copy(w_out, weights, load_sem.at[3])
+    for copy in (load_query, load_k, load_v, load):
+        copy.start()
     x_up, x_far, x_down = (lax.rem(x + shift, 4) for shift in (1, 2, 3))
     z_up, z_far, z_down = (lax.rem(z + shift, 4) for shift in (1, 2, 3))
     to_x_up, to_x_down = x_up * 4 + z, x_down * 4 + z
@@ -636,60 +564,144 @@
     barrier = pltpu.get_barrier_semaphore()
     for to in (to_x_up, to_x_down, to_z_up, to_z_down, x * 4 + z_far):
         pl.semaphore_signal(barrier, inc=1, device_id=(group, to), device_id_type=MESH)
+
+    half = HEADS * SUF
+    own_head = lax.div(z, 2)
+
+    def score(keys, query):
+        return lax.dot_general(
+            keys, query, (((1,), (1,)), ((), ())), preferred_element_type=F32
+        )
+
+    def mix(values, shares):
+        return lax.dot_general(
+            values,
+            shares.astype(BF16),
+            (((0,), (0,)), ((), ())),
+            preferred_element_type=F32,
+        )
+
+    causal = row_iota((SUF, half)) <= (lane_iota((SUF, half)) & (SUF - 1))
+    load_query.wait()
+    for i in range(CONVS):
+        rows = slice(i * SUF, (i + 1) * SUF)
+        scores = score(key_new[rows], queries[0, i])
+        scores = jnp.where(causal, scores * SCALE, NEGATIVE)
+        peak = jnp.max(scores, axis=0, keepdims=True)
+        shares = jnp.exp2(scores - peak)
+        own_accum[i] = mix(value_new[rows], shares)
+        own_stats[i, 0:1, :] = peak
+        own_stats[i, 1:2, :] = jnp.sum(shares, axis=0, keepdims=True)
+    load_k.wait()
+    load_v.wait()
+
+    token = row_iota((PAGE, half))
+
+    def attend(head, sides):
+        def block(b, state):
+            codes = [lists[b * STEP + p, 0] for p in range(STEP)]
+            conv = lists[b, 1]
+            first = lists[b, 2] == 1
+            keys = jnp.concatenate([got_k[code >> 7, head] for code in codes], axis=0)
+            values = jnp.concatenate([got_v[code >> 7, head] for code in codes], axis=0)
+            out = []
+            for side, (peak, total, accum) in zip(sides, state):
+                scores = score(keys, queries[side, conv])
+                scores = jnp.concatenate(
+                    [
+                        jnp.where(
+                            token < (codes[p] & 127),
+                            scores[p * PAGE : (p + 1) * PAGE] * SCALE,
+                            NEGATIVE,
+                        )
+                        for p in range(STEP)
+                    ],
+                    axis=0,
+                )
+                peak = jnp.where(first, NEGATIVE, peak)
+                fresh = jnp.maximum(peak, jnp.max(scores, axis=0, keepdims=True))
+                shrink = jnp.exp2(peak - fresh)
+                shares = jnp.exp2(scores - fresh)
+                total = total * shrink + jnp.sum(shares, axis=0, keepdims=True)
+                accum = accum * shrink + mix(values, shares)
+                accums[side, b] = accum
+                stats[side, b, 0:1, :] = fresh
+                stats[side, b, 1:2, :] = total
+                out.append((fresh, total, accum))
+            return tuple(out)
+
+        empty = (
+            jnp.full((1, half), NEGATIVE, F32),
+            jnp.zeros((1, half), F32),
+            jnp.zeros((HD, half), F32),
+        )
+        lax.fori_loop(0, BLOCKS, block, tuple(empty for _ in sides))
+
+    def result(side, i):
+        last = lists[i, 3]
+        some = lists[i, 4] == 1
+        peak = jnp.where(some, stats[side, last, 0:1, :], NEGATIVE)
+        total = jnp.where(some, stats[side, last, 1:2, :], 0.0)
+        accum = accums[side, last] * jnp.where(some, 1.0, 0.0)
+        return peak, total, accum
+
+    def send(side):
+        for i in range(CONVS):
+            peak, total, accum = result(side, i)
+            safe = jnp.where(total > 0.0, total, 1.0)
+            mixed_out[side, i] = (accum * (1.0 / safe)).astype(BF16)
+            lse = jnp.where(total > 0.0, peak + jnp.log(safe) * (1.0 / LN2), NEGATIVE)
+            lse_out[side, i] = jnp.broadcast_to(lse, (8, half))
+        copies = [
+            remote(
+                source.at[side],
+                target.at[side],
+                send_sem.at[side],
+                recv_sem.at[side],
+                group,
+                x * 4 + partner_z[side],
+            )
+            for source, target, send_sem, recv_sem in (
+                (mixed_out, mixed_got, mixed_send, mixed_recv),
+                (lse_out, lse_got, lse_send, lse_recv),
+            )
+        ]
+        for copy in copies:
+            copy.start()
+        return copies
+
+    attend(1 - own_head, (2, 3))
     pl.semaphore_wait(barrier, 5)
-
-    lse_out = [
-        remote(
-            lse_ref.at[r],
-            lse_got.at[r],
-            lse_send.at[r],
-            lse_recv.at[r],
-            group,
-            x * 4 + partner_z[r],
-        )
-        for r in (1, 2, 3)
-    ]
-    mixed_out = [
-        [
-            remote(
-                mixed_ref.at[r, i],
-                mixed_got.at[r, i],
-                mixed_send.at[r, i],
-                mixed_recv.at[r, i],
-                group,
-                x * 4 + partner_z[r],
-            )
-            for r in (1, 2, 3)
-        ]
-        for i in range(CONVS)
-    ]
-    for copy in lse_out + mixed_out[0] + mixed_out[1]:
-        copy.start()
-    row_of = lane_iota((1, HEADS * SUF)) & (SUF - 1)
-    pending = []
+    exchanged = send(2) + send(3)
+    attend(own_head, (1,))
+    exchanged = exchanged + send(1)
+    attend(own_head, (0,))
+    for copy in exchanged:
+        copy.wait_recv()
+    row_of = lane_iota((1, half)) & (SUF - 1)
 
     def combine(i):
-        if i == 0:
-            for copy in lse_out:
-                copy.wait_recv()
-        for copy in mixed_out[i]:
-            copy.wait_recv()
-        if i + 2 < CONVS:
-            for copy in mixed_out[i + 2]:
-                copy.start()
-        logs = [lse_ref[0, i, 0:1, :]] + [lse_got[r, i, 0:1, :] for r in (1, 2, 3)]
-        peak = jnp.maximum(jnp.maximum(logs[0], logs[1]), jnp.maximum(logs[2], logs[3]))
-        shares = [jnp.exp2(log - peak) for log in logs]
-        scale = jnp.where(row_of < suffix_ref[conv_ref[group * CONVS + i]], 1.0, 0.0)
-        scale = scale / (shares[0] + shares[1] + shares[2] + shares[3])
-        joined = mixed_ref[0, i].astype(F32) * (shares[0] * scale)
+        peak, total, accum = result(0, i)
+        own_peak = own_stats[i, 0:1, :]
+        logs = [lse_got[r, i, 0:1, :] for r in (1, 2, 3)]
+        top = jnp.maximum(
+            jnp.maximum(peak, own_peak), jnp.maximum(jnp.maximum(logs[0], logs[1]), logs[2])
+        )
+        shares = [jnp.exp2(log - top) for log in logs]
+        first, second = jnp.exp2(peak - top), jnp.exp2(own_peak - top)
+        total = total * first + own_stats[i, 1:2, :] * second
+        total = total + shares[0] + shares[1] + shares[2]
+        scale = jnp.where(row_of < suffix_ref[conv_ref[group * CONVS + i]], 1.0, 0.0) / total
+        joined = accum * (first * scale) + own_accum[i] * (second * scale)
         for r in (1, 2, 3):
-            joined = joined + mixed_got[r, i].astype(F32) * (shares[r] * scale)
+            joined = joined + mixed_got[r, i].astype(F32) * (shares[r - 1] * scale)
         turned = jnp.transpose(joined).astype(BF16)
         for head in range(HEADS):
             mixed[i * SUF : (i + 1) * SUF, head * HD : (head + 1) * HD] = turned[
                 head * SUF : (head + 1) * SUF, :
             ]
+
+    pending = []
 
     class Ring:
         def __init__(self, side, first, pick, buffers, way):
@@ -793,7 +805,7 @@
     seconds[0].finish()
     seconds[1].finish()
     out_ref[...] = part[x, z]
-    for copy in lse_out + mixed_out[0] + mixed_out[1] + mixed_out[2] + mixed_out[3] + pending:
+    for copy in exchanged + pending:
         copy.wait_send()
 
 
@@ -839,7 +851,7 @@
             shape((4, CONVS, HEADS * SUF, HD), BF16),
             shape((ROWS, HD), BF16),
             shape((ROWS, HD), BF16),
-            shape((PAGES + 8, HD), I32),
+            shape((LIST, HD), I32),
             shape((TENSOR, SUF, HD), BF16),
         ],
         in_specs=[smem_spec()] * 4
@@ -902,40 +914,31 @@
         b_value,
         freq,
     )
-    mixed, lse = pl.pallas_call(
+    attn_out = pl.pallas_call(
         attend_kernel,
-        out_shape=[
-            shape((4, CONVS, HD, HEADS * SUF), BF16),
-            shape((4, CONVS, 8, HEADS * SUF), F32),
-        ],
-        in_specs=[smem_spec()] + [vmem_spec()] * 5,
-        out_specs=[vmem_spec()] * 2,
-        compiler_params=pltpu.CompilerParams(vmem_limit_bytes=60 * 1024 * 1024),
-        name="attend",
-    )(
-        lists,
-        got_k.reshape(PAGES, 2, PAGE, HD),
-        got_v.reshape(PAGES, 2, PAGE, HD),
-        queries,
-        key_new,
-        value_new,
-    )
-    attn_out = pl.pallas_call(
-        reduce_kernel,
         out_shape=shape((ROWS, PART), BF16),
-        in_specs=[smem_spec()] * 2 + [vmem_spec()] * 2 + [any_spec()],
+        in_specs=[smem_spec()] * 3 + [vmem_spec()] * 2 + [any_spec()] * 4,
         out_specs=vmem_spec(),
         scratch_shapes=[
+            pltpu.VMEM((4, CONVS, HEADS * SUF, HD), BF16),
+            pltpu.VMEM((PAGES, 2, PAGE, HD), BF16),
+            pltpu.VMEM((PAGES, 2, PAGE, HD), BF16),
             pltpu.VMEM((HEADS * HD, WIDTH), BF16),
+            pltpu.VMEM((4, BLOCKS, HD, HEADS * SUF), F32),
+            pltpu.VMEM((4, BLOCKS, 8, HEADS * SUF), F32),
+            pltpu.VMEM((CONVS, HD, HEADS * SUF), F32),
+            pltpu.VMEM((CONVS, 8, HEADS * SUF), F32),
+            pltpu.VMEM((4, CONVS, HD, HEADS * SUF), BF16),
+            pltpu.VMEM((4, CONVS, 8, HEADS * SUF), F32),
             pltpu.VMEM((4, CONVS, HD, HEADS * SUF), BF16),
             pltpu.VMEM((4, CONVS, 8, HEADS * SUF), F32),
             pltpu.VMEM((ROWS, HEADS * HD), BF16),
             pltpu.VMEM((4, 4, ROWS, PART), BF16),
             pltpu.VMEM((2, 6, 4, SUF, PART), BF16),
             pltpu.VMEM((2, 6, SUF, PART), BF16),
-            dma((1,)),
-            dma((4, CONVS)),
-            dma((4, CONVS)),
+            dma((4,)),
+            dma((4,)),
+            dma((4,)),
             dma((4,)),
             dma((4,)),
             dma((24,)),
@@ -944,8 +947,18 @@
         compiler_params=pltpu.CompilerParams(
             collective_id=1, has_side_effects=True, vmem_limit_bytes=60 * 1024 * 1024
         ),
-        name="reduce",
-    )(conv_slots, suffix_len, mixed, lse, w_out)
+        name="attend",
+    )(
+        lists,
+        conv_slots,
+        suffix_len,
+        key_new,
+        value_new,
+        queries,
+        got_k.reshape(PAGES, 2, PAGE, HD),
+        got_v.reshape(PAGES, 2, PAGE, HD),
+        w_out,
+    )
     pages = new_pages.reshape(TENSOR // 2, 2, SUF, HD)
     return (attn_out, pages[None, :, 0], pages[None, :, 1])
 

time: 148 us -> 148 us (level)
    pallas_call x1, Pallas kernels: 83.2 us -> 74.5 us  [shards(): pl.pallas_call(gather_kernel, out_shape=[shape((4, GROUPS, 2, 2, PAGE, HD...]
    pallas_call x2 -> x1, Pallas kernels: 61.8 us -> 70.1 us  [shards(): pl.pallas_call(attend_kernel, out_shape=shape((ROWS, PART), BF16), in_spe...]
where the time goes in v4:
time: 148 us
  Pallas kernels  145 us (98%)
  local copies, waits for them, and re-layouts  2.39 us (2%)
    pallas_call x1, Pallas kernels, shards(): pl.pallas_call(gather_kernel, out_shape=[shape((4, GROUPS, 2, 2, PAGE, HD...  74.5 us
    pallas_call x1, Pallas kernels, shards(): pl.pallas_call(attend_kernel, out_shape=shape((ROWS, PART), BF16), in_spe...  70.1 us

profile of v4, /device:TPU:0, one launch (start us, length us, event | category | flops | bytes accessed | tf_op | source)
XLA Modules:
  0.0 147.7 jit_solution(11384020573509899150)
XLA Ops:
  0.6 74.5 %gather.1 = (bf16[4,8,2,2,64,128]{5,4,3,2,1,0:T(8,128)(2,1)}, bf16[4,8,2,2,64,128]{5,4,3,2,1,0:T(8,128)(2,1)}, bf16[4,4,256,128]{3,2,1,0:T(8,128)(2,1)}, bf16[25...) custom-call(s32[32]{0:T(128)} %conv_ref.3, s32[32]{0:T(128)} %prefix_ref.1, ...), custom_call_target="tpu_custom_call" | custom-call | tf_op jit(solution)/shard_map/gather/pallas_call | solution.py:846
  75.2 0.0 copy-start
  75.2 70.1 %attend.1 = bf16[256,512]{1,0:T(8,128)(2,1)} custom-call(s32[80,128]{1,0:T(8,128)} %get-tuple-element.10.lists, s32[32]{0:T(128)} %conv_ref.3, s32[32]{0:T(128)} %suffix_ref.3, bf16[256,128]{1,0:T(8,128)(2,1)} %get-tuple-element.11.key_new, bf16[256,128]{1,0:T(8,128)(2,1)} %get-tuple-element.12.value_new, ...), custom_call_target="tpu_custom_call" | custom-call | tf_op jit(solution)/shard_map/attend/pallas_call | solution.py:917
  145.3 0.0 copy-done
  145.3 0.7 slice_bitcast_fusion
  146.0 1.7 %copy.25 = bf16[256,512]{1,0:T(8,128)(2,1)} copy(bf16[256,512]{1,0:T(8,128)(2,1)} %attend.1) | data formatting | bytes 524288
Async XLA Ops:
  75.2 70.1 %copy-start = (bf16[16,64,128]{2,1,0:T(8,128)(2,1)S(1)}, bf16[16,64,128]{2,1,0:T(8,128)(2,1)}, u32[]{:S(2)}) copy-start(bf16[16,64,128]{2,1,0:T(8,128)(2,1)} %get-tuple-element.16) | copy-start | bytes 786436

commit v5 on v4

--- a/solution.py
+++ b/solution.py
@@ -22,7 +22,8 @@
 NEGATIVE = -1e30
 SCALE = HD**-0.5 * 1.4426950408889634
 STEP = 4
-BLOCKS = (PAGES + CONVS * (STEP - 1)) // STEP
+PACK = 4
+BLOCKS = -(-((PAGES + CONVS * (STEP - 1)) // STEP) // PACK) * PACK
 LIST = 80
 LN2 = 0.6931471805599453
 MESH = pl.DeviceIdType.MESH
@@ -555,7 +556,7 @@
     load_k = pltpu.make_async_copy(got_k_hbm, got_k, load_sem.at[1])
     load_v = pltpu.make_async_copy(got_v_hbm, got_v, load_sem.at[2])
     load = pltpu.make_async_copy(w_out, weights, load_sem.at[3])
-    for copy in (load_query, load_k, load_v, load):
+    for copy in (load_query, load_k, load_v):
         copy.start()
     x_up, x_far, x_down = (lax.rem(x + shift, 4) for shift in (1, 2, 3))
     z_up, z_far, z_down = (lax.rem(z + shift, 4) for shift in (1, 2, 3))
@@ -594,48 +595,72 @@
         own_stats[i, 1:2, :] = jnp.sum(shares, axis=0, keepdims=True)
     load_k.wait()
     load_v.wait()
+    load.start()
 
     token = row_iota((PAGE, half))
 
     def attend(head, sides):
-        def block(b, state):
-            codes = [lists[b * STEP + p, 0] for p in range(STEP)]
-            conv = lists[b, 1]
-            first = lists[b, 2] == 1
-            keys = jnp.concatenate([got_k[code >> 7, head] for code in codes], axis=0)
-            values = jnp.concatenate([got_v[code >> 7, head] for code in codes], axis=0)
-            out = []
-            for side, (peak, total, accum) in zip(sides, state):
-                scores = score(keys, queries[side, conv])
-                scores = jnp.concatenate(
+        def pack(index, state):
+            blocks = [index * PACK + k for k in range(PACK)]
+            codes = [[lists[b * STEP + p, 0] for p in range(STEP)] for b in blocks]
+            convs = [lists[b, 1] for b in blocks]
+            firsts = [lists[b, 2] == 1 for b in blocks]
+            keys = [
+                jnp.concatenate([got_k[code >> 7, head] for code in row], axis=0)
+                for row in codes
+            ]
+            values = [
+                jnp.concatenate([got_v[code >> 7, head] for code in row], axis=0)
+                for row in codes
+            ]
+            pairs = [(k, s) for k in range(PACK) for s in range(len(sides))]
+            scores = {
+                (k, s): score(keys[k], queries[sides[s], convs[k]]) for k, s in pairs
+            }
+            for k, s in pairs:
+                scores[k, s] = jnp.concatenate(
                     [
                         jnp.where(
-                            token < (codes[p] & 127),
-                            scores[p * PAGE : (p + 1) * PAGE] * SCALE,
+                            token < (codes[k][p] & 127),
+                            scores[k, s][p * PAGE : (p + 1) * PAGE] * SCALE,
                             NEGATIVE,
                         )
                         for p in range(STEP)
                     ],
                     axis=0,
                 )
-                peak = jnp.where(first, NEGATIVE, peak)
-                fresh = jnp.maximum(peak, jnp.max(scores, axis=0, keepdims=True))
-                shrink = jnp.exp2(peak - fresh)
-                shares = jnp.exp2(scores - fresh)
-                total = total * shrink + jnp.sum(shares, axis=0, keepdims=True)
-                accum = accum * shrink + mix(values, shares)
-                accums[side, b] = accum
-                stats[side, b, 0:1, :] = fresh
-                stats[side, b, 1:2, :] = total
-                out.append((fresh, total, accum))
-            return tuple(out)
+            tops = {
+                key: jnp.max(value, axis=0, keepdims=True) for key, value in scores.items()
+            }
+            state = list(state)
+            fresh, shrink = {}, {}
+            for s in range(len(sides)):
+                peak = state[s][0]
+                for k in range(PACK):
+                    peak = jnp.where(firsts[k], NEGATIVE, peak)
+                    fresh[k, s] = jnp.maximum(peak, tops[k, s])
+                    shrink[k, s] = jnp.exp2(peak - fresh[k, s])
+                    peak = fresh[k, s]
+            shares = {key: jnp.exp2(scores[key] - fresh[key]) for key in pairs}
+            sums = {key: jnp.sum(shares[key], axis=0, keepdims=True) for key in pairs}
+            mixes = {(k, s): mix(values[k], shares[k, s]) for k, s in pairs}
+            for s, side in enumerate(sides):
+                peak, total, accum = state[s]
+                for k in range(PACK):
+                    total = total * shrink[k, s] + sums[k, s]
+                    accum = accum * shrink[k, s] + mixes[k, s]
+                    accums[side, blocks[k]] = accum
+                    stats[side, blocks[k], 0:1, :] = fresh[k, s]
+                    stats[side, blocks[k], 1:2, :] = total
+                state[s] = (fresh[PACK - 1, s], total, accum)
+            return tuple(state)
 
         empty = (
             jnp.full((1, half), NEGATIVE, F32),
             jnp.zeros((1, half), F32),
             jnp.zeros((HD, half), F32),
         )
-        lax.fori_loop(0, BLOCKS, block, tuple(empty for _ in sides))
+        lax.fori_loop(0, BLOCKS // PACK, pack, tuple(empty for _ in sides))
 
     def result(side, i):
         last = lists[i, 3]
@@ -673,9 +698,8 @@
     attend(1 - own_head, (2, 3))
     pl.semaphore_wait(barrier, 5)
     exchanged = send(2) + send(3)
-    attend(own_head, (1,))
+    attend(own_head, (1, 0))
     exchanged = exchanged + send(1)
-    attend(own_head, (0,))
     for copy in exchanged:
         copy.wait_recv()
     row_of = lane_iota((1, half)) & (SUF - 1)
@@ -724,16 +748,15 @@
             pending.append(copy)
             return copy
 
-        def start(self, ready):
+        def start_far(self):
             pick = self.pick
-            ready(self.far)
             self.c0 = self.send(0, pick(self.far, self.top), self.to_up)
             self.c1 = self.send(1, pick(self.far, self.bottom), self.to_down)
-            ready(self.up)
+
+        def start_near(self):
+            pick = self.pick
             self.c2 = self.send(2, pick(self.up, self.bottom), self.to_up)
-            ready(self.down)
             self.c3 = self.send(3, pick(self.down, self.top), self.to_down)
-            ready(self.me)
 
         def add(self, ref, *indices):
             total = ref[...].astype(F32)
@@ -770,36 +793,34 @@
         Ring(1, 18, lambda j, rows: part.at[j, z, rows], small, along_x),
     )
 
-    def begin(side):
-        combine(2 * side)
-        combine(2 * side + 1)
-        if side == 0:
-            load.wait()
-        rows = slice(side * 2 * SUF, (side + 1) * 2 * SUF)
-
-        def ready(j):
-            def one(k, carry):
-                bx, bz = (j, k) if side == 0 else (k, j)
-                columns = pl.ds(pl.multiple_of((bx * 4 + bz) * PART, PART), PART)
-                part[bx, bz, rows] = jnp.dot(
-                    mixed[rows], weights[:, columns], preferred_element_type=F32
-                ).astype(BF16)
-                return carry
-
-            lax.fori_loop(0, 4, one, 0)
-
-        firsts[side].start(ready)
-
-    def turn(side):
-        firsts[side].finish()
-        seconds[side].start(lambda j: None)
-
-    begin(0)
-    begin(1)
+    def project(bx, bz):
+        columns = pl.ds(pl.multiple_of((bx * 4 + bz) * PART, PART), PART)
+        part[bx, bz] = jnp.dot(
+            mixed[...], weights[:, columns], preferred_element_type=F32
+        ).astype(BF16)
+
+    def project_many(pairs):
+        for bx, bz in pairs:
+            project(bx, bz)
+
+    for i in range(CONVS):
+        combine(i)
+    load.wait()
+    project_many([(x_far, bz) for bz in (z_far, z_up, z_down, z)])
+    firsts[0].start_far()
+    project_many([(bx, z_far) for bx in (x_up, x_down, x)])
+    firsts[1].start_far()
+    project_many([(x_up, z_up), (x_up, z_down), (x_up, z)])
+    project_many([(x_down, z_up), (x_down, z_down), (x_down, z)])
+    firsts[0].start_near()
+    project_many([(x, z_up), (x, z_down), (x, z)])
+    firsts[1].start_near()
     firsts[0].relay()
     firsts[1].relay()
-    turn(0)
-    turn(1)
+    for first, second in zip(firsts, seconds):
+        first.finish()
+        second.start_far()
+        second.start_near()
     seconds[0].relay()
     seconds[1].relay()
     seconds[0].finish()

time: 148 us -> 132 us (0.89)
  Pallas kernels: 145 us -> 128 us
    pallas_call x1, Pallas kernels: 70.1 us -> 53.6 us  [shards(): pl.pallas_call(attend_kernel, out_shape=shape((ROWS, PART), BF16), in_spe...]
where the time goes in v5:
time: 132 us; the launch traced here: 131 us
  Pallas kernels  128 us (97%)
  local copies, waits for them, and re-layouts  2.39 us (2%)
    pallas_call x1, Pallas kernels, shards(): pl.pallas_call(gather_kernel, out_shape=[shape((4, GROUPS, 2, 2, PAGE, HD...  74.5 us
    pallas_call x1, Pallas kernels, shards(): pl.pallas_call(attend_kernel, out_shape=shape((ROWS, PART), BF16), in_spe...  53.6 us

profile of v5, /device:TPU:0, one launch (start us, length us, event | category | flops | bytes accessed | tf_op | source)
XLA Modules:
  0.0 131.2 jit_solution(12405418340962024082)
XLA Ops:
  0.6 74.5 %gather.1 = (bf16[4,8,2,2,64,128]{5,4,3,2,1,0:T(8,128)(2,1)}, bf16[4,8,2,2,64,128]{5,4,3,2,1,0:T(8,128)(2,1)}, bf16[4,4,256,128]{3,2,1,0:T(8,128)(2,1)}, bf16[25...) custom-call(s32[32]{0:T(128)} %conv_ref.3, s32[32]{0:T(128)} %prefix_ref.1, ...), custom_call_target="tpu_custom_call" | custom-call | tf_op jit(solution)/shard_map/gather/pallas_call | solution.py:867
  75.2 0.0 copy-start
  75.2 53.6 %attend.1 = bf16[256,512]{1,0:T(8,128)(2,1)} custom-call(s32[80,128]{1,0:T(8,128)} %get-tuple-element.10.lists, s32[32]{0:T(128)} %conv_ref.3, s32[32]{0:T(128)} %suffix_ref.3, bf16[256,128]{1,0:T(8,128)(2,1)} %get-tuple-element.11.key_new, bf16[256,128]{1,0:T(8,128)(2,1)} %get-tuple-element.12.value_new, ...), custom_call_target="tpu_custom_call" | custom-call | tf_op jit(solution)/shard_map/attend/pallas_call | solution.py:938
  128.8 0.0 copy-done
  128.8 0.7 slice_bitcast_fusion
  129.5 1.7 %copy.25 = bf16[256,512]{1,0:T(8,128)(2,1)} copy(bf16[256,512]{1,0:T(8,128)(2,1)} %attend.1) | data formatting | bytes 524288
Async XLA Ops:
  75.2 53.7 %copy-start = (bf16[16,64,128]{2,1,0:T(8,128)(2,1)S(1)}, bf16[16,64,128]{2,1,0:T(8,128)(2,1)}, u32[]{:S(2)}) copy-start(bf16[16,64,128]{2,1,0:T(8,128)(2,1)} %get-tuple-element.16) | copy-start | bytes 786436

commit v6 on v5

--- a/solution.py
+++ b/solution.py
@@ -22,8 +22,7 @@
 NEGATIVE = -1e30
 SCALE = HD**-0.5 * 1.4426950408889634
 STEP = 4
-PACK = 4
-BLOCKS = -(-((PAGES + CONVS * (STEP - 1)) // STEP) // PACK) * PACK
+BLOCKS = 20
 LIST = 80
 LN2 = 0.6931471805599453
 MESH = pl.DeviceIdType.MESH
@@ -64,7 +63,7 @@
     return lax.broadcasted_iota(I32, shape, len(shape) - 2)
 
 
-def gather_kernel(
+def layer_kernel(
     conv_ref,
     prefix_ref,
     suffix_ref,
@@ -76,17 +75,13 @@
     w_query,
     w_key,
     w_value,
+    w_out,
     gain_ref,
     b_query,
     b_key,
     b_value,
     freq_ref,
-    got_k,
-    got_v,
-    queries,
-    key_new,
-    value_new,
-    lists,
+    out_ref,
     new_pages,
     feat,
     wq,
@@ -96,13 +91,32 @@
     squares,
     stage_k,
     stage_v,
-    query_own,
+    got_k,
+    got_v,
+    queries,
+    key_new,
+    value_new,
     kv_own,
     kv_other,
     new_all,
-    new_send,
+    table_out,
+    lists,
     chosen,
     gain,
+    weights,
+    accums,
+    stats,
+    own_accum,
+    own_stats,
+    mixed_out,
+    lse_out,
+    mixed_got,
+    lse_got,
+    mixed,
+    part,
+    big,
+    small,
+    new_send,
     load_sem,
     keep_sem,
     feat_send,
@@ -117,6 +131,12 @@
     pair_recv,
     group_send,
     group_recv,
+    mixed_send,
+    mixed_recv,
+    lse_send,
+    lse_recv,
+    ring_send,
+    ring_recv,
     page_send,
     page_recv,
 ):
@@ -154,6 +174,7 @@
 
     own.wait()
     x_at = [lax.rem(x + shift, 4) for shift in range(4)]
+    x_up, x_far, x_down = x_at[1:]
     z_up, z_far, z_down = (lax.rem(z + shift, 4) for shift in (1, 2, 3))
     to_x_up, to_x_down = x_at[1] * 4 + z, x_at[3] * 4 + z
     to_z_up, to_z_down = x * 4 + z_up, x * 4 + z_down
@@ -216,7 +237,7 @@
                 source = pool_k.at[slots(0), heads(step)]
             else:
                 source = stage_k.at[shift, :, heads(step)]
-            target = got_k.at[step, shift]
+            target = got_k.at[pl.ds(2 * (step * GROUPS + shift), 2)]
             if step == 0:
                 keep(source, target, keep_sem.at[0, shift])
             else:
@@ -247,7 +268,7 @@
                 source = pool_v.at[slots(shift), heads(0)]
             else:
                 source = stage_v.at[step, slots(shift)]
-            target = got_v.at[step, shift]
+            target = got_v.at[pl.ds(2 * (step * GROUPS + shift), 2)]
             if shift == 0:
                 keep(source, target, keep_sem.at[1, step])
             else:
@@ -333,7 +354,9 @@
     table = jnp.zeros((LIST, HD), F32)
     for column, data in enumerate((codes, block_conv, block_first, last_block, has_block)):
         table = jnp.where(lane == column, data, table)
-    lists[...] = table.astype(I32)
+    table_out[...] = table.astype(I32)
+    list_copy = pltpu.make_async_copy(table_out, lists, load_sem.at[4])
+    list_copy.start()
 
     def find(to, carry):
         target = group * TENSOR + to
@@ -349,6 +372,8 @@
 
     for load in loads:
         load.wait()
+    load_out = pltpu.make_async_copy(w_out, weights, load_sem.at[5])
+    load_out.start()
     gain[...] = gain_ref[...].astype(F32).reshape(1, WIDTH)
     query_bias = b_query[...].astype(F32).reshape(1, HEADS * HD)
     acc_q[...] = jnp.zeros_like(acc_q)
@@ -418,10 +443,10 @@
         values = acc_q[:, columns] * factor + query_bias[:, columns]
         values = rotate(values).astype(BF16)
         for i in range(CONVS):
-            query_own[i, head * SUF : (head + 1) * SUF, :] = values[i * SUF : (i + 1) * SUF, :]
+            queries[0, i, head * SUF : (head + 1) * SUF, :] = values[i * SUF : (i + 1) * SUF, :]
     query_out = [
         remote(
-            query_own,
+            queries.at[0],
             queries.at[r],
             pair_send.at[r],
             pair_recv.at[r],
@@ -432,8 +457,6 @@
     ]
     for copy in query_out:
         copy.start()
-    query_keep = pltpu.make_async_copy(query_own, queries.at[0], load_sem.at[4])
-    query_keep.start()
 
     kv_copy.wait_recv()
     mine = kv_own[...].astype(F32)
@@ -450,8 +473,8 @@
     page = jnp.where(parity == 0, keys.astype(BF16).astype(F32), values)
     live_row = jnp.concatenate([offsets < suffix[i] for i in range(CONVS)], axis=0)
     page = jnp.where(live_row, page, 0.0).astype(BF16)
-    new_all[pl.ds(group * CONVS, CONVS)] = page.reshape(CONVS, SUF, HD)
     new_ref = new_all.at[pl.ds(group * CONVS, CONVS)]
+    new_ref[...] = page.reshape(CONVS, SUF, HD)
     group_out = [
         remote(
             new_ref,
@@ -465,106 +488,6 @@
     ]
     for copy in group_out:
         copy.start()
-    for copy in group_out:
-        copy.wait_recv()
-
-    def choose(to, carry):
-        page = new_all[chosen[0, to]].astype(F32)
-        new_send[to] = (page * chosen[1, to].astype(F32)).astype(BF16)
-        return carry
-
-    lax.fori_loop(0, TENSOR, choose, 0)
-    mine_copy = pltpu.make_async_copy(
-        new_send.at[tensor], new_pages.at[tensor], load_sem.at[5]
-    )
-    mine_copy.start()
-
-    def page_copy(off):
-        to = lax.rem(tensor + off, TENSOR)
-        return remote(
-            new_send.at[to],
-            new_pages.at[tensor],
-            page_send.at[off],
-            page_recv.at[off],
-            group,
-            to,
-        )
-
-    def page_start(off, carry):
-        page_copy(off).start()
-        return carry
-
-    lax.fori_loop(1, TENSOR, page_start, 0)
-
-    mine_copy.wait()
-    query_keep.wait()
-    kv_copy.wait_send()
-    for copy in query_out:
-        copy.wait()
-    for copy in sent + pages_out + group_out:
-        copy.wait_send()
-
-    def page_end(off, carry):
-        page_copy(off).wait()
-        return carry
-
-    lax.fori_loop(1, TENSOR, page_end, 0)
-    for copy in kept:
-        copy.wait()
-    for copy in keys_last:
-        copy.wait_recv()
-
-
-def attend_kernel(
-    lists,
-    conv_ref,
-    suffix_ref,
-    key_new,
-    value_new,
-    queries_hbm,
-    got_k_hbm,
-    got_v_hbm,
-    w_out,
-    out_ref,
-    queries,
-    got_k,
-    got_v,
-    weights,
-    accums,
-    stats,
-    own_accum,
-    own_stats,
-    mixed_out,
-    lse_out,
-    mixed_got,
-    lse_got,
-    mixed,
-    part,
-    big,
-    small,
-    load_sem,
-    mixed_send,
-    mixed_recv,
-    lse_send,
-    lse_recv,
-    ring_send,
-    ring_recv,
-):
-    group, tensor, y, core, x, z = place()
-    partner_z = [z, z + 1 - 2 * lax.rem(z, 2), lax.rem(z + 2, 4), 3 - z]
-    load_query = pltpu.make_async_copy(queries_hbm, queries, load_sem.at[0])
-    load_k = pltpu.make_async_copy(got_k_hbm, got_k, load_sem.at[1])
-    load_v = pltpu.make_async_copy(got_v_hbm, got_v, load_sem.at[2])
-    load = pltpu.make_async_copy(w_out, weights, load_sem.at[3])
-    for copy in (load_query, load_k, load_v):
-        copy.start()
-    x_up, x_far, x_down = (lax.rem(x + shift, 4) for shift in (1, 2, 3))
-    z_up, z_far, z_down = (lax.rem(z + shift, 4) for shift in (1, 2, 3))
-    to_x_up, to_x_down = x_up * 4 + z, x_down * 4 + z
-    to_z_up, to_z_down = x * 4 + z_up, x * 4 + z_down
-    barrier = pltpu.get_barrier_semaphore()
-    for to in (to_x_up, to_x_down, to_z_up, to_z_down, x * 4 + z_far):
-        pl.semaphore_signal(barrier, inc=1, device_id=(group, to), device_id_type=MESH)
 
     half = HEADS * SUF
     own_head = lax.div(z, 2)
@@ -583,7 +506,6 @@
         )
 
     causal = row_iota((SUF, half)) <= (lane_iota((SUF, half)) & (SUF - 1))
-    load_query.wait()
     for i in range(CONVS):
         rows = slice(i * SUF, (i + 1) * SUF)
         scores = score(key_new[rows], queries[0, i])
@@ -593,27 +515,30 @@
         own_accum[i] = mix(value_new[rows], shares)
         own_stats[i, 0:1, :] = peak
         own_stats[i, 1:2, :] = jnp.sum(shares, axis=0, keepdims=True)
-    load_k.wait()
-    load_v.wait()
-    load.start()
+    list_copy.wait()
+    for copy in query_out + keys_last:
+        copy.wait_recv()
+    for copy in kept:
+        copy.wait()
 
     token = row_iota((PAGE, half))
 
-    def attend(head, sides):
+    def attend(head, sides, width):
         def pack(index, state):
-            blocks = [index * PACK + k for k in range(PACK)]
+            blocks = [index * width + k for k in range(width)]
             codes = [[lists[b * STEP + p, 0] for p in range(STEP)] for b in blocks]
-            convs = [lists[b, 1] for b in blocks]
+            convs = [jnp.clip(lists[b, 1], 0, CONVS - 1) for b in blocks]
+            spots = [[jnp.clip(code >> 7, 0, PAGES - 1) for code in row] for row in codes]
             firsts = [lists[b, 2] == 1 for b in blocks]
             keys = [
-                jnp.concatenate([got_k[code >> 7, head] for code in row], axis=0)
-                for row in codes
+                jnp.concatenate([got_k[spot, head] for spot in row], axis=0)
+                for row in spots
             ]
             values = [
-                jnp.concatenate([got_v[code >> 7, head] for code in row], axis=0)
-                for row in codes
+                jnp.concatenate([got_v[spot, head] for spot in row], axis=0)
+                for row in spots
             ]
-            pairs = [(k, s) for k in range(PACK) for s in range(len(sides))]
+            pairs = [(k, s) for k in range(width) for s in range(len(sides))]
             scores = {
                 (k, s): score(keys[k], queries[sides[s], convs[k]]) for k, s in pairs
             }
@@ -636,7 +561,7 @@
             fresh, shrink = {}, {}
             for s in range(len(sides)):
                 peak = state[s][0]
-                for k in range(PACK):
+                for k in range(width):
                     peak = jnp.where(firsts[k], NEGATIVE, peak)
                     fresh[k, s] = jnp.maximum(peak, tops[k, s])
                     shrink[k, s] = jnp.exp2(peak - fresh[k, s])
@@ -646,13 +571,13 @@
             mixes = {(k, s): mix(values[k], shares[k, s]) for k, s in pairs}
             for s, side in enumerate(sides):
                 peak, total, accum = state[s]
-                for k in range(PACK):
+                for k in range(width):
                     total = total * shrink[k, s] + sums[k, s]
                     accum = accum * shrink[k, s] + mixes[k, s]
                     accums[side, blocks[k]] = accum
                     stats[side, blocks[k], 0:1, :] = fresh[k, s]
                     stats[side, blocks[k], 1:2, :] = total
-                state[s] = (fresh[PACK - 1, s], total, accum)
+                state[s] = (fresh[width - 1, s], total, accum)
             return tuple(state)
 
         empty = (
@@ -660,10 +585,10 @@
             jnp.zeros((1, half), F32),
             jnp.zeros((HD, half), F32),
         )
-        lax.fori_loop(0, BLOCKS // PACK, pack, tuple(empty for _ in sides))
+        lax.fori_loop(0, BLOCKS // width, pack, tuple(empty for _ in sides))
 
     def result(side, i):
-        last = lists[i, 3]
+        last = jnp.clip(lists[i, 3], 0, BLOCKS - 1)
         some = lists[i, 4] == 1
         peak = jnp.where(some, stats[side, last, 0:1, :], NEGATIVE)
         total = jnp.where(some, stats[side, last, 1:2, :], 0.0)
@@ -695,11 +620,45 @@
             copy.start()
         return copies
 
-    attend(1 - own_head, (2, 3))
-    pl.semaphore_wait(barrier, 5)
-    exchanged = send(2) + send(3)
-    attend(own_head, (1, 0))
+    attend(1 - own_head, (2,), 10)
+    exchanged = send(2)
+    attend(1 - own_head, (3,), 10)
+    exchanged = exchanged + send(3)
+
+    attend(own_head, (1,), 10)
     exchanged = exchanged + send(1)
+
+    for copy in group_out:
+        copy.wait_recv()
+
+    def choose(to, carry):
+        page = new_all[jnp.clip(chosen[0, to], 0, GROUPS * CONVS - 1)].astype(F32)
+        new_send[to] = (page * chosen[1, to].astype(F32)).astype(BF16)
+        return carry
+
+    lax.fori_loop(0, TENSOR, choose, 0)
+    mine_copy = pltpu.make_async_copy(
+        new_send.at[tensor], new_pages.at[tensor], load_sem.at[6]
+    )
+    mine_copy.start()
+
+    def page_copy(off):
+        to = lax.rem(tensor + off, TENSOR)
+        return remote(
+            new_send.at[to],
+            new_pages.at[tensor],
+            page_send.at[off],
+            page_recv.at[off],
+            group,
+            to,
+        )
+
+    def page_start(off, carry):
+        page_copy(off).start()
+        return carry
+
+    lax.fori_loop(1, TENSOR, page_start, 0)
+    attend(own_head, (0,), 10)
     for copy in exchanged:
         copy.wait_recv()
     row_of = lane_iota((1, half)) & (SUF - 1)
@@ -793,7 +752,7 @@
         Ring(1, 18, lambda j, rows: part.at[j, z, rows], small, along_x),
     )
 
-    def project(bx, bz):
+    def out_block(bx, bz):
         columns = pl.ds(pl.multiple_of((bx * 4 + bz) * PART, PART), PART)
         part[bx, bz] = jnp.dot(
             mixed[...], weights[:, columns], preferred_element_type=F32
@@ -801,11 +760,11 @@
 
     def project_many(pairs):
         for bx, bz in pairs:
-            project(bx, bz)
+            out_block(bx, bz)
 
     for i in range(CONVS):
         combine(i)
-    load.wait()
+    load_out.wait()
     project_many([(x_far, bz) for bz in (z_far, z_up, z_down, z)])
     firsts[0].start_far()
     project_many([(bx, z_far) for bx in (x_up, x_down, x)])
@@ -826,8 +785,15 @@
     seconds[0].finish()
     seconds[1].finish()
     out_ref[...] = part[x, z]
-    for copy in exchanged + pending:
+    for copy in exchanged + pending + sent + pages_out + group_out + query_out + [kv_copy]:
         copy.wait_send()
+    mine_copy.wait()
+
+    def page_end(off, carry):
+        page_copy(off).wait()
+        return carry
+
+    lax.fori_loop(1, TENSOR, page_end, 0)
 
 
 def any_spec():
@@ -864,22 +830,14 @@
     freq = THETA ** (-(np.arange(HD // 2, dtype=np.float64) * 2.0 / HD))
     freq = jnp.asarray(np.concatenate([freq, freq])[None, :], F32)
     shape = jax.ShapeDtypeStruct
-    got_k, got_v, queries, key_new, value_new, lists, new_pages = pl.pallas_call(
-        gather_kernel,
-        out_shape=[
-            shape((4, GROUPS, 2, 2, PAGE, HD), BF16),
-            shape((4, GROUPS, 2, 2, PAGE, HD), BF16),
-            shape((4, CONVS, HEADS * SUF, HD), BF16),
-            shape((ROWS, HD), BF16),
-            shape((ROWS, HD), BF16),
-            shape((LIST, HD), I32),
-            shape((TENSOR, SUF, HD), BF16),
-        ],
+    attn_out, new_pages = pl.pallas_call(
+        layer_kernel,
+        out_shape=[shape((ROWS, PART), BF16), shape((TENSOR, SUF, HD), BF16)],
         in_specs=[smem_spec()] * 4
         + [vmem_spec()]
-        + [any_spec()] * 6
+        + [any_spec()] * 7
         + [vmem_spec()] * 5,
-        out_specs=[any_spec()] * 3 + [vmem_spec()] * 3 + [any_spec()],
+        out_specs=[vmem_spec(), any_spec()],
         scratch_shapes=[
             pltpu.VMEM((4, 4, ROWS, PART), BF16),
             pltpu.VMEM((WIDTH, HEADS * HD), BF16),
@@ -889,13 +847,32 @@
             pltpu.VMEM((ROWS, HD), F32),
             pltpu.VMEM((GROUPS, 2, 8, PAGE, HD), BF16),
             pltpu.VMEM((4, 2 * GROUPS, 2, PAGE, HD), BF16),
-            pltpu.VMEM((CONVS, HEADS * SUF, HD), BF16),
+            pltpu.VMEM((PAGES, 2, PAGE, HD), BF16),
+            pltpu.VMEM((PAGES, 2, PAGE, HD), BF16),
+            pltpu.VMEM((4, CONVS, HEADS * SUF, HD), BF16),
+            pltpu.VMEM((ROWS, HD), BF16),
+            pltpu.VMEM((ROWS, HD), BF16),
             pltpu.VMEM((ROWS, HD), BF16),
             pltpu.VMEM((ROWS, HD), BF16),
             pltpu.VMEM((GROUPS * CONVS, SUF, HD), BF16),
-            pltpu.VMEM((TENSOR, SUF, HD), BF16),
+            pltpu.VMEM((LIST, HD), I32),
+            pltpu.SMEM((LIST, HD), I32),
             pltpu.SMEM((2, TENSOR), I32),
             pltpu.VMEM((1, WIDTH), F32),
+            pltpu.VMEM((HEADS * HD, WIDTH), BF16),
+            pltpu.VMEM((4, BLOCKS, HD, HEADS * SUF), F32),
+            pltpu.VMEM((4, BLOCKS, 8, HEADS * SUF), F32),
+            pltpu.VMEM((CONVS, HD, HEADS * SUF), F32),
+            pltpu.VMEM((CONVS, 8, HEADS * SUF), F32),
+            pltpu.VMEM((4, CONVS, HD, HEADS * SUF), BF16),
+            pltpu.VMEM((4, CONVS, 8, HEADS * SUF), F32),
+            pltpu.VMEM((4, CONVS, HD, HEADS * SUF), BF16),
+            pltpu.VMEM((4, CONVS, 8, HEADS * SUF), F32),
+            pltpu.VMEM((ROWS, HEADS * HD), BF16),
+            pltpu.VMEM((4, 4, ROWS, PART), BF16),
+            pltpu.VMEM((2, 6, 4, SUF, PART), BF16),
+            pltpu.VMEM((2, 6, SUF, PART), BF16),
+            pltpu.VMEM((TENSOR, SUF, HD), BF16),
             dma((8,)),
             dma((2, GROUPS)),
             dma((20,)),
@@ -910,13 +887,19 @@
             dma((4,)),
             dma((GROUPS,)),
             dma((GROUPS,)),
+            dma((4,)),
+            dma((4,)),
+            dma((4,)),
+            dma((4,)),
+            dma((24,)),
+            dma((24,)),
             dma((TENSOR,)),
             dma((TENSOR,)),
         ],
         compiler_params=pltpu.CompilerParams(
-            collective_id=0, has_side_effects=True, vmem_limit_bytes=60 * 1024 * 1024
+            collective_id=0, has_side_effects=True, vmem_limit_bytes=62 * 1024 * 1024
         ),
-        name="gather",
+        name="layer",
     )(
         conv_slots,
         prefix_len,
@@ -929,56 +912,12 @@
         w_query,
         w_key.T,
         w_value.T,
+        w_out,
         norm_gain,
         b_query,
         b_key,
         b_value,
         freq,
-    )
-    attn_out = pl.pallas_call(
-        attend_kernel,
-        out_shape=shape((ROWS, PART), BF16),
-        in_specs=[smem_spec()] * 3 + [vmem_spec()] * 2 + [any_spec()] * 4,
-        out_specs=vmem_spec(),
-        scratch_shapes=[
-            pltpu.VMEM((4, CONVS, HEADS * SUF, HD), BF16),
-            pltpu.VMEM((PAGES, 2, PAGE, HD), BF16),
-            pltpu.VMEM((PAGES, 2, PAGE, HD), BF16),
-            pltpu.VMEM((HEADS * HD, WIDTH), BF16),
-            pltpu.VMEM((4, BLOCKS, HD, HEADS * SUF), F32),
-            pltpu.VMEM((4, BLOCKS, 8, HEADS * SUF), F32),
-            pltpu.VMEM((CONVS, HD, HEADS * SUF), F32),
-            pltpu.VMEM((CONVS, 8, HEADS * SUF), F32),
-            pltpu.VMEM((4, CONVS, HD, HEADS * SUF), BF16),
-            pltpu.VMEM((4, CONVS, 8, HEADS * SUF), F32),
-            pltpu.VMEM((4, CONVS, HD, HEADS * SUF), BF16),
-            pltpu.VMEM((4, CONVS, 8, HEADS * SUF), F32),
-            pltpu.VMEM((ROWS, HEADS * HD), BF16),
-            pltpu.VMEM((4, 4, ROWS, PART), BF16),
-            pltpu.VMEM((2, 6, 4, SUF, PART), BF16),
-            pltpu.VMEM((2, 6, SUF, PART), BF16),
-            dma((4,)),
-            dma((4,)),
-            dma((4,)),
-            dma((4,)),
-            dma((4,)),
-            dma((24,)),
-            dma((24,)),
-        ],
-        compiler_params=pltpu.CompilerParams(
-            collective_id=1, has_side_effects=True, vmem_limit_bytes=60 * 1024 * 1024
-        ),
-        name="attend",
-    )(
-        lists,
-        conv_slots,
-        suffix_len,
-        key_new,
-        value_new,
-        queries,
-        got_k.reshape(PAGES, 2, PAGE, HD),
-        got_v.reshape(PAGES, 2, PAGE, HD),
-        w_out,
     )
     pages = new_pages.reshape(TENSOR // 2, 2, SUF, HD)
     return (attn_out, pages[None, :, 0], pages[None, :, 1])

time: 132 us -> 122 us (0.924)
  Pallas kernels: 128 us -> 118 us
    pallas_call x2 -> x1, Pallas kernels: 128 us -> 118 us  [shards(): pl.pallas_call(layer_kernel, out_shape=[shape((ROWS, PART), BF16), shape(...]
where the time goes in v6:
time: 122 us
  Pallas kernels  118 us (97%)
  local copies, waits for them, and re-layouts  3.36 us (3%)
    pallas_call x1, Pallas kernels, shards(): pl.pallas_call(layer_kernel, out_shape=[shape((ROWS, PART), BF16), shape(...  118 us

profile of v6, /device:TPU:0, one launch (start us, length us, event | category | flops | bytes accessed | tf_op | source)
XLA Modules:
  0.0 122.0 jit_solution(3235113345576957848)
XLA Ops:
  0.6 118.0 %layer.1 = (bf16[256,512]{1,0:T(8,128)(2,1)}, bf16[16,64,128]{2,1,0:T(8,128)(2,1)}) custom-call(s32[32]{0:T(128)} %conv_ref.1, s32[32]{0:T(128)} %prefix_ref.1, s32[32]{0:T(128)} %suffix_ref.1, s32[32]{0:T(128)} %dest_ref.1, s32[32,64]{1,0:T(8,128)} %table_ref.1, bf16[256,512]{1,0:T(8,128)(2,1)} %hidden.1, bf16[16,8,64,128]{3,2,1,0:T(8,128)(2,1)} %pool_k.1, ...), custom_call_target="tpu_custom_call" | custom-call | tf_op jit(solution)/shard_map/layer/pallas_call | solution.py:833
  118.7 1.7 %slice_bitcast_fusion = (bf16[1,8,64,128]{3,2,1,0:T(8,128)(2,1)}, bf16[1,8,64,128]{3,2,1,0:T(8,128)(2,1)}) fusion(bf16[8,2,64,128]{3,2,1,0:T(8,128)(2,1)} %bitcast.13), kind=kLoop, calls=%fused_computation | loop fusion | bytes 524288 | tf_op jit(solution)/shard_map/broadcast_in_dim;squeeze | solution.py:923
  120.3 1.7 %copy.25 = bf16[256,512]{1,0:T(8,128)(2,1)} copy(bf16[256,512]{1,0:T(8,128)(2,1)} %get-tuple-element.12) | data formatting | bytes 524288

commit v7 on v6

--- a/solution.py
+++ b/solution.py
@@ -294,6 +294,7 @@
     f1.wait_recv()
     f3 = pass_on(3, feat.at[x_at[1], z, high_rows], to_x_down)
     s2 = spread(2, 1)
+    value_first = {step: values_first(step) for step in (1, 3, 2)}
     prefix = [prefix_ref[conv_ref[group * CONVS + i]] for i in range(CONVS)]
     suffix = [suffix_ref[conv_ref[group * CONVS + i]] for i in range(CONVS)]
 
@@ -307,12 +308,127 @@
     f2.wait_recv()
     f3.wait_recv()
     s3 = spread(3, 2)
-    value_first = {step: values_first(step) for step in (1, 3, 2)}
-    keys_second(0)
+    r0 = spread_on(0, 0, s0)
+
+    for load in loads:
+        load.wait()
+    load_out = pltpu.make_async_copy(w_out, weights, load_sem.at[5])
+    load_out.start()
+    gain[...] = gain_ref[...].astype(F32).reshape(1, WIDTH)
+    query_bias = b_query[...].astype(F32).reshape(1, HEADS * HD)
+    acc_q[...] = jnp.zeros_like(acc_q)
+    acc_kv[...] = jnp.zeros_like(acc_kv)
+    squares[...] = jnp.zeros_like(squares)
+
+    def project(bz, first, end):
+        def one(bx, carry):
+            block = bx * 4 + bz
+            rows = pl.ds(pl.multiple_of(block * PART, PART), PART)
+            wide = feat[bx, bz].astype(F32)
+            scaled = (wide * gain[:, rows]).astype(BF16)
+            acc_q[...] += jnp.dot(scaled, wq[rows, :], preferred_element_type=F32)
+            acc_kv[...] += lax.dot_general(
+                scaled,
+                wkv[:, rows],
+                (((1,), (1,)), ((), ())),
+                preferred_element_type=F32,
+            )
+            wide = wide * wide
+            total = squares[...]
+            for part in range(PART // HD):
+                total = total + wide[:, part * HD : (part + 1) * HD]
+            squares[...] = total
+            return carry
+
+        lax.fori_loop(first, end, one, 0)
+
+    project(z, 0, 4)
+    r1 = spread_on(1, 3, s1)
+    r2 = spread_on(2, 1, s2)
+    r3 = spread_on(3, 2, s3)
+    for shift in (1, 2, 6, 3, 7, 4, 5):
+        key_first[shift].wait_recv()
     values_second(0)
-    key_first[1].wait_recv()
-    keys_second(1)
-    r0 = spread_on(0, 0, s0)
+    for shift in (0, 1, 2, 6, 3, 7, 4, 5):
+        keys_second(shift)
+    project(z_up, 0, 4)
+    project(z_down, 0, 4)
+    for step in (1, 3, 2):
+        value_first[step].wait_recv()
+        values_second(step)
+    for shift, copies in ((0, r0), (3, r1), (1, r2), (2, r3)):
+        for copy in copies:
+            copy.wait_recv()
+        project(z_far, x_at[shift], x_at[shift] + 1)
+    mean = jnp.sum(squares[...], axis=1, keepdims=True) * (1.0 / WIDTH)
+    factor = lax.rsqrt(mean + EPSILON)
+    bias = jnp.concatenate(
+        [ref[...].astype(F32).reshape(1, HD // 2) for ref in (b_key, b_value)], axis=1
+    )
+    kv_own[...] = (acc_kv[...] * factor + bias).astype(BF16)
+    kv_copy = remote(
+        kv_own,
+        kv_other,
+        pair_send.at[0],
+        pair_recv.at[0],
+        group,
+        x * 4 + partner_z[1],
+    )
+    kv_copy.start()
+
+    def rotate(values):
+        return values * cosine + pltpu.roll(values, HD // 2, 1) * sine
+
+    for head in range(HEADS):
+        columns = slice(head * HD, (head + 1) * HD)
+        values = acc_q[:, columns] * factor + query_bias[:, columns]
+        values = rotate(values).astype(BF16)
+        for i in range(CONVS):
+            queries[0, i, head * SUF : (head + 1) * SUF, :] = values[i * SUF : (i + 1) * SUF, :]
+    query_out = [
+        remote(
+            queries.at[0],
+            queries.at[r],
+            pair_send.at[r],
+            pair_recv.at[r],
+            group,
+            x * 4 + partner_z[r],
+        )
+        for r in (1, 2, 3)
+    ]
+    for copy in query_out:
+        copy.start()
+
+    kv_copy.wait_recv()
+    mine = kv_own[...].astype(F32)
+    theirs = kv_other[...].astype(F32)
+    even = jnp.where(parity == 0, mine, theirs)
+    odd = jnp.where(parity == 0, theirs, mine)
+    low = lane_iota((ROWS, HD)) < HD // 2
+    keys = jnp.where(low, even, pltpu.roll(odd, HD // 2, 1))
+    keys = rotate(keys)
+    values = jnp.where(low, pltpu.roll(even, HD // 2, 1), odd)
+    key_new[...] = keys.astype(BF16)
+    value_new[...] = values.astype(BF16)
+
+    page = jnp.where(parity == 0, keys.astype(BF16).astype(F32), values)
+    live_row = jnp.concatenate([offsets < suffix[i] for i in range(CONVS)], axis=0)
+    page = jnp.where(live_row, page, 0.0).astype(BF16)
+    new_ref = new_all.at[pl.ds(group * CONVS, CONVS)]
+    new_ref[...] = page.reshape(CONVS, SUF, HD)
+    group_out = [
+        remote(
+            new_ref,
+            new_ref,
+            group_send.at[shift],
+            group_recv.at[shift],
+            group_at(shift),
+            tensor,
+        )
+        for shift in range(1, GROUPS)
+    ]
+    for copy in group_out:
+        copy.start()
 
     page_ids = lane_iota((1, PAGES))
     below = (row_iota((PAGES, PAGES)) < lane_iota((PAGES, PAGES))).astype(F32)
@@ -370,124 +486,7 @@
         chosen[1, to] = found
         return carry
 
-    for load in loads:
-        load.wait()
-    load_out = pltpu.make_async_copy(w_out, weights, load_sem.at[5])
-    load_out.start()
-    gain[...] = gain_ref[...].astype(F32).reshape(1, WIDTH)
-    query_bias = b_query[...].astype(F32).reshape(1, HEADS * HD)
-    acc_q[...] = jnp.zeros_like(acc_q)
-    acc_kv[...] = jnp.zeros_like(acc_kv)
-    squares[...] = jnp.zeros_like(squares)
-
-    def project(bz):
-        def one(bx, carry):
-            block = bx * 4 + bz
-            rows = pl.ds(pl.multiple_of(block * PART, PART), PART)
-            wide = feat[bx, bz].astype(F32)
-            scaled = (wide * gain[:, rows]).astype(BF16)
-            acc_q[...] += jnp.dot(scaled, wq[rows, :], preferred_element_type=F32)
-            acc_kv[...] += lax.dot_general(
-                scaled,
-                wkv[:, rows],
-                (((1,), (1,)), ((), ())),
-                preferred_element_type=F32,
-            )
-            wide = wide * wide
-            total = squares[...]
-            for part in range(PART // HD):
-                total = total + wide[:, part * HD : (part + 1) * HD]
-            squares[...] = total
-            return carry
-
-        lax.fori_loop(0, 4, one, 0)
-
-    project(z)
     lax.fori_loop(0, TENSOR, find, 0)
-    r1 = spread_on(1, 3, s1)
-    r2 = spread_on(2, 1, s2)
-    for shift in (2, 6, 3, 7, 4, 5):
-        key_first[shift].wait_recv()
-        keys_second(shift)
-    r3 = spread_on(3, 2, s3)
-    project(z_up)
-    project(z_down)
-    for step in (1, 3, 2):
-        value_first[step].wait_recv()
-        values_second(step)
-    for copies in (r0, r1, r2, r3):
-        for copy in copies:
-            copy.wait_recv()
-    project(z_far)
-    mean = jnp.sum(squares[...], axis=1, keepdims=True) * (1.0 / WIDTH)
-    factor = lax.rsqrt(mean + EPSILON)
-    bias = jnp.concatenate(
-        [ref[...].astype(F32).reshape(1, HD // 2) for ref in (b_key, b_value)], axis=1
-    )
-    kv_own[...] = (acc_kv[...] * factor + bias).astype(BF16)
-    kv_copy = remote(
-        kv_own,
-        kv_other,
-        pair_send.at[0],
-        pair_recv.at[0],
-        group,
-        x * 4 + partner_z[1],
-    )
-    kv_copy.start()
-
-    def rotate(values):
-        return values * cosine + pltpu.roll(values, HD // 2, 1) * sine
-
-    for head in range(HEADS):
-        columns = slice(head * HD, (head + 1) * HD)
-        values = acc_q[:, columns] * factor + query_bias[:, columns]
-        values = rotate(values).astype(BF16)
-        for i in range(CONVS):
-            queries[0, i, head * SUF : (head + 1) * SUF, :] = values[i * SUF : (i + 1) * SUF, :]
-    query_out = [
-        remote(
-            queries.at[0],
-            queries.at[r],
-            pair_send.at[r],
-            pair_recv.at[r],
-            group,
-            x * 4 + partner_z[r],
-        )
-        for r in (1, 2, 3)
-    ]
-    for copy in query_out:
-        copy.start()
-
-    kv_copy.wait_recv()
-    mine = kv_own[...].astype(F32)
-    theirs = kv_other[...].astype(F32)
-    even = jnp.where(parity == 0, mine, theirs)
-    odd = jnp.where(parity == 0, theirs, mine)
-    low = lane_iota((ROWS, HD)) < HD // 2
-    keys = jnp.where(low, even, pltpu.roll(odd, HD // 2, 1))
-    keys = rotate(keys)
-    values = jnp.where(low, pltpu.roll(even, HD // 2, 1), odd)
-    key_new[...] = keys.astype(BF16)
-    value_new[...] = values.astype(BF16)
-
-    page = jnp.where(parity == 0, keys.astype(BF16).astype(F32), values)
-    live_row = jnp.concatenate([offsets < suffix[i] for i in range(CONVS)], axis=0)
-    page = jnp.where(live_row, page, 0.0).astype(BF16)
-    new_ref = new_all.at[pl.ds(group * CONVS, CONVS)]
-    new_ref[...] = page.reshape(CONVS, SUF, HD)
-    group_out = [
-        remote(
-            new_ref,
-            new_ref,
-            group_send.at[shift],
-            group_recv.at[shift],
-            group_at(shift),
-            tensor,
-        )
-        for shift in range(1, GROUPS)
-    ]
-    for copy in group_out:
-        copy.start()
 
     half = HEADS * SUF
     own_head = lax.div(z, 2)
@@ -794,6 +793,18 @@
         return carry
 
     lax.fori_loop(1, TENSOR, page_end, 0)
+
+
+def place_kernel(part_out, pages, attn_out, new_keys, new_values, sems):
+    copies = [
+        pltpu.make_async_copy(part_out, attn_out, sems.at[0]),
+        pltpu.make_async_copy(pages.at[:, 0], new_keys.at[0], sems.at[1]),
+        pltpu.make_async_copy(pages.at[:, 1], new_values.at[0], sems.at[2]),
+    ]
+    for copy in copies:
+        copy.start()
+    for copy in copies:
+        copy.wait()
 
 
 def any_spec():
@@ -919,8 +930,16 @@
         b_value,
         freq,
     )
-    pages = new_pages.reshape(TENSOR // 2, 2, SUF, HD)
-    return (attn_out, pages[None, :, 0], pages[None, :, 1])
+    page_shape = shape((1, TENSOR // 2, SUF, HD), BF16)
+    return pl.pallas_call(
+        place_kernel,
+        out_shape=[shape((ROWS, PART), BF16), page_shape, page_shape],
+        in_specs=[any_spec()] * 2,
+        out_specs=[any_spec()] * 3,
+        scratch_shapes=[dma((3,))],
+        compiler_params=pltpu.CompilerParams(vmem_limit_bytes=62 * 1024 * 1024),
+        name="place",
+    )(attn_out, new_pages.reshape(TENSOR // 2, 2, SUF, HD))
 
 
 def solution(mesh):

time: 122 us -> 136 us (1.11)
  Pallas kernels: 118 us -> 135 us
  local copies, waits for them, and re-layouts: 3.36 us -> 0 us
    pallas_call x0 -> x1, Pallas kernels: none -> 17 us  [shards(): pl.pallas_call(place_kernel, out_shape=[shape((ROWS, PART), BF16), page_s...]
    another operation x1 -> x0, local copies, waits for them, and re-layouts: 1.69 us -> none  [shards(): return (attn_out, pages[None, :, 0], pages[None, :, 1])]
    unnamed x1 -> x0, local copies, waits for them, and re-layouts: 1.67 us -> none
where the time goes in v7:
time: 136 us
  Pallas kernels  135 us (99%)
    pallas_call x1, Pallas kernels, shards(): pl.pallas_call(layer_kernel, out_shape=[shape((ROWS, PART), BF16), shape(...  118 us
    pallas_call x1, Pallas kernels, shards(): pl.pallas_call(place_kernel, out_shape=[shape((ROWS, PART), BF16), page_s...  17 us

profile of v7, /device:TPU:0, one launch (start us, length us, event | category | flops | bytes accessed | tf_op | source)
XLA Modules:
  0.0 135.7 jit_solution(10861821394293711907)
XLA Ops:
  0.6 117.9 %layer.1 = (bf16[256,512]{1,0:T(8,128)(2,1)}, bf16[16,64,128]{2,1,0:T(8,128)(2,1)}) custom-call(s32[32]{0:T(128)} %conv_ref.1, s32[32]{0:T(128)} %prefix_ref.1, s32[32]{0:T(128)} %suffix_ref.1, s32[32]{0:T(128)} %dest_ref.1, s32[32,64]{1,0:T(8,128)} %table_ref.1, bf16[256,512]{1,0:T(8,128)(2,1)} %hidden.1, bf16[16,8,64,128]{3,2,1,0:T(8,128)(2,1)} %pool_k.1, ...), custom_call_target="tpu_custom_call" | custom-call | tf_op jit(solution)/shard_map/layer/pallas_call | solution.py:844
  118.6 17.0 %place.1 = (bf16[256,512]{1,0:T(8,128)(2,1)}, bf16[1,8,64,128]{3,2,1,0:T(8,128)(2,1)}, bf16[1,8,64,128]{3,2,1,0:T(8,128)(2,1)}) custom-call(bf16[256,512]{1,0:T(8,128)(2,1)} %get-tuple-element.5.part_out, bf16[8,2,64,128]{3,2,1,0:T(8,128)(2,1)} %bitcast.5), custom_call_target="tpu_custom_call" | custom-call | tf_op jit(solution)/shard_map/place/pallas_call | solution.py:934

commit v8 on v6

--- a/solution.py
+++ b/solution.py
@@ -794,6 +794,12 @@
         return carry
 
     lax.fori_loop(1, TENSOR, page_end, 0)
+
+
+def place_kernel(part_out, pages, attn_out, new_keys, new_values):
+    attn_out[...] = part_out[...]
+    new_keys[0] = pages[:, 0]
+    new_values[0] = pages[:, 1]
 
 
 def any_spec():
@@ -919,8 +925,15 @@
         b_value,
         freq,
     )
-    pages = new_pages.reshape(TENSOR // 2, 2, SUF, HD)
-    return (attn_out, pages[None, :, 0], pages[None, :, 1])
+    page_shape = shape((1, TENSOR // 2, SUF, HD), BF16)
+    return pl.pallas_call(
+        place_kernel,
+        out_shape=[shape((ROWS, PART), BF16), page_shape, page_shape],
+        in_specs=[vmem_spec()] * 2,
+        out_specs=[vmem_spec()] * 3,
+        compiler_params=pltpu.CompilerParams(vmem_limit_bytes=62 * 1024 * 1024),
+        name="place",
+    )(attn_out, new_pages.reshape(TENSOR // 2, 2, SUF, HD))
 
 
 def solution(mesh):

time: 122 us -> 121 us (level)
  local copies, waits for them, and re-layouts: 3.36 us -> 0 us
  Pallas kernels: 118 us -> 120 us
    pallas_call x0 -> x1, Pallas kernels: none -> 1.82 us  [shards(): pl.pallas_call(place_kernel, out_shape=[shape((ROWS, PART), BF16), page_s...]
    another operation x1 -> x0, local copies, waits for them, and re-layouts: 1.69 us -> none  [shards(): return (attn_out, pages[None, :, 0], pages[None, :, 1])]
    unnamed x1 -> x0, local copies, waits for them, and re-layouts: 1.67 us -> none
where the time goes in v8:
time: 121 us; the launch traced here: 120 us
  Pallas kernels  120 us (99%)
    pallas_call x1, Pallas kernels, shards(): pl.pallas_call(layer_kernel, out_shape=[shape((ROWS, PART), BF16), shape(...  118 us

profile of v8, /device:TPU:0, one launch (start us, length us, event | category | flops | bytes accessed | tf_op | source)
XLA Modules:
  0.0 120.5 jit_solution(12569065489097404939)
XLA Ops:
  0.6 118.0 %layer.1 = (bf16[256,512]{1,0:T(8,128)(2,1)}, bf16[16,64,128]{2,1,0:T(8,128)(2,1)}) custom-call(s32[32]{0:T(128)} %conv_ref.1, s32[32]{0:T(128)} %prefix_ref.1, s32[32]{0:T(128)} %suffix_ref.1, s32[32]{0:T(128)} %dest_ref.1, s32[32,64]{1,0:T(8,128)} %table_ref.1, bf16[256,512]{1,0:T(8,128)(2,1)} %hidden.1, bf16[16,8,64,128]{3,2,1,0:T(8,128)(2,1)} %pool_k.1, ...), custom_call_target="tpu_custom_call" | custom-call | tf_op jit(solution)/shard_map/layer/pallas_call | solution.py:839
  118.7 1.8 %place.1 = (bf16[256,512]{1,0:T(8,128)(2,1)}, bf16[1,8,64,128]{3,2,1,0:T(8,128)(2,1)}, bf16[1,8,64,128]{3,2,1,0:T(8,128)(2,1)}) custom-call(bf16[256,512]{1,0:T(8,128)(2,1)} %get-tuple-element.5.part_out, bf16[8,2,64,128]{3,2,1,0:T(8,128)(2,1)} %bitcast.5), custom_call_target="tpu_custom_call" | custom-call | tf_op jit(solution)/shard_map/place/pallas_call | solution.py:929

commit v9 on v8

--- a/solution.py
+++ b/solution.py
@@ -294,6 +294,7 @@
     f1.wait_recv()
     f3 = pass_on(3, feat.at[x_at[1], z, high_rows], to_x_down)
     s2 = spread(2, 1)
+    value_first = {step: values_first(step) for step in (1, 3, 2)}
     prefix = [prefix_ref[conv_ref[group * CONVS + i]] for i in range(CONVS)]
     suffix = [suffix_ref[conv_ref[group * CONVS + i]] for i in range(CONVS)]
 
@@ -307,11 +308,6 @@
     f2.wait_recv()
     f3.wait_recv()
     s3 = spread(3, 2)
-    value_first = {step: values_first(step) for step in (1, 3, 2)}
-    keys_second(0)
-    values_second(0)
-    key_first[1].wait_recv()
-    keys_second(1)
     r0 = spread_on(0, 0, s0)
 
     page_ids = lane_iota((1, PAGES))
@@ -406,15 +402,17 @@
     lax.fori_loop(0, TENSOR, find, 0)
     r1 = spread_on(1, 3, s1)
     r2 = spread_on(2, 1, s2)
-    for shift in (2, 6, 3, 7, 4, 5):
+    r3 = spread_on(3, 2, s3)
+    for shift in (1, 2, 6, 3, 7, 4, 5):
         key_first[shift].wait_recv()
-        keys_second(shift)
-    r3 = spread_on(3, 2, s3)
+    values_second(0)
     project(z_up)
-    project(z_down)
     for step in (1, 3, 2):
         value_first[step].wait_recv()
         values_second(step)
+    for shift in (0, 1, 2, 6, 3, 7, 4, 5):
+        keys_second(shift)
+    project(z_down)
     for copies in (r0, r1, r2, r3):
         for copy in copies:
             copy.wait_recv()

time: 121 us -> 121 us (level)
  no operation moved by 1% of the time
where the time goes in v9:
time: 121 us
  Pallas kernels  120 us (99%)
    pallas_call x1, Pallas kernels, shards(): pl.pallas_call(layer_kernel, out_shape=[shape((ROWS, PART), BF16), shape(...  118 us

profile of v9, /device:TPU:0, one launch (start us, length us, event | category | flops | bytes accessed | tf_op | source)
XLA Modules:
  0.0 120.8 jit_solution(17924574597160769401)
XLA Ops:
  0.6 118.3 %layer.1 = (bf16[256,512]{1,0:T(8,128)(2,1)}, bf16[16,64,128]{2,1,0:T(8,128)(2,1)}) custom-call(s32[32]{0:T(128)} %conv_ref.1, s32[32]{0:T(128)} %prefix_ref.1, s32[32]{0:T(128)} %suffix_ref.1, s32[32]{0:T(128)} %dest_ref.1, s32[32,64]{1,0:T(8,128)} %table_ref.1, bf16[256,512]{1,0:T(8,128)(2,1)} %hidden.1, bf16[16,8,64,128]{3,2,1,0:T(8,128)(2,1)} %pool_k.1, ...), custom_call_target="tpu_custom_call" | custom-call | tf_op jit(solution)/shard_map/layer/pallas_call | solution.py:837
  118.9 1.8 %place.1 = (bf16[256,512]{1,0:T(8,128)(2,1)}, bf16[1,8,64,128]{3,2,1,0:T(8,128)(2,1)}, bf16[1,8,64,128]{3,2,1,0:T(8,128)(2,1)}) custom-call(bf16[256,512]{1,0:T(8,128)(2,1)} %get-tuple-element.5.part_out, bf16[8,2,64,128]{3,2,1,0:T(8,128)(2,1)} %bitcast.5), custom_call_target="tpu_custom_call" | custom-call | tf_op jit(solution)/shard_map/place/pallas_call | solution.py:927
